TPU v7x, 32 devices: a whole 2x2x4 slice. The times are simulated.
32 devices in a mesh: groups: 2 (over x), ctx: 16 (over z, y, core).
Axes of the slice: x: 2, y: 2, z: 4, core: 2. Of those that a mesh axis runs over, the one named last changes fastest.
Arguments:
- query_gate: bfloat16 [4096, 4096], P(('groups', 'ctx')), parts along dimension 0, may hold values from -6 to 6
- key_branch: bfloat16 [4096, 4096], P(('groups', 'ctx')), parts along dimension 0, may hold values from -6 to 6
- value_branch: bfloat16 [4096, 4096], P(('groups', 'ctx')), parts along dimension 0, may hold values from -6 to 6
- out_grad: bfloat16 [4096, 4096], P(('groups', 'ctx')), parts along dimension 0, may hold values from -6 to 6
- filter_taps: bfloat16 [4096, 256], P('ctx'), may hold values from -0.375 to 0.375
- doc_blocks: int32 [8], P('groups'), parts along dimension 0, may hold values from 1 to 8, 16 in all
Outputs:
- key_grad: bfloat16 [4096, 4096], P(('groups', 'ctx')), parts along dimension 0
- value_grad: bfloat16 [4096, 4096], P(('groups', 'ctx')), parts along dimension 0
- filter_grad: float32 [8192, 256], P(('groups', 'ctx')), parts along dimension 0
There are 2 independent parts, one for each index of `groups`. A program takes and returns all parts, laid end to end along the dimension named above; an argument that names none is the same for every part. Nothing has to cross between parts.
Inputs may be any that keep to these rules, and one draw needn't show every extreme that they name: `doc_blocks`: documents follow one another along the sequence, each a whole number of blocks of 128 tokens; the lengths sum to 16 and the longest is exactly 8 blocks.
All inputs are finite; a program needn't handle non-finite values.
Results may differ from a plain program's by a relative error of at most 0.005.
Values may be sent and summed in bfloat16 or wider, within the bound.
No kernel may reach another device: no remote copies, remote signals or barrier semaphores. Data moves between devices by JAX's collectives and lax.ppermute only.
A program may use at most 128 MiB of HBM per device.

v0:
```python
from functools import partial
import math

import jax
import jax.numpy as jnp
from jax import lax
from jax.sharding import PartitionSpec as P

TOK_DEV = 128
REACH = 2


highest = lax.Precision.HIGHEST


def shifted(value, axis, steps):
    count = lax.axis_size(axis)
    first, last = (max(0, -steps), min(count, count - steps))
    return lax.ppermute(value, axis, [(source, source + steps) for source in range(first, last)])


def make_forward(block_rows):
    length = 2 * block_rows
    freq_ids = jnp.arange(block_rows, dtype=jnp.int32)[:, None]
    sample_ids = jnp.arange(block_rows, dtype=jnp.int32)[None, :]
    angle = 2.0 * math.pi / length * (freq_ids * sample_ids % length).astype(jnp.float32)
    cosine = jnp.cos(angle)
    nyquist = jnp.where(sample_ids % 2 == 0, 1.0, -1.0)
    sine = jnp.where(freq_ids == 0, nyquist, -jnp.sin(angle))
    return jnp.concatenate([cosine, sine], axis=0)


def make_inverse(block_rows):
    length = 2 * block_rows
    sample_ids = jnp.arange(block_rows, dtype=jnp.int32)[:, None]
    freq_ids = jnp.arange(block_rows, dtype=jnp.int32)[None, :]
    angle = 2.0 * math.pi / length * (freq_ids * sample_ids % length).astype(jnp.float32)
    cosine = jnp.where(freq_ids == 0, 1.0, 2.0 * jnp.cos(angle)) / length
    nyquist = jnp.where(sample_ids % 2 == 0, 1.0, -1.0)
    sine = jnp.where(freq_ids == 0, nyquist, -2.0 * jnp.sin(angle)) / length
    return jnp.concatenate([cosine, sine], axis=1)


def row_column(count, ndims):
    return jnp.arange(count).reshape((count,) + (1,) * (ndims - 1))


def conjugate(spectrum):
    block_rows = spectrum.shape[0] // 2
    row_ids = row_column(2 * block_rows, spectrum.ndim)
    return jnp.where(row_ids > block_rows, -spectrum, spectrum)


def alternate(spectrum):
    block_rows = spectrum.shape[0] // 2
    row_ids = row_column(2 * block_rows, spectrum.ndim)
    return jnp.where(row_ids % block_rows % 2 == 0, spectrum, -spectrum)


def spectral_product(left_spec, right_spec):
    block_rows = left_spec.shape[0] // 2
    left_real, left_imag = (left_spec[:block_rows], left_spec[block_rows:])
    right_real, right_imag = (right_spec[:block_rows], right_spec[block_rows:])
    leading = row_column(block_rows, max(left_spec.ndim, right_spec.ndim)) == 0
    imag_cross = left_imag * right_imag
    real_part = left_real * right_real - jnp.where(leading, 0.0, imag_cross)
    imag_part = jnp.where(leading, imag_cross, left_real * right_imag + left_imag * right_real)
    return jnp.concatenate([real_part, imag_part], axis=0)


def transform(forward_table, held):
    return jnp.dot(forward_table, held.astype(jnp.float32), precision=highest)


def conj_transform(forward_table, held):
    return conjugate(transform(forward_table, held))


def back_half(inverse_table, spectrum):
    return jnp.dot(inverse_table, spectrum, precision=highest)


def back_pair(inverse_table, left_spec, right_spec):
    return back_half(inverse_table, spectral_product(left_spec, right_spec))


def weighted(weight, builder):
    return weight * builder()


def pair_weights(doc_blocks, block_index, block_count, direction):
    doc_starts = jnp.cumsum(doc_blocks) - doc_blocks
    own_doc = jnp.sum((doc_starts <= block_index).astype(jnp.int32)) - 1
    weights = []
    for offset in range(REACH + 1):
        partner = block_index + direction * offset
        in_range = (partner >= 0) & (partner < block_count)
        clipped = jnp.clip(partner, 0, block_count - 1)
        partner_doc = jnp.sum((doc_starts <= clipped).astype(jnp.int32)) - 1
        weights.append(jnp.where(in_range & (partner_doc == own_doc), 1.0, 0.0).astype(jnp.float32))
    return weights


def tap_blocks(piece_rows):
    forward_table = make_forward(TOK_DEV)
    widened = piece_rows.astype(jnp.float32)
    spectra = []
    for segment in range(REACH):
        taps_block = widened[:, segment * TOK_DEV : (segment + 1) * TOK_DEV]
        spectra.append(
            lax.dot_general(forward_table, taps_block, (((1,), (1,)), ((), ())), precision=highest)
        )
    return jnp.stack(spectra, axis=0)


def combine_pairs(tap_spectra):
    pair_spectra = []
    for offset in range(REACH + 1):
        combined = jnp.zeros(tap_spectra.shape[1:], jnp.float32)
        if offset < REACH:
            combined = conjugate(tap_spectra[offset])
        if offset >= 1:
            combined = combined + alternate(conjugate(tap_spectra[offset - 1]))
        pair_spectra.append(combined)
    return pair_spectra


def push_terms(grad_held, conv_held, earlier, pair_spectra, weights, forward_table, inverse_table):
    grad_spec = transform(forward_table, grad_held)
    partials = [back_pair(inverse_table, grad_spec, pair_spectra[0])]
    conj_inputs = [conj_transform(forward_table, conv_held)]
    for offset in range(1, len(pair_spectra)):
        partials.append(
            weighted(
                weights[offset], partial(back_pair, inverse_table, grad_spec, pair_spectra[offset])
            )
        )
        conj_inputs.append(
            weighted(weights[offset], partial(conj_transform, forward_table, earlier[offset - 1]))
        )
    tap_specs = []
    for segment in range(len(pair_spectra) - 1):
        tap_specs.append(
            spectral_product(grad_spec, conj_inputs[segment] + alternate(conj_inputs[segment + 1]))
        )
    return (partials, tap_specs)


def shards(query_gate, key_branch, value_branch, out_grad, filter_taps, doc_blocks):
    block_count = lax.axis_size("ctx")
    block_index = lax.axis_index("ctx")
    block_rows = query_gate.shape[0]
    forward_table = make_forward(block_rows)
    inverse_table = make_inverse(block_rows)
    conv_held = (key_branch.astype(jnp.float32) * value_branch.astype(jnp.float32)).astype(
        jnp.bfloat16
    )
    grad_held = (out_grad.astype(jnp.float32) * query_gate.astype(jnp.float32)).astype(jnp.bfloat16)
    norm_scale = 1.0 / math.sqrt(block_rows * block_count)
    tap_spectra = tap_blocks(lax.all_gather(filter_taps, "ctx", axis=0, tiled=True))
    pair_spectra = combine_pairs(tap_spectra)
    weights = pair_weights(doc_blocks, block_index, block_count, -1)
    earlier = [shifted(conv_held, "ctx", offset) for offset in range(1, REACH + 1)]
    partials, tap_specs = push_terms(
        grad_held, conv_held, earlier, pair_spectra, weights, forward_table, inverse_table
    )
    grad_input = partials[0]
    for offset in range(1, REACH + 1):
        grad_input = grad_input + shifted(partials[offset], "ctx", -offset)
    pieces = []
    for spectrum in tap_specs:
        pieces.append(
            lax.dot_general(spectrum, inverse_table, (((0,), (1,)), ((), ())), precision=highest)
        )
    filter_grad = lax.psum_scatter(
        jnp.concatenate(pieces, axis=1) * norm_scale, "ctx", scatter_dimension=0, tiled=True
    )
    key_grad = (grad_input * value_branch.astype(jnp.float32)).astype(jnp.bfloat16)
    value_grad = (grad_input * key_branch.astype(jnp.float32)).astype(jnp.bfloat16)
    return (key_grad, value_grad, filter_grad)


def solution(mesh):
    in_specs = (
        P(("groups", "ctx"), None),
        P(("groups", "ctx"), None),
        P(("groups", "ctx"), None),
        P(("groups", "ctx"), None),
        P("ctx", None),
        P("groups"),
    )
    out_specs = (P(("groups", "ctx"), None), P(("groups", "ctx"), None), P(("groups", "ctx"), None))
    return jax.shard_map(shards, mesh=mesh, in_specs=in_specs, out_specs=out_specs, check_vma=False)
```

profile of v0, /device:TPU:23, one launch (start us, length us, event | category | flops | bytes accessed | tf_op | source)
XLA Modules:
  0.0 210.3 jit_solution(8816425614126127469)
XLA Ops:
  7.2 0.0 copy-start.11
  7.2 0.0 copy-start.10
  7.2 0.0 all-gather.2.cloned.1.call-start
  7.2 0.7 all-gather.2.cloned.1.call-update
  7.9 0.0 reduce-scatter.2.cloned.1.call-start
  8.0 1.8 fusion.25
  9.8 3.1 %collective-permute-start.3 = (bf16[128,4096]{1,0:T(8,128)(2,1)S(1)}, bf16[128,4096]{1,0:T(8,128)(2,1)}, u32[]{:S(2)}, u32[]{:S(2)}) collective-permute-start(bf16[128,4096]{1,0:T(8,128)(2,1)S(1)} %fusion.25), channel_id=1, source_target_pairs={{0,2},{1,3},{2,4},{3,5},{4,6},{5,7},{6,8},{7,9},{8,10},{9,11},{10,... | collective-permute-start | bytes 3145736 | tf_op jit(solution)/shard_map/ppermute | solution.py:19
  12.9 4.0 %collective-permute-start.2 = (bf16[128,4096]{1,0:T(8,128)(2,1)S(1)}, bf16[128,4096]{1,0:T(8,128)(2,1)}, u32[]{:S(2)}, u32[]{:S(2)}) collective-permute-start(bf16[128,4096]{1,0:T(8,128)(2,1)S(1)} %fusion.25), channel_id=1, source_target_pairs={{0,1},{1,2},{2,3},{3,4},{4,5},{5,6},{6,7},{7,8},{8,9},{9,10},{10,1... | collective-permute-start | bytes 3145736 | tf_op jit(solution)/shard_map/ppermute | solution.py:19
  16.9 0.3 select_multiply_fusion
  17.2 0.0 copy-done.11
  17.2 0.0 copy-done.10
  17.3 0.0 copy-start.12
  17.3 3.8 %fusion.26 = f32[256,4096]{1,0:T(8,128)} fusion(bf16[128,4096]{1,0:T(8,128)(2,1)S(1)} %copy-done.10, bf16[128,4096]{1,0:T(8,128)(2,1)S(1)} %copy-done.11, f32[128,128]{1,0:T(8,128)S(1)} %get-tuple-element.28, f32[128,128]{1,0:T(8,128)S(1)} %get-tuple-element.30), kind=kOutput, calls=%fused_computation.58 | convolution fusion | flops 1612742656 | bytes 6422528 | tf_op jit(solution)/shard_map/dot_general | solution.py:72
  21.0 0.0 copy-done.12
  21.0 0.2 reduce-window.9
  21.2 0.7 fusion.39
  23.9 35.9 %collective-permute-done.2 = bf16[128,4096]{1,0:T(8,128)(2,1)} collective-permute-done((bf16[128,4096]{1,0:T(8,128)(2,1)S(1)}, bf16[128,4096]{1,0:T(8,128)(2,1)}, u32[]{:S(2)}, u32[]{:S(2)}) %collective-permute-start.2) | collective-permute-done | bytes 1048608 | tf_op jit(solution)/shard_map/ppermute | solution.py:19
  59.7 3.2 %fusion = f32[256,4096]{1,0:T(8,128)S(1)} fusion(bf16[128,4096]{1,0:T(8,128)(2,1)} %collective-permute-done.2, f32[]{:T(128)S(6)} %select_n.195, pred[256]{0:T(512)(128)(4,1)S(1)} %get-tuple-element.32, f32[128,128]{1,0:T(8,128)S(1)} %get-tuple-element.28, f32[128,128]{1,0:T(8,128)S(1)} %get-tuple-element.30), kind=kOutput, calls=%fused_computation.9 | convolution fusion | flops 1613791232 | bytes 5374212 | tf_op jit(solution)/shard_map/dot_general | solution.py:72
  63.0 4.4 %fusion.5 = f32[256,4096]{1,0:T(8,128)} fusion(f32[256,4096]{1,0:T(8,128)S(1)} %fusion, pred[256]{0:T(512)(128)(4,1)S(1)} %get-tuple-element.31, bf16[128,4096]{1,0:T(8,128)(2,1)S(1)} %fusion.25, pred[256]{0:T(512)(128)(4,1)S(1)} %get-tuple-element.32, f32[128,128]{1,0:T(8,128)S(1)} %get-tuple-element.28, f32[128,128]{1,0:T(8,128)S(1)} %get-tuple-element.30), kind=kOutput, calls=%fused_computation.17 | convolution fusion | flops 1615888384 | bytes 9568768 | tf_op jit(solution)/shard_map/dot_general | solution.py:72
  67.4 0.0 collective-permute-done.3
  67.4 5.8 %fusion.2 = f32[256,4096]{1,0:T(8,128)} fusion(f32[256,4096]{1,0:T(8,128)S(1)} %fusion, bf16[128,4096]{1,0:T(8,128)(2,1)} %collective-permute-done.3, f32[]{:T(128)S(6)} %select_n.202, pred[256]{0:T(512)(128)(4,1)S(1)} %get-tuple-element.31, pred[256]{0:T(512)(128)(4,1)S(1)} %get-tuple-element.32, f32[128,128]{1,0:T(8,128)S(1)} %get-tuple-element.28, ...), kind=kOutput, calls=%fused_computation.11 | convolution fusion | flops 1616936960 | bytes 9568772 | tf_op jit(solution)/shard_map/dot_general | solution.py:72
  73.2 3.3 %negate_select_fusion.8 = f32[256,4096]{1,0:T(8,128)S(1)} fusion(pred[256]{0:T(512)(128)(4,1)S(1)} %get-tuple-element.32, bf16[4096,256]{1,0:T(8,128)(2,1)} %all-gather.2.cloned.1.call-done, f32[128,128]{1,0:T(8,128)S(1)} %get-tuple-element.28, f32[128,128]{1,0:T(8,128)S(1)} %get-tuple-element.30), kind=kOutput, calls=%fused_computation.8 | convolution fusion | flops 1612742656 | bytes 5374208 | tf_op jit(solution)/shard_map/dot_general | solution.py:111
  76.6 0.0 copy-done.9
  76.6 0.0 copy-start.2
  76.6 0.0 copy-start
  76.6 0.0 copy-start.5
  76.6 2.9 %fusion.4 = (f32[256,4096]{1,0:T(8,128)S(1)}, f32[256,4096]{1,0:T(8,128)S(1)}) fusion(f32[256,4096]{1,0:T(8,128)S(1)} %negate_select_fusion.8, pred[256]{0:T(512)(128)(4,1)S(1)} %get-tuple-element.31, bf16[4096,256]{1,0:T(8,128)(2,1)S(1)} %copy-done.9, f32[128,128]{1,0:T(8,128)S(1)} %get-tuple-element.28, f32[128,128]{1,0:T(8,128)S(1)} %get-tuple-element.30, ...), kind=kOutput, calls=%fused_computation.16 | convolution fusion | flops 1617985536 | bytes 13763584 | tf_op jit(solution)/shard_map/dot_general | solution.py:111
  79.5 0.7 copy-done
  80.3 1.3 copy-done.5
  81.6 2.5 %select_subtract_fusion.1 = (f32[128,4096]{1,0:T(8,128)S(1)}, f32[128,4096]{1,0:T(8,128)S(1)}, f32[128,4096]{1,0:T(8,128)S(1)}, f32[128,4096]{1,0:T(8,128)}) fusion(f32[256,4096]{1,0:T(8,128)S(1)} %copy-done.5, pred[128]{0:T(512)(128)(4,1)S(1)} %iota_compare_fusion.1, f32[256,4096]{1,0:T(8,128)S(1)} %copy-done, f32[256,4096]{1,0:T(8,128)S(1)} %get-tuple-element.23), kind=kLoop, calls=%fused_computation.45 | loop fusion | flops 8388608 | bytes 20971648 | tf_op jit(solution)/shard_map/sub | solution.py:66
  84.1 0.2 copy-done.4
  84.3 3.0 %select_subtract_fusion = (f32[128,4096]{1,0:T(8,128)S(1)}, f32[128,4096]{1,0:T(8,128)S(1)}, f32[128,4096]{1,0:T(8,128)}, f32[128,4096]{1,0:T(8,128)}) fusion(f32[256,4096]{1,0:T(8,128)S(1)} %copy-done.4, pred[128]{0:T(512)(128)(4,1)S(1)} %iota_compare_fusion.1, f32[256,4096]{1,0:T(8,128)S(1)} %copy-done, f32[256,4096]{1,0:T(8,128)S(1)} %get-tuple-element.24), kind=kLoop, calls=%fused_computation.43 | loop fusion | flops 8388608 | bytes 20971648 | tf_op jit(solution)/shard_map/sub | solution.py:66
  87.3 2.5 %fusion.19 = f32[4096,128]{0,1:T(8,128)S(1)} fusion(f32[128,4096]{1,0:T(8,128)S(1)} %get-tuple-element.12, f32[128,4096]{1,0:T(8,128)S(1)} %get-tuple-element.11, f32[128,128]{1,0:T(8,128)S(1)} %get-tuple-element.27, f32[128,128]{1,0:T(8,128)S(1)} %get-tuple-element.29), kind=kOutput, calls=%fused_computation.31 | convolution fusion | flops 1611694080 | bytes 6422528 | tf_op jit(solution)/shard_map/dot_general | solution.py:173
  89.8 2.5 %fusion.15 = f32[4096,128]{0,1:T(8,128)S(1)} fusion(f32[128,4096]{1,0:T(8,128)S(1)} %get-tuple-element.10, f32[128,4096]{1,0:T(8,128)S(1)} %get-tuple-element.9, f32[128,128]{1,0:T(8,128)S(1)} %get-tuple-element.27, f32[128,128]{1,0:T(8,128)S(1)} %get-tuple-element.29), kind=kOutput, calls=%fused_computation.27 | convolution fusion | flops 1611694080 | bytes 6422528 | tf_op jit(solution)/shard_map/dot_general | solution.py:173
  92.3 2.5 %maximum_multiply_fusion = f32[4096,256]{0,1:T(8,128)} fusion(f32[4096,128]{0,1:T(8,128)S(1)} %fusion.19, f32[4096,128]{0,1:T(8,128)S(1)} %fusion.15), kind=kLoop, calls=%fused_computation.35 | loop fusion | flops 2097152 | bytes 8388608 | tf_op jit(solution)/shard_map/mul | solution.py:176
  94.8 0.0 reduce-scatter.2.cloned.1.call-update
  94.8 4.7 %convolution_multiply_fusion = f32[128,4096]{1,0:T(8,128)S(1)} fusion(f32[128,4096]{1,0:T(8,128)} %get-tuple-element.21, f32[128,4096]{1,0:T(8,128)} %get-tuple-element.22, f32[]{:T(128)S(6)} %select_n.202, f32[128,128]{1,0:T(8,128)S(1)} %get-tuple-element.27, f32[128,128]{1,0:T(8,128)S(1)} %get-tuple-element.29), kind=kOutput, calls=%fused_computation.12 | convolution fusion | flops 1612218368 | bytes 6422532 | tf_op jit(solution)/shard_map/dot_general | solution.py:80
  99.5 2.1 %collective-permute-start.1 = (f32[128,4096]{1,0:T(8,128)S(1)}, f32[128,4096]{1,0:T(8,128)S(1)}, u32[]{:S(2)}, u32[]{:S(2)}) collective-permute-start(f32[128,4096]{1,0:T(8,128)S(1)} %convolution_multiply_fusion), channel_id=1, source_target_pairs={{2,0},{3,1},{4,2},{5,3},{6,4},{7,5},{8,6},{9,7},{10,8},{11,9},{12,... | collective-permute-start | bytes 6291464 | tf_op jit(solution)/shard_map/ppermute | solution.py:19
  101.7 2.3 %convolution_multiply_fusion.1 = f32[128,4096]{1,0:T(8,128)S(1)} fusion(f32[128,4096]{1,0:T(8,128)S(1)} %get-tuple-element.19, f32[128,4096]{1,0:T(8,128)S(1)} %copy-done.6, f32[]{:T(128)S(6)} %select_n.195, f32[128,128]{1,0:T(8,128)S(1)} %get-tuple-element.27, f32[128,128]{1,0:T(8,128)S(1)} %get-tuple-element.29), kind=kOutput, calls=%fused_computation.13 | convolution fusion | flops 1612218368 | bytes 6422532 | tf_op jit(solution)/shard_map/dot_general | solution.py:80
  104.0 0.0 copy-start.7
  104.0 0.0 copy-start.8
  104.0 4.9 %collective-permute-start = (f32[128,4096]{1,0:T(8,128)S(1)}, f32[128,4096]{1,0:T(8,128)S(1)}, u32[]{:S(2)}, u32[]{:S(2)}) collective-permute-start(f32[128,4096]{1,0:T(8,128)S(1)} %convolution_multiply_fusion.1), channel_id=1, source_target_pairs={{1,0},{2,1},{3,2},{4,3},{5,4},{6,5},{7,6},{8,7},{9,8},{10,9},{11,1... | collective-permute-start | bytes 6291464 | tf_op jit(solution)/shard_map/ppermute | solution.py:19
  108.9 1.2 select_subtract_fusion.4
  110.2 53.8 %collective-permute-done.1 = f32[128,4096]{1,0:T(8,128)S(1)} collective-permute-done((f32[128,4096]{1,0:T(8,128)S(1)}, f32[128,4096]{1,0:T(8,128)S(1)}, u32[]{:S(2)}, u32[]{:S(2)}) %collective-permute-start.1) | collective-permute-done | bytes 2097184 | tf_op jit(solution)/shard_map/ppermute | solution.py:19
  164.0 33.4 %collective-permute-done = f32[128,4096]{1,0:T(8,128)S(1)} collective-permute-done((f32[128,4096]{1,0:T(8,128)S(1)}, f32[128,4096]{1,0:T(8,128)S(1)}, u32[]{:S(2)}, u32[]{:S(2)}) %collective-permute-start) | collective-permute-done | bytes 2097184 | tf_op jit(solution)/shard_map/ppermute | solution.py:19
  197.4 0.0 copy-done.8
  197.4 4.2 %fusion.24 = (bf16[128,4096]{1,0:T(8,128)(2,1)}, bf16[128,4096]{1,0:T(8,128)(2,1)}) fusion(bf16[128,4096]{1,0:T(8,128)(2,1)S(1)} %copy-done.7, bf16[128,4096]{1,0:T(8,128)(2,1)S(1)} %copy-done.8, f32[128,4096]{1,0:T(8,128)S(1)} %collective-permute-done.1, f32[128,4096]{1,0:T(8,128)S(1)} %collective-permute-done, f32[128,4096]{1,0:T(8,128)S(1)} %get-tuple-element.14, ...), kind=kOutput, calls=%fused_computation.40 | convolution fusion | flops 1615888384 | bytes 12713984 | tf_op jit(solution)/shard_map/dot_general | solution.py:80
  201.6 1.8 copy.9
  (15 shorter events, 0.0 us)
Async XLA Ops:
  7.2 10.1 %copy-start.11 = (bf16[128,4096]{1,0:T(8,128)(2,1)S(1)}, bf16[128,4096]{1,0:T(8,128)(2,1)}, u32[]{:S(2)}) copy-start(bf16[128,4096]{1,0:T(8,128)(2,1)} %param.9) | copy-start | bytes 3145732
  7.2 10.1 %copy-start.10 = (bf16[128,4096]{1,0:T(8,128)(2,1)S(1)}, bf16[128,4096]{1,0:T(8,128)(2,1)}, u32[]{:S(2)}) copy-start(bf16[128,4096]{1,0:T(8,128)(2,1)} %param.6) | copy-start | bytes 3145732
  7.2 66.0 %all-gather.2.cloned.1.call-start = ((), (), s32[]{:S(2)}) async-start(), calls=%async_computation.1 | async-start | bytes 2228224 | tf_op jit(solution)/shard_map/all_gather | solution.py:160
  7.9 193.7 %reduce-scatter.2.cloned.1.call-start = ((), (), s32[]{:S(2)}) async-start(), calls=%async_computation.2 | async-start | bytes 4456448 | tf_op jit(solution)/shard_map/reduce_scatter | solution.py:175
  9.8 57.7 %collective-permute-start.3 = (bf16[128,4096]{1,0:T(8,128)(2,1)S(1)}, bf16[128,4096]{1,0:T(8,128)(2,1)}, u32[]{:S(2)}, u32[]{:S(2)}) collective-permute-start(bf16[128,4096]{1,0:T(8,128)(2,1)S(1)} %fusion.25), channel_id=1, source_target_pairs={{0,2},{1,3},{2,4},{3,5},{4,6},{5,7},{6,8},{7,9},{8,10},{9,11},{10,... | collective-permute-start | bytes 3145736 | tf_op jit(solution)/shard_map/ppermute | solution.py:19
  12.9 46.8 %collective-permute-start.2 = (bf16[128,4096]{1,0:T(8,128)(2,1)S(1)}, bf16[128,4096]{1,0:T(8,128)(2,1)}, u32[]{:S(2)}, u32[]{:S(2)}) collective-permute-start(bf16[128,4096]{1,0:T(8,128)(2,1)S(1)} %fusion.25), channel_id=1, source_target_pairs={{0,1},{1,2},{2,3},{3,4},{4,5},{5,6},{6,7},{7,8},{8,9},{9,10},{10,1... | collective-permute-start | bytes 3145736 | tf_op jit(solution)/shard_map/ppermute | solution.py:19
  17.3 3.8 %copy-start.12 = (s32[4]{0:T(128)S(1)}, s32[4]{0:T(128)}, u32[]{:S(2)}) copy-start(s32[4]{0:T(128)} %param.11) | copy-start | bytes 52
  73.2 3.3 %copy-start.9 = (bf16[4096,256]{1,0:T(8,128)(2,1)S(1)}, bf16[4096,256]{1,0:T(8,128)(2,1)}, u32[]{:S(2)}) copy-start(bf16[4096,256]{1,0:T(8,128)(2,1)} %all-gather.2.cloned.1.call-done) | copy-start | bytes 6291460
  76.6 3.0 %copy-start.2 = (f32[256,4096]{1,0:T(8,128)}, f32[256,4096]{1,0:T(8,128)S(1)}, u32[]{:S(2)}) copy-start(f32[256,4096]{1,0:T(8,128)S(1)} %negate_select_fusion.8) | copy-start | bytes 12582916
  76.6 3.7 %copy-start = (f32[256,4096]{1,0:T(8,128)S(1)}, f32[256,4096]{1,0:T(8,128)}, u32[]{:S(2)}) copy-start(f32[256,4096]{1,0:T(8,128)} %fusion.26) | copy-start | bytes 12582916
  76.6 5.0 %copy-start.5 = (f32[256,4096]{1,0:T(8,128)S(1)}, f32[256,4096]{1,0:T(8,128)}, u32[]{:S(2)}) copy-start(f32[256,4096]{1,0:T(8,128)} %fusion.5) | copy-start | bytes 12582916
  81.5 2.7 %copy-start.4 = (f32[256,4096]{1,0:T(8,128)S(1)}, f32[256,4096]{1,0:T(8,128)}, u32[]{:S(2)}) copy-start(f32[256,4096]{1,0:T(8,128)} %fusion.2) | copy-start | bytes 12582916
  94.8 6.8 %copy-start.6 = (f32[128,4096]{1,0:T(8,128)S(1)}, f32[128,4096]{1,0:T(8,128)}, u32[]{:S(2)}) copy-start(f32[128,4096]{1,0:T(8,128)} %get-tuple-element.20) | copy-start | bytes 6291460
  94.8 14.1 %copy-start.3 = (f32[256,4096]{1,0:T(8,128)S(1)}, f32[256,4096]{1,0:T(8,128)}, u32[]{:S(2)}) copy-start(f32[256,4096]{1,0:T(8,128)} %copy-done.2) | copy-start | bytes 12582916
  99.5 64.5 %collective-permute-start.1 = (f32[128,4096]{1,0:T(8,128)S(1)}, f32[128,4096]{1,0:T(8,128)S(1)}, u32[]{:S(2)}, u32[]{:S(2)}) collective-permute-start(f32[128,4096]{1,0:T(8,128)S(1)} %convolution_multiply_fusion), channel_id=1, source_target_pairs={{2,0},{3,1},{4,2},{5,3},{6,4},{7,5},{8,6},{9,7},{10,8},{11,9},{12,... | collective-permute-start | bytes 6291464 | tf_op jit(solution)/shard_map/ppermute | solution.py:19
  101.6 7.3 %copy-start.1 = (f32[256,4096]{1,0:T(8,128)S(1)}, f32[256,4096]{1,0:T(8,128)}, u32[]{:S(2)}) copy-start(f32[256,4096]{1,0:T(8,128)} %fusion.26) | copy-start | bytes 12582916
  104.0 93.4 %copy-start.7 = (bf16[128,4096]{1,0:T(8,128)(2,1)S(1)}, bf16[128,4096]{1,0:T(8,128)(2,1)}, u32[]{:S(2)}) copy-start(bf16[128,4096]{1,0:T(8,128)(2,1)} %param.7) | copy-start | bytes 3145732
  104.0 93.4 %copy-start.8 = (bf16[128,4096]{1,0:T(8,128)(2,1)S(1)}, bf16[128,4096]{1,0:T(8,128)(2,1)}, u32[]{:S(2)}) copy-start(bf16[128,4096]{1,0:T(8,128)(2,1)} %param.8) | copy-start | bytes 3145732
  104.0 93.4 %collective-permute-start = (f32[128,4096]{1,0:T(8,128)S(1)}, f32[128,4096]{1,0:T(8,128)S(1)}, u32[]{:S(2)}, u32[]{:S(2)}) collective-permute-start(f32[128,4096]{1,0:T(8,128)S(1)} %convolution_multiply_fusion.1), channel_id=1, source_target_pairs={{1,0},{2,1},{3,2},{4,3},{5,4},{6,5},{7,6},{8,7},{9,8},{10,9},{11,1... | collective-permute-start | bytes 6291464 | tf_op jit(solution)/shard_map/ppermute | solution.py:19
Sparse Core Ops, SparseCore 0:
  10.2 45.0 all-gather.1
  94.9 91.0 reduce-scatter.1
where the time goes:
time: 211 us; the launch traced here: 210 us
  waiting for transfers between devices  124 us (59%)
  matrix products  39.7 us (19%)
  between operations  16.3 us (8%)
  starting transfers between devices  14.2 us (7%)
  other arithmetic  12.2 us (6%)
  local copies, waits for them, and re-layouts  4.02 us (2%)
    ppermute x4, waiting for transfers between devices, shifted(): lax.ppermute(value, axis, [(source, source + steps) for source in range(f...  123 us
    dot_general x4, matrix products, transform(): return jnp.dot(forward_table, held.astype(jnp.float32), precision=highest)  17.2 us
    ppermute x4, starting transfers between devices, shifted(): lax.ppermute(value, axis, [(source, source + steps) for source in range(f...  14.2 us
    dot_general x3, matrix products, back_half(): return jnp.dot(inverse_table, spectrum, precision=highest)  11.2 us
    sub x3, other arithmetic, spectral_product(): real_part = left_real * right_real - jnp.where(leading, 0.0, imag_cross)  6.78 us
    dot_general x2, matrix products, tap_blocks(): lax.dot_general(forward_table, taps_block, (((1,), (1,)), ((), ())), prec...  6.25 us
    dot_general x2, matrix products, shards(): lax.dot_general(spectrum, inverse_table, (((0,), (1,)), ((), ())), precis...  4.99 us
  transfers between devices with their start and end apart: 6, of which 3 were waited for; matrix products, arithmetic and copies ran while one was open for 16% of the time, Pallas kernels for 0%

commit v1 on v0

v1 whole, which is shorter than its diff:
```python
import math
from functools import partial

import jax
import jax.numpy as jnp
import ml_dtypes
import numpy as np
from jax import lax
from jax.experimental import pallas as pl
from jax.experimental.pallas import tpu as pltpu
from jax.sharding import PartitionSpec as P

QUAD = 4
CHUNKS = 2
REACH = 2
TILE = 256
F32 = jnp.float32
BF16 = jnp.bfloat16
SMEM = pl.BlockSpec(memory_space=pltpu.SMEM)
VMEM = pl.BlockSpec(memory_space=pltpu.VMEM)
PARAMS = pltpu.CompilerParams(vmem_limit_bytes=40 * 1024 * 1024)


def split_bf16(table):
    high = table.astype(ml_dtypes.bfloat16)
    low = (table - high.astype(np.float64)).astype(ml_dtypes.bfloat16)
    return high, low


def tables(rows):
    length = 2 * rows
    omega = 2.0 * math.pi * (np.arange(rows) + 0.5) / length
    angle = omega[:, None] * np.arange(length)[None, :]
    forward = np.concatenate([np.cos(angle), -np.sin(angle)], axis=0)
    high, low = split_bf16(forward)
    half = np.concatenate([high[:, :rows], low[:, :rows]], axis=1)
    back_high, back_low = split_bf16(forward[:, :rows].T / rows)
    back = np.concatenate([back_high, back_low], axis=0)
    return np.concatenate([high, low, half, back], axis=0)


def dot(left, right):
    return jnp.dot(left, right, preferred_element_type=F32)


def conj_product(left, right):
    (lr, li), (rr, ri) = left, right
    return lr * rr + li * ri, li * rr - lr * ri


def halves(spectrum):
    rows = spectrum.shape[0] // 2
    return spectrum[:rows], spectrum[rows:]


def add(left, right):
    return left[0] + right[0], left[1] + right[1]


def invert(back, real, imag):
    rows = real.shape[0]
    spectrum = jnp.concatenate([real, imag], axis=0)
    high = spectrum.astype(BF16)
    low = (spectrum - high.astype(F32)).astype(BF16)
    both = dot(back, high)
    return both[:rows] + both[rows:] + dot(back[:rows], low)


def prep_kernel(pieces, offset, pos_ref, left_ref, right_ref, *outs):
    place = pos_ref[0] % QUAD
    count, width = pieces
    for k, out in enumerate(outs):
        member = lax.bitwise_xor(place, k)
        for i in range(count):
            lanes = pl.ds(pl.multiple_of(offset(i, member), 128), width)
            product = left_ref[:, lanes].astype(F32) * right_ref[:, lanes].astype(F32)
            out[:, i * width : (i + 1) * width] = product.astype(BF16)


def halo_kernel(pos_ref, *refs):
    place = pos_ref[0] % QUAD
    out = refs[-1]
    rows = refs[0].shape[0]
    for block in range(REACH):
        for k in range(QUAD):

            @pl.when(lax.bitwise_xor(place, k) == block)
            def _():
                out[block * rows : (block + 1) * rows, :] = refs[k][...]


def conv_kernel(chunk, quads, docs, pos_ref, docs_ref, table_ref, halo_ref, *refs):
    grads, inputs, taps = refs[:QUAD], refs[QUAD : 2 * QUAD], refs[2 * QUAD : 2 * QUAD + quads]
    outs = refs[2 * QUAD + quads : 3 * QUAD + quads]
    terms = refs[3 * QUAD + quads : 3 * QUAD + 2 * quads]
    grad_all, input_all, taps_all, out_all, terms_all = refs[3 * QUAD + 2 * quads :]
    rows, width = grads[0].shape
    length = 2 * rows
    piece = taps[0].shape[0] // CHUNKS
    place, quad = pos_ref[0] % QUAD, pos_ref[0] // QUAD
    joined = []
    for j in range(QUAD + 1):
        same, end = jnp.int32(1), jnp.int32(0)
        for d in range(docs):
            end = end + docs_ref[d]
            same = jnp.where(end == quad * QUAD + j + 1, 0, same)
        joined.append(same.astype(F32))
    for k in range(QUAD):
        at = pl.ds(pl.multiple_of(lax.bitwise_xor(place, k) * rows, rows), rows)
        grad_all[at, :] = grads[k][...]
        input_all[at, :] = inputs[k][...]
    grad_all[QUAD * rows :, :] = halo_ref[...]
    for s in range(quads):
        at = pl.ds(pl.multiple_of((quad + s) % quads * piece, piece), piece)
        taps_all[at, :] = taps[s][chunk * piece : (chunk + 1) * piece, :]
    high, low = table_ref[:length], table_ref[length : 2 * length]
    half, back = table_ref[2 * length : 3 * length], table_ref[3 * length :]
    for first in range(0, width, TILE):
        lanes = slice(first, min(first + TILE, width))
        filters = []
        for segment in range(REACH):
            part = taps_all[lanes, segment * rows : (segment + 1) * rows]
            twice = jnp.concatenate([part, part], axis=1)
            filters.append(
                halves(lax.dot_general(half, twice, (((1,), (1,)), ((), ())), preferred_element_type=F32))
            )
        windows = []
        for j in range(QUAD + 1):
            ahead = grad_all[(j + 1) * rows : (j + 2) * rows, lanes].astype(F32) * joined[j]
            window = jnp.concatenate([grad_all[j * rows : (j + 1) * rows, lanes], ahead.astype(BF16)], axis=0)
            windows.append(dot(high, window) + dot(low, window))
        sums = [None] * REACH
        for j in range(QUAD):
            held = input_all[j * rows : (j + 1) * rows, lanes]
            source = halves(dot(half, jnp.concatenate([held, held], axis=0)))
            near, far = halves(windows[j]), halves(windows[j + 1] * joined[j])
            real, imag = add(conj_product(near, filters[0]), conj_product(far, filters[1]))
            out_all[j * rows : (j + 1) * rows, lanes] = invert(back, real, imag).astype(BF16)
            for segment, window in enumerate((near, far)):
                term = conj_product(window, source)
                sums[segment] = term if j == 0 else add(sums[segment], term)
        for segment in range(REACH):
            lags = invert(back, *sums[segment])
            terms_all[lanes, segment * rows : (segment + 1) * rows] = lags.T
    for k in range(QUAD):
        at = pl.ds(pl.multiple_of(lax.bitwise_xor(place, k) * rows, rows), rows)
        outs[k][...] = out_all[at, :]
    for s in range(quads):
        at = pl.ds(pl.multiple_of((quad + s) % quads * piece, piece), piece)
        terms[s][...] = terms_all[at, :].astype(terms[s].dtype)


def final_kernel(pieces, offsets, pos_ref, key_ref, value_ref, *refs):
    grads, (key_out, value_out) = refs[:-2], refs[-2:]
    place = pos_ref[0] % QUAD
    count, width = pieces
    for chunk in range(CHUNKS):
        for k in range(QUAD):
            member = lax.bitwise_xor(place, k)
            for i in range(count):
                lanes = pl.ds(pl.multiple_of(offsets[chunk](i, member), 128), width)
                grad = grads[chunk * QUAD + k][:, i * width : (i + 1) * width].astype(F32)
                key_out[:, lanes] = (grad * value_ref[:, lanes].astype(F32)).astype(BF16)
                value_out[:, lanes] = (grad * key_ref[:, lanes].astype(F32)).astype(BF16)


def shards(query_gate, key_branch, value_branch, out_grad, filter_taps, doc_blocks):
    blocks = lax.axis_size("ctx")
    quads = blocks // QUAD
    rows, channels = query_gate.shape
    lags = filter_taps.shape[1]
    piece = channels // (QUAD * quads * CHUNKS)
    width = quads * piece
    pos = lax.axis_index("ctx").astype(jnp.int32).reshape(1)
    table = jnp.asarray(tables(rows))
    aligned = piece % 128 == 0

    def grouped(array):
        if aligned:
            return array
        parts = array.reshape(rows, quads, QUAD, CHUNKS, piece)
        return parts.transpose(0, 2, 3, 1, 4).reshape(rows, channels)

    def ungrouped(array):
        if aligned:
            return array
        parts = array.reshape(rows, QUAD, CHUNKS, quads, piece)
        return parts.transpose(0, 3, 1, 2, 4).reshape(rows, channels)

    if aligned:
        pieces = (quads, piece)
        offsets = [lambda i, member, c=c: ((i * QUAD + member) * CHUNKS + c) * piece for c in range(CHUNKS)]
    else:
        pieces = (1, width)
        offsets = [lambda i, member, c=c: (member * CHUNKS + c) * width for c in range(CHUNKS)]

    def to_member(value, k):
        if k == 0:
            return value
        return lax.ppermute(value, "ctx", [(i, i ^ k) for i in range(blocks)])

    def to_quad(value, s):
        if s == 0:
            return value
        return lax.ppermute(value, "ctx", [(i, (i + QUAD * s) % blocks) for i in range(blocks)])

    key_branch, value_branch = grouped(key_branch), grouped(value_branch)
    out_grad, query_gate = grouped(out_grad), grouped(query_gate)
    taps = [to_quad(filter_taps, quads - s if s else 0) for s in range(quads)]

    block_type = jax.ShapeDtypeStruct((rows, width), BF16)

    def prep(chunk, left, right, name):
        sent = pl.pallas_call(
            partial(prep_kernel, pieces, offsets[chunk]),
            out_shape=[block_type] * QUAD,
            in_specs=[SMEM, VMEM, VMEM],
            out_specs=[VMEM] * QUAD,
            compiler_params=PARAMS,
            name=name,
        )(pos, left, right)
        return [to_member(sent[k], k) for k in range(QUAD)]

    grads, inputs, halos = [], [], []
    for chunk in range(CHUNKS):
        grads.append(prep(chunk, out_grad, query_gate, f"gated_grad_{chunk}"))
        inputs.append(prep(chunk, key_branch, value_branch, f"conv_input_{chunk}"))
    results, terms = [], []
    for chunk in range(CHUNKS):
        first_blocks = pl.pallas_call(
            halo_kernel,
            out_shape=jax.ShapeDtypeStruct((REACH * rows, width), BF16),
            in_specs=[SMEM] + [VMEM] * QUAD,
            out_specs=VMEM,
            compiler_params=PARAMS,
            name=f"halo_{chunk}",
        )(pos, *grads[chunk])
        halo = lax.ppermute(first_blocks, "ctx", [(i, i - QUAD) for i in range(QUAD, blocks)])
        done = pl.pallas_call(
            partial(conv_kernel, chunk, quads, doc_blocks.shape[0]),
            out_shape=[block_type] * QUAD
            + [jax.ShapeDtypeStruct((piece, lags), BF16 if s else F32) for s in range(quads)],
            in_specs=[SMEM, SMEM, VMEM, VMEM] + [VMEM] * (2 * QUAD + quads),
            out_specs=[VMEM] * (QUAD + quads),
            scratch_shapes=[
                pltpu.VMEM(((QUAD + REACH) * rows, width), BF16),
                pltpu.VMEM((QUAD * rows, width), BF16),
                pltpu.VMEM((width, lags), BF16),
                pltpu.VMEM((QUAD * rows, width), BF16),
                pltpu.VMEM((width, lags), F32),
            ],
            compiler_params=PARAMS,
            name=f"conv_{chunk}",
        )(pos, doc_blocks, table, halo, *grads[chunk], *inputs[chunk], *taps)
        results.extend(to_member(done[k], k) for k in range(QUAD))
        received = [to_quad(done[QUAD + s], s) for s in range(quads)]
        total = received[0]
        for term in received[1:]:
            total = total + term.astype(F32)
        terms.append(total)
    filter_grad = jnp.concatenate(terms, axis=0) * (1.0 / math.sqrt(rows * blocks))
    step = 32
    key_grad, value_grad = pl.pallas_call(
        partial(final_kernel, pieces, offsets),
        grid=(rows // step,),
        out_shape=[jax.ShapeDtypeStruct((rows, channels), BF16)] * 2,
        in_specs=[SMEM]
        + [pl.BlockSpec((step, channels), lambda i: (i, 0))] * 2
        + [pl.BlockSpec((step, width), lambda i: (i, 0))] * (CHUNKS * QUAD),
        out_specs=[pl.BlockSpec((step, channels), lambda i: (i, 0))] * 2,
        compiler_params=PARAMS,
        name="gate_products",
    )(pos, key_branch, value_branch, *results)
    return (ungrouped(key_grad), ungrouped(value_grad), filter_grad)


def solution(mesh):
    in_specs = (
        P(("groups", "ctx"), None),
        P(("groups", "ctx"), None),
        P(("groups", "ctx"), None),
        P(("groups", "ctx"), None),
        P("ctx", None),
        P("groups"),
    )
    out_specs = (P(("groups", "ctx"), None), P(("groups", "ctx"), None), P(("groups", "ctx"), None))
    return jax.shard_map(shards, mesh=mesh, in_specs=in_specs, out_specs=out_specs, check_vma=False)
```

time: 211 us -> 64.8 us (0.31)
  the two profiles are of different devices: /device:TPU:23 before, /device:TPU:0 now
where the time goes in v1:
time: 64.8 us; the launch traced here: 64.6 us
  starting transfers between devices  32.3 us (50%)
  waiting for transfers between devices  16.3 us (25%)
  Pallas kernels  11.9 us (18%)
  local copies, waits for them, and re-layouts  2.47 us (4%)
  between operations  0.85 us (1%)
  other arithmetic  0.79 us (1%)
    ppermute x9, starting transfers between devices, to_quad(): lax.ppermute(value, 'ctx', [(i, (i + QUAD * s) % blocks) for i in range(b...  16.9 us
    ppermute x18, starting transfers between devices, to_member(): return lax.ppermute(value, 'ctx', [(i, i ^ k) for i in range(blocks)])  12.7 us
    ppermute x18, waiting for transfers between devices, to_member(): return lax.ppermute(value, 'ctx', [(i, i ^ k) for i in range(blocks)])  10.7 us
    pallas_call x2, Pallas kernels, shards(): pl.pallas_call(partial(conv_kernel, chunk, quads, doc_blocks.shape[0]), o...  8.24 us
    ppermute x9, waiting for transfers between devices, to_quad(): lax.ppermute(value, 'ctx', [(i, (i + QUAD * s) % blocks) for i in range(b...  5.56 us
    ppermute x2, starting transfers between devices, shards(): lax.ppermute(first_blocks, 'ctx', [(i, i - QUAD) for i in range(QUAD, blo...  2.7 us
    unnamed x14, local copies, waits for them, and re-layouts  2.47 us
    pallas_call x1, Pallas kernels, shards(): pl.pallas_call(partial(final_kernel, pieces, offsets), grid=(rows // step...  2.42 us
  transfers between devices with their start and end apart: 29, of which 9 were waited for; matrix products, arithmetic and copies ran while one was open for 1% of the time, Pallas kernels for 15%

profile of v1, /device:TPU:0, one launch (start us, length us, event | category | flops | bytes accessed | tf_op | source)
XLA Modules:
  0.0 64.6 jit_solution(4045120962626897127)
XLA Ops:
  0.6 3.1 %collective-permute-start.9 = (bf16[256,256]{1,0:T(8,128)(2,1)}, bf16[256,256]{1,0:T(8,128)(2,1)S(1)}, u32[]{:S(2)}, u32[]{:S(2)}) collective-permute-start(bf16[256,256]{1,0:T(8,128)(2,1)} %refs_8_.3), channel_id=1, source_target_pairs={{0,4},{1,5},{2,6},{3,7},{4,8},{5,9},{6,10},{7,11},{8,12},{9,13},{1... | collective-permute-start | bytes 393224 | tf_op jit(solution)/shard_map/ppermute | solution.py:205
  3.7 1.2 %copy-done.2 = bf16[128,4096]{1,0:T(8,128)(2,1)S(1)} copy-done((bf16[128,4096]{1,0:T(8,128)(2,1)S(1)}, bf16[128,4096]{1,0:T(8,128)(2,1)}, u32[]{:S(2)}) %copy-start.2) | copy-done | bytes 1048600
  4.9 1.2 %copy-done.3 = bf16[128,4096]{1,0:T(8,128)(2,1)S(1)} copy-done((bf16[128,4096]{1,0:T(8,128)(2,1)S(1)}, bf16[128,4096]{1,0:T(8,128)(2,1)}, u32[]{:S(2)}) %copy-start.3) | copy-done | bytes 1048600
  6.2 0.3 gated_grad_0.1
  6.4 0.1 collective-permute-start
  6.5 1.6 %collective-permute-start.1 = (bf16[128,512]{1,0:T(8,128)(2,1)S(1)}, bf16[128,512]{1,0:T(8,128)(2,1)S(1)}, u32[]{:S(2)}, u32[]{:S(2)}) collective-permute-start(bf16[128,512]{1,0:T(8,128)(2,1)S(1)} %get-tuple-element.39), channel_id=1, source_target_pairs={{0,2},{1,3},{2,0},{3,1},{4,6},{5,7},{6,4},{7,5},{8,10},{9,11},{10,... | collective-permute-start | bytes 393224 | tf_op jit(solution)/shard_map/ppermute | solution.py:200
  8.1 0.3 collective-permute-start.2
  8.4 2.6 %collective-permute-start.8 = (bf16[256,256]{1,0:T(8,128)(2,1)S(1)}, bf16[256,256]{1,0:T(8,128)(2,1)S(1)}, u32[]{:S(2)}, u32[]{:S(2)}) collective-permute-start(bf16[256,256]{1,0:T(8,128)(2,1)S(1)} %copy-done.5), channel_id=1, source_target_pairs={{0,8},{1,9},{2,10},{3,11},{4,12},{5,13},{6,14},{7,15},{8,0},{9,1},... | collective-permute-start | bytes 393224 | tf_op jit(solution)/shard_map/ppermute | solution.py:205
  11.0 0.3 gated_grad_1.1
  11.2 0.0 collective-permute-done.9.refs_11_
  11.3 0.1 collective-permute-start.13
  11.4 0.0 collective-permute-done.refs_1_
  11.4 1.5 %collective-permute-start.14 = (bf16[128,512]{1,0:T(8,128)(2,1)S(1)}, bf16[128,512]{1,0:T(8,128)(2,1)S(1)}, u32[]{:S(2)}, u32[]{:S(2)}) collective-permute-start(bf16[128,512]{1,0:T(8,128)(2,1)S(1)} %get-tuple-element.51), channel_id=1, source_target_pairs={{0,2},{1,3},{2,0},{3,1},{4,6},{5,7},{6,4},{7,5},{8,10},{9,11},{10,... | collective-permute-start | bytes 393224 | tf_op jit(solution)/shard_map/ppermute | solution.py:200
  12.9 0.3 collective-permute-start.15
  13.2 1.6 %collective-permute-done.2.refs_3_ = bf16[128,512]{1,0:T(8,128)(2,1)S(1)} collective-permute-done((bf16[128,512]{1,0:T(8,128)(2,1)S(1)}, bf16[128,512]{1,0:T(8,128)(2,1)S(1)}, u32[]{:S(2)}, u32[]{:S(2)}) %collective-permute-start.2) | collective-permute-done | bytes 131104 | tf_op jit(solution)/shard_map/ppermute | solution.py:200
  14.8 2.2 %collective-permute-start.7 = (bf16[256,256]{1,0:T(8,128)(2,1)S(1)}, bf16[256,256]{1,0:T(8,128)(2,1)S(1)}, u32[]{:S(2)}, u32[]{:S(2)}) collective-permute-start(bf16[256,256]{1,0:T(8,128)(2,1)S(1)} %copy-done.5), channel_id=1, source_target_pairs={{0,12},{1,13},{2,14},{3,15},{4,0},{5,1},{6,2},{7,3},{8,4},{9,5},{1... | collective-permute-start | bytes 393224 | tf_op jit(solution)/shard_map/ppermute | solution.py:205
  17.0 0.8 %collective-permute-done.8.refs_10_ = bf16[256,256]{1,0:T(8,128)(2,1)S(1)} collective-permute-done((bf16[256,256]{1,0:T(8,128)(2,1)S(1)}, bf16[256,256]{1,0:T(8,128)(2,1)S(1)}, u32[]{:S(2)}, u32[]{:S(2)}) %collective-permute-start.8) | collective-permute-done | bytes 131104 | tf_op jit(solution)/shard_map/ppermute | solution.py:205
  17.8 1.3 %collective-permute-start.3 = (bf16[256,512]{1,0:T(8,128)(2,1)S(1)}, bf16[256,512]{1,0:T(8,128)(2,1)S(1)}, u32[]{:S(2)}, u32[]{:S(2)}) collective-permute-start(bf16[256,512]{1,0:T(8,128)(2,1)S(1)} %halo_0.1), channel_id=1, source_target_pairs={{4,0},{5,1},{6,2},{7,3},{8,4},{9,5},{10,6},{11,7},{12,8},{13,9},{1... | collective-permute-start | bytes 786440 | tf_op jit(solution)/shard_map/ppermute | solution.py:238
  19.1 0.3 conv_input_0.1
  19.4 0.0 collective-permute-done.13.refs_1_
  19.4 0.1 collective-permute-start.4
  19.5 1.6 %collective-permute-start.5 = (bf16[128,512]{1,0:T(8,128)(2,1)S(1)}, bf16[128,512]{1,0:T(8,128)(2,1)S(1)}, u32[]{:S(2)}, u32[]{:S(2)}) collective-permute-start(bf16[128,512]{1,0:T(8,128)(2,1)S(1)} %get-tuple-element.43), channel_id=1, source_target_pairs={{0,2},{1,3},{2,0},{3,1},{4,6},{5,7},{6,4},{7,5},{8,10},{9,11},{10,... | collective-permute-start | bytes 393224 | tf_op jit(solution)/shard_map/ppermute | solution.py:200
  21.1 1.0 %collective-permute-start.6 = (bf16[128,512]{1,0:T(8,128)(2,1)S(1)}, bf16[128,512]{1,0:T(8,128)(2,1)S(1)}, u32[]{:S(2)}, u32[]{:S(2)}) collective-permute-start(bf16[128,512]{1,0:T(8,128)(2,1)S(1)} %get-tuple-element.44), channel_id=1, source_target_pairs={{0,3},{1,2},{2,1},{3,0},{4,7},{5,6},{6,5},{7,4},{8,11},{9,10},{10,... | collective-permute-start | bytes 393224 | tf_op jit(solution)/shard_map/ppermute | solution.py:200
  22.1 0.0 copy-start.4
  22.2 1.4 %collective-permute-start.16 = (bf16[256,512]{1,0:T(8,128)(2,1)S(1)}, bf16[256,512]{1,0:T(8,128)(2,1)S(1)}, u32[]{:S(2)}, u32[]{:S(2)}) collective-permute-start(bf16[256,512]{1,0:T(8,128)(2,1)S(1)} %halo_1.1), channel_id=1, source_target_pairs={{4,0},{5,1},{6,2},{7,3},{8,4},{9,5},{10,6},{11,7},{12,8},{13,9},{1... | collective-permute-start | bytes 786440 | tf_op jit(solution)/shard_map/ppermute | solution.py:238
  23.6 0.3 conv_input_1.1
  23.9 0.1 collective-permute-start.17
  24.0 1.9 %collective-permute-done.5.refs_6_ = bf16[128,512]{1,0:T(8,128)(2,1)S(1)} collective-permute-done((bf16[128,512]{1,0:T(8,128)(2,1)S(1)}, bf16[128,512]{1,0:T(8,128)(2,1)S(1)}, u32[]{:S(2)}, u32[]{:S(2)}) %collective-permute-start.5) | collective-permute-done | bytes 131104 | tf_op jit(solution)/shard_map/ppermute | solution.py:200
  25.9 1.5 %collective-permute-start.18 = (bf16[128,512]{1,0:T(8,128)(2,1)S(1)}, bf16[128,512]{1,0:T(8,128)(2,1)S(1)}, u32[]{:S(2)}, u32[]{:S(2)}) collective-permute-start(bf16[128,512]{1,0:T(8,128)(2,1)S(1)} %get-tuple-element.55), channel_id=1, source_target_pairs={{0,2},{1,3},{2,0},{3,1},{4,6},{5,7},{6,4},{7,5},{8,10},{9,11},{10,... | collective-permute-start | bytes 393224 | tf_op jit(solution)/shard_map/ppermute | solution.py:200
  27.4 0.4 collective-permute-done.6.refs_7_
  27.8 2.2 %collective-permute-start.19 = (bf16[128,512]{1,0:T(8,128)(2,1)S(1)}, bf16[128,512]{1,0:T(8,128)(2,1)S(1)}, u32[]{:S(2)}, u32[]{:S(2)}) collective-permute-start(bf16[128,512]{1,0:T(8,128)(2,1)S(1)} %get-tuple-element.56), channel_id=1, source_target_pairs={{0,3},{1,2},{2,1},{3,0},{4,7},{5,6},{6,5},{7,4},{8,11},{9,10},{10,... | collective-permute-start | bytes 393224 | tf_op jit(solution)/shard_map/ppermute | solution.py:200
  30.0 4.1 %conv_0.1 = (bf16[128,512]{1,0:T(8,128)(2,1)S(1)}, bf16[128,512]{1,0:T(8,128)(2,1)S(1)}, bf16[128,512]{1,0:T(8,128)(2,1)S(1)}, bf16[128,512]{1,0:T(8,128)(2,1)S(...) custom-call(s32[1]{0:T(128)} %bitcast.pos_ref, ...), custom_call_target="tpu_custom_call" | custom-call | tf_op jit(solution)/shard_map/conv_0/pallas_call | solution.py:239
  34.1 2.7 %collective-permute-start.23 = (bf16[128,256]{1,0:T(8,128)(2,1)S(1)}, bf16[128,256]{1,0:T(8,128)(2,1)S(1)}, u32[]{:S(2)}, u32[]{:S(2)}) collective-permute-start(bf16[128,256]{1,0:T(8,128)(2,1)S(1)} %get-tuple-element.64), channel_id=1, source_target_pairs={{0,4},{1,5},{2,6},{3,7},{4,8},{5,9},{6,10},{7,11},{8,12},{9,13},{1... | collective-permute-start | bytes 196616 | tf_op jit(solution)/shard_map/ppermute | solution.py:205
  36.8 2.4 %collective-permute-start.25 = (bf16[128,256]{1,0:T(8,128)(2,1)S(1)}, bf16[128,256]{1,0:T(8,128)(2,1)S(1)}, u32[]{:S(2)}, u32[]{:S(2)}) collective-permute-start(bf16[128,256]{1,0:T(8,128)(2,1)S(1)} %get-tuple-element.66), channel_id=1, source_target_pairs={{0,12},{1,13},{2,14},{3,15},{4,0},{5,1},{6,2},{7,3},{8,4},{9,5},{1... | collective-permute-start | bytes 196616 | tf_op jit(solution)/shard_map/ppermute | solution.py:205
  39.3 0.6 collective-permute-start.11
  39.8 4.1 %conv_1.1 = (bf16[128,512]{1,0:T(8,128)(2,1)S(1)}, bf16[128,512]{1,0:T(8,128)(2,1)S(1)}, bf16[128,512]{1,0:T(8,128)(2,1)S(1)}, bf16[128,512]{1,0:T(8,128)(2,1)S(...) custom-call(s32[1]{0:T(128)} %bitcast.pos_ref, ...), custom_call_target="tpu_custom_call" | custom-call | tf_op jit(solution)/shard_map/conv_1/pallas_call | solution.py:239
  44.0 0.1 collective-permute-start.26
  44.1 2.5 %collective-permute-start.27 = (bf16[128,256]{1,0:T(8,128)(2,1)S(1)}, bf16[128,256]{1,0:T(8,128)(2,1)S(1)}, u32[]{:S(2)}, u32[]{:S(2)}) collective-permute-start(bf16[128,256]{1,0:T(8,128)(2,1)S(1)} %get-tuple-element.69), channel_id=1, source_target_pairs={{0,8},{1,9},{2,10},{3,11},{4,12},{5,13},{6,14},{7,15},{8,0},{9,1},... | collective-permute-start | bytes 196616 | tf_op jit(solution)/shard_map/ppermute | solution.py:205
  46.5 1.4 %collective-permute-start.28 = (bf16[128,256]{1,0:T(8,128)(2,1)S(1)}, bf16[128,256]{1,0:T(8,128)(2,1)S(1)}, u32[]{:S(2)}, u32[]{:S(2)}) collective-permute-start(bf16[128,256]{1,0:T(8,128)(2,1)S(1)} %get-tuple-element.70), channel_id=1, source_target_pairs={{0,12},{1,13},{2,14},{3,15},{4,0},{5,1},{6,2},{7,3},{8,4},{9,5},{1... | collective-permute-start | bytes 196616 | tf_op jit(solution)/shard_map/ppermute | solution.py:205
  48.0 2.9 %collective-permute-done.26 = bf16[128,256]{1,0:T(8,128)(2,1)S(1)} collective-permute-done((bf16[128,256]{1,0:T(8,128)(2,1)S(1)}, bf16[128,256]{1,0:T(8,128)(2,1)S(1)}, u32[]{:S(2)}, u32[]{:S(2)}) %collective-permute-start.26) | collective-permute-done | bytes 65568 | tf_op jit(solution)/shard_map/ppermute | solution.py:205
  50.8 1.9 %collective-permute-done.27 = bf16[128,256]{1,0:T(8,128)(2,1)S(1)} collective-permute-done((bf16[128,256]{1,0:T(8,128)(2,1)S(1)}, bf16[128,256]{1,0:T(8,128)(2,1)S(1)}, u32[]{:S(2)}, u32[]{:S(2)}) %collective-permute-start.27) | collective-permute-done | bytes 65568 | tf_op jit(solution)/shard_map/ppermute | solution.py:205
  52.7 1.5 %collective-permute-start.21 = (bf16[128,512]{1,0:T(8,128)(2,1)S(1)}, bf16[128,512]{1,0:T(8,128)(2,1)S(1)}, u32[]{:S(2)}, u32[]{:S(2)}) collective-permute-start(bf16[128,512]{1,0:T(8,128)(2,1)S(1)} %get-tuple-element.59), channel_id=1, source_target_pairs={{0,2},{1,3},{2,0},{3,1},{4,6},{5,7},{6,4},{7,5},{8,10},{9,11},{10,... | collective-permute-start | bytes 393224 | tf_op jit(solution)/shard_map/ppermute | solution.py:200
  54.2 0.3 collective-permute-start.22
  54.6 0.7 %maximum_multiply_fusion = f32[256,256]{1,0:T(8,128)} fusion(f32[128,256]{1,0:T(8,128)S(1)} %convert_add_fusion, f32[128,256]{1,0:T(8,128)S(1)} %convert_add_fusion.1), kind=kLoop, calls=%fused_computation | loop fusion | flops 131072 | bytes 524288 | tf_op jit(solution)/shard_map/mul | solution.py:261
  55.3 1.2 %collective-permute-done.12.refs_3_ = bf16[128,512]{1,0:T(8,128)(2,1)S(1)} collective-permute-done((bf16[128,512]{1,0:T(8,128)(2,1)S(1)}, bf16[128,512]{1,0:T(8,128)(2,1)S(1)}, u32[]{:S(2)}, u32[]{:S(2)}) %collective-permute-start.12) | collective-permute-done | bytes 131104 | tf_op jit(solution)/shard_map/ppermute | solution.py:200
  56.5 2.9 %collective-permute-done.21.refs_6_ = bf16[128,512]{1,0:T(8,128)(2,1)S(1)} collective-permute-done((bf16[128,512]{1,0:T(8,128)(2,1)S(1)}, bf16[128,512]{1,0:T(8,128)(2,1)S(1)}, u32[]{:S(2)}, u32[]{:S(2)}) %collective-permute-start.21) | collective-permute-done | bytes 131104 | tf_op jit(solution)/shard_map/ppermute | solution.py:200
  59.5 2.7 %collective-permute-done.22.refs_7_ = bf16[128,512]{1,0:T(8,128)(2,1)S(1)} collective-permute-done((bf16[128,512]{1,0:T(8,128)(2,1)S(1)}, bf16[128,512]{1,0:T(8,128)(2,1)S(1)}, u32[]{:S(2)}, u32[]{:S(2)}) %collective-permute-start.22) | collective-permute-done | bytes 131104 | tf_op jit(solution)/shard_map/ppermute | solution.py:200
  62.2 2.4 %gate_products.1 = (bf16[128,4096]{1,0:T(8,128)(2,1)}, bf16[128,4096]{1,0:T(8,128)(2,1)}) custom-call(s32[1]{0:T(128)} %bitcast.pos_ref, bf16[128,4096]{1,0:T(8,128)(2,1)S(1)} %copy-done, bf16[128,4096]{1,0:T(8,128)(2,1)S(1)} %copy-done.1, bf16[128,512]{1,0:T(8,128)(2,1)S(1)} %get-tuple-element.45.refs_0_, ...), custom_call_target="tpu_custom_call" | custom-call | tf_op jit(solution)/shard_map/gate_products/pallas_call | solution.py:263
  (36 shorter events, 0.2 us)
Async XLA Ops:
  0.6 10.6 %collective-permute-start.9 = (bf16[256,256]{1,0:T(8,128)(2,1)}, bf16[256,256]{1,0:T(8,128)(2,1)S(1)}, u32[]{:S(2)}, u32[]{:S(2)}) collective-permute-start(bf16[256,256]{1,0:T(8,128)(2,1)} %refs_8_.3), channel_id=1, source_target_pairs={{0,4},{1,5},{2,6},{3,7},{4,8},{5,9},{6,10},{7,11},{8,12},{9,13},{1... | collective-permute-start | bytes 393224 | tf_op jit(solution)/shard_map/ppermute | solution.py:205
  3.7 1.2 %copy-start.2 = (bf16[128,4096]{1,0:T(8,128)(2,1)S(1)}, bf16[128,4096]{1,0:T(8,128)(2,1)}, u32[]{:S(2)}) copy-start(bf16[128,4096]{1,0:T(8,128)(2,1)} %left_ref.6) | copy-start | bytes 3145732
  4.9 1.2 %copy-start.3 = (bf16[128,4096]{1,0:T(8,128)(2,1)S(1)}, bf16[128,4096]{1,0:T(8,128)(2,1)}, u32[]{:S(2)}) copy-start(bf16[128,4096]{1,0:T(8,128)(2,1)} %right_ref.6) | copy-start | bytes 3145732
  6.2 2.2 %copy-start.5 = (bf16[256,256]{1,0:T(8,128)(2,1)S(1)}, bf16[256,256]{1,0:T(8,128)(2,1)}, u32[]{:S(2)}) copy-start(bf16[256,256]{1,0:T(8,128)(2,1)} %refs_8_.3) | copy-start | bytes 393220
  6.4 5.0 %collective-permute-start = (bf16[128,512]{1,0:T(8,128)(2,1)S(1)}, bf16[128,512]{1,0:T(8,128)(2,1)S(1)}, u32[]{:S(2)}, u32[]{:S(2)}) collective-permute-start(bf16[128,512]{1,0:T(8,128)(2,1)S(1)} %get-tuple-element.38), channel_id=1, source_target_pairs={{0,1},{1,0},{2,3},{3,2},{4,5},{5,4},{6,7},{7,6},{8,9},{9,8},{10,11... | collective-permute-start | bytes 393224 | tf_op jit(solution)/shard_map/ppermute | solution.py:200
  6.5 6.4 %collective-permute-start.1 = (bf16[128,512]{1,0:T(8,128)(2,1)S(1)}, bf16[128,512]{1,0:T(8,128)(2,1)S(1)}, u32[]{:S(2)}, u32[]{:S(2)}) collective-permute-start(bf16[128,512]{1,0:T(8,128)(2,1)S(1)} %get-tuple-element.39), channel_id=1, source_target_pairs={{0,2},{1,3},{2,0},{3,1},{4,6},{5,7},{6,4},{7,5},{8,10},{9,11},{10,... | collective-permute-start | bytes 393224 | tf_op jit(solution)/shard_map/ppermute | solution.py:200
  8.1 11.0 %copy-start = (bf16[128,4096]{1,0:T(8,128)(2,1)S(1)}, bf16[128,4096]{1,0:T(8,128)(2,1)}, u32[]{:S(2)}) copy-start(bf16[128,4096]{1,0:T(8,128)(2,1)} %key_ref.1) | copy-start | bytes 3145732
  8.1 11.0 %copy-start.1 = (bf16[128,4096]{1,0:T(8,128)(2,1)S(1)}, bf16[128,4096]{1,0:T(8,128)(2,1)}, u32[]{:S(2)}) copy-start(bf16[128,4096]{1,0:T(8,128)(2,1)} %value_ref.1) | copy-start | bytes 3145732
  8.1 6.7 %collective-permute-start.2 = (bf16[128,512]{1,0:T(8,128)(2,1)S(1)}, bf16[128,512]{1,0:T(8,128)(2,1)S(1)}, u32[]{:S(2)}, u32[]{:S(2)}) collective-permute-start(bf16[128,512]{1,0:T(8,128)(2,1)S(1)} %get-tuple-element.40), channel_id=1, source_target_pairs={{0,3},{1,2},{2,1},{3,0},{4,7},{5,6},{6,5},{7,4},{8,11},{9,10},{10,... | collective-permute-start | bytes 393224 | tf_op jit(solution)/shard_map/ppermute | solution.py:200
  8.4 9.5 %collective-permute-start.8 = (bf16[256,256]{1,0:T(8,128)(2,1)S(1)}, bf16[256,256]{1,0:T(8,128)(2,1)S(1)}, u32[]{:S(2)}, u32[]{:S(2)}) collective-permute-start(bf16[256,256]{1,0:T(8,128)(2,1)S(1)} %copy-done.5), channel_id=1, source_target_pairs={{0,8},{1,9},{2,10},{3,11},{4,12},{5,13},{6,14},{7,15},{8,0},{9,1},... | collective-permute-start | bytes 393224 | tf_op jit(solution)/shard_map/ppermute | solution.py:205
  11.3 8.2 %collective-permute-start.13 = (bf16[128,512]{1,0:T(8,128)(2,1)S(1)}, bf16[128,512]{1,0:T(8,128)(2,1)S(1)}, u32[]{:S(2)}, u32[]{:S(2)}) collective-permute-start(bf16[128,512]{1,0:T(8,128)(2,1)S(1)} %get-tuple-element.50), channel_id=1, source_target_pairs={{0,1},{1,0},{2,3},{3,2},{4,5},{5,4},{6,7},{7,6},{8,9},{9,8},{10,11... | collective-permute-start | bytes 393224 | tf_op jit(solution)/shard_map/ppermute | solution.py:200
  11.4 8.1 %collective-permute-start.14 = (bf16[128,512]{1,0:T(8,128)(2,1)S(1)}, bf16[128,512]{1,0:T(8,128)(2,1)S(1)}, u32[]{:S(2)}, u32[]{:S(2)}) collective-permute-start(bf16[128,512]{1,0:T(8,128)(2,1)S(1)} %get-tuple-element.51), channel_id=1, source_target_pairs={{0,2},{1,3},{2,0},{3,1},{4,6},{5,7},{6,4},{7,5},{8,10},{9,11},{10,... | collective-permute-start | bytes 393224 | tf_op jit(solution)/shard_map/ppermute | solution.py:200
  12.9 8.2 %collective-permute-start.15 = (bf16[128,512]{1,0:T(8,128)(2,1)S(1)}, bf16[128,512]{1,0:T(8,128)(2,1)S(1)}, u32[]{:S(2)}, u32[]{:S(2)}) collective-permute-start(bf16[128,512]{1,0:T(8,128)(2,1)S(1)} %get-tuple-element.52), channel_id=1, source_target_pairs={{0,3},{1,2},{2,1},{3,0},{4,7},{5,6},{6,5},{7,4},{8,11},{9,10},{10,... | collective-permute-start | bytes 393224 | tf_op jit(solution)/shard_map/ppermute | solution.py:200
  14.8 7.4 %collective-permute-start.7 = (bf16[256,256]{1,0:T(8,128)(2,1)S(1)}, bf16[256,256]{1,0:T(8,128)(2,1)S(1)}, u32[]{:S(2)}, u32[]{:S(2)}) collective-permute-start(bf16[256,256]{1,0:T(8,128)(2,1)S(1)} %copy-done.5), channel_id=1, source_target_pairs={{0,12},{1,13},{2,14},{3,15},{4,0},{5,1},{6,2},{7,3},{8,4},{9,5},{1... | collective-permute-start | bytes 393224 | tf_op jit(solution)/shard_map/ppermute | solution.py:205
  17.8 12.1 %collective-permute-start.3 = (bf16[256,512]{1,0:T(8,128)(2,1)S(1)}, bf16[256,512]{1,0:T(8,128)(2,1)S(1)}, u32[]{:S(2)}, u32[]{:S(2)}) collective-permute-start(bf16[256,512]{1,0:T(8,128)(2,1)S(1)} %halo_0.1), channel_id=1, source_target_pairs={{4,0},{5,1},{6,2},{7,3},{8,4},{9,5},{10,6},{11,7},{12,8},{13,9},{1... | collective-permute-start | bytes 786440 | tf_op jit(solution)/shard_map/ppermute | solution.py:238
  19.4 4.4 %collective-permute-start.4 = (bf16[128,512]{1,0:T(8,128)(2,1)S(1)}, bf16[128,512]{1,0:T(8,128)(2,1)S(1)}, u32[]{:S(2)}, u32[]{:S(2)}) collective-permute-start(bf16[128,512]{1,0:T(8,128)(2,1)S(1)} %get-tuple-element.42), channel_id=1, source_target_pairs={{0,1},{1,0},{2,3},{3,2},{4,5},{5,4},{6,7},{7,6},{8,9},{9,8},{10,11... | collective-permute-start | bytes 393224 | tf_op jit(solution)/shard_map/ppermute | solution.py:200
  19.5 6.4 %collective-permute-start.5 = (bf16[128,512]{1,0:T(8,128)(2,1)S(1)}, bf16[128,512]{1,0:T(8,128)(2,1)S(1)}, u32[]{:S(2)}, u32[]{:S(2)}) collective-permute-start(bf16[128,512]{1,0:T(8,128)(2,1)S(1)} %get-tuple-element.43), channel_id=1, source_target_pairs={{0,2},{1,3},{2,0},{3,1},{4,6},{5,7},{6,4},{7,5},{8,10},{9,11},{10,... | collective-permute-start | bytes 393224 | tf_op jit(solution)/shard_map/ppermute | solution.py:200
  21.1 6.7 %collective-permute-start.6 = (bf16[128,512]{1,0:T(8,128)(2,1)S(1)}, bf16[128,512]{1,0:T(8,128)(2,1)S(1)}, u32[]{:S(2)}, u32[]{:S(2)}) collective-permute-start(bf16[128,512]{1,0:T(8,128)(2,1)S(1)} %get-tuple-element.44), channel_id=1, source_target_pairs={{0,3},{1,2},{2,1},{3,0},{4,7},{5,6},{6,5},{7,4},{8,11},{9,10},{10,... | collective-permute-start | bytes 393224 | tf_op jit(solution)/shard_map/ppermute | solution.py:200
  22.1 7.8 %copy-start.4 = (bf16[1024,256]{1,0:T(8,128)(2,1)S(1)}, bf16[1024,256]{1,0:T(8,128)(2,1)}, u32[]{:S(2)}) copy-start(bf16[1024,256]{1,0:T(8,128)(2,1)} %constant.8.clone.table_ref) | copy-start | bytes 1572868
  22.2 17.1 %collective-permute-start.16 = (bf16[256,512]{1,0:T(8,128)(2,1)S(1)}, bf16[256,512]{1,0:T(8,128)(2,1)S(1)}, u32[]{:S(2)}, u32[]{:S(2)}) collective-permute-start(bf16[256,512]{1,0:T(8,128)(2,1)S(1)} %halo_1.1), channel_id=1, source_target_pairs={{4,0},{5,1},{6,2},{7,3},{8,4},{9,5},{10,6},{11,7},{12,8},{13,9},{1... | collective-permute-start | bytes 786440 | tf_op jit(solution)/shard_map/ppermute | solution.py:238
  23.9 12.9 %collective-permute-start.17 = (bf16[128,512]{1,0:T(8,128)(2,1)S(1)}, bf16[128,512]{1,0:T(8,128)(2,1)S(1)}, u32[]{:S(2)}, u32[]{:S(2)}) collective-permute-start(bf16[128,512]{1,0:T(8,128)(2,1)S(1)} %get-tuple-element.54), channel_id=1, source_target_pairs={{0,1},{1,0},{2,3},{3,2},{4,5},{5,4},{6,7},{7,6},{8,9},{9,8},{10,11... | collective-permute-start | bytes 393224 | tf_op jit(solution)/shard_map/ppermute | solution.py:200
  25.9 10.9 %collective-permute-start.18 = (bf16[128,512]{1,0:T(8,128)(2,1)S(1)}, bf16[128,512]{1,0:T(8,128)(2,1)S(1)}, u32[]{:S(2)}, u32[]{:S(2)}) collective-permute-start(bf16[128,512]{1,0:T(8,128)(2,1)S(1)} %get-tuple-element.55), channel_id=1, source_target_pairs={{0,2},{1,3},{2,0},{3,1},{4,6},{5,7},{6,4},{7,5},{8,10},{9,11},{10,... | collective-permute-start | bytes 393224 | tf_op jit(solution)/shard_map/ppermute | solution.py:200
  27.8 2.2 %copy-start.6 = (s32[4]{0:T(128)S(1)}, s32[4]{0:T(128)}, u32[]{:S(2)}) copy-start(s32[4]{0:T(128)} %docs_ref.3) | copy-start | bytes 52
  27.8 11.5 %collective-permute-start.19 = (bf16[128,512]{1,0:T(8,128)(2,1)S(1)}, bf16[128,512]{1,0:T(8,128)(2,1)S(1)}, u32[]{:S(2)}, u32[]{:S(2)}) collective-permute-start(bf16[128,512]{1,0:T(8,128)(2,1)S(1)} %get-tuple-element.56), channel_id=1, source_target_pairs={{0,3},{1,2},{2,1},{3,0},{4,7},{5,6},{6,5},{7,4},{8,11},{9,10},{10,... | collective-permute-start | bytes 393224 | tf_op jit(solution)/shard_map/ppermute | solution.py:200
  34.1 9.9 %collective-permute-start.23 = (bf16[128,256]{1,0:T(8,128)(2,1)S(1)}, bf16[128,256]{1,0:T(8,128)(2,1)S(1)}, u32[]{:S(2)}, u32[]{:S(2)}) collective-permute-start(bf16[128,256]{1,0:T(8,128)(2,1)S(1)} %get-tuple-element.64), channel_id=1, source_target_pairs={{0,4},{1,5},{2,6},{3,7},{4,8},{5,9},{6,10},{7,11},{8,12},{9,13},{1... | collective-permute-start | bytes 196616 | tf_op jit(solution)/shard_map/ppermute | solution.py:205
  36.8 7.2 %collective-permute-start.24 = (bf16[128,256]{1,0:T(8,128)(2,1)S(1)}, bf16[128,256]{1,0:T(8,128)(2,1)S(1)}, u32[]{:S(2)}, u32[]{:S(2)}) collective-permute-start(bf16[128,256]{1,0:T(8,128)(2,1)S(1)} %get-tuple-element.65), channel_id=1, source_target_pairs={{0,8},{1,9},{2,10},{3,11},{4,12},{5,13},{6,14},{7,15},{8,0},{9,1},... | collective-permute-start | bytes 196616 | tf_op jit(solution)/shard_map/ppermute | solution.py:205
  36.8 9.7 %collective-permute-start.25 = (bf16[128,256]{1,0:T(8,128)(2,1)S(1)}, bf16[128,256]{1,0:T(8,128)(2,1)S(1)}, u32[]{:S(2)}, u32[]{:S(2)}) collective-permute-start(bf16[128,256]{1,0:T(8,128)(2,1)S(1)} %get-tuple-element.66), channel_id=1, source_target_pairs={{0,12},{1,13},{2,14},{3,15},{4,0},{5,1},{6,2},{7,3},{8,4},{9,5},{1... | collective-permute-start | bytes 196616 | tf_op jit(solution)/shard_map/ppermute | solution.py:205
  39.3 15.0 %collective-permute-start.10 = (bf16[128,512]{1,0:T(8,128)(2,1)S(1)}, bf16[128,512]{1,0:T(8,128)(2,1)S(1)}, u32[]{:S(2)}, u32[]{:S(2)}) collective-permute-start(bf16[128,512]{1,0:T(8,128)(2,1)S(1)} %get-tuple-element.46), channel_id=1, source_target_pairs={{0,1},{1,0},{2,3},{3,2},{4,5},{5,4},{6,7},{7,6},{8,9},{9,8},{10,11... | collective-permute-start | bytes 393224 | tf_op jit(solution)/shard_map/ppermute | solution.py:200
  39.3 16.1 %collective-permute-start.11 = (bf16[128,512]{1,0:T(8,128)(2,1)S(1)}, bf16[128,512]{1,0:T(8,128)(2,1)S(1)}, u32[]{:S(2)}, u32[]{:S(2)}) collective-permute-start(bf16[128,512]{1,0:T(8,128)(2,1)S(1)} %get-tuple-element.47), channel_id=1, source_target_pairs={{0,2},{1,3},{2,0},{3,1},{4,6},{5,7},{6,4},{7,5},{8,10},{9,11},{10,... | collective-permute-start | bytes 393224 | tf_op jit(solution)/shard_map/ppermute | solution.py:200
  44.0 6.8 %collective-permute-start.26 = (bf16[128,256]{1,0:T(8,128)(2,1)S(1)}, bf16[128,256]{1,0:T(8,128)(2,1)S(1)}, u32[]{:S(2)}, u32[]{:S(2)}) collective-permute-start(bf16[128,256]{1,0:T(8,128)(2,1)S(1)} %get-tuple-element.68), channel_id=1, source_target_pairs={{0,4},{1,5},{2,6},{3,7},{4,8},{5,9},{6,10},{7,11},{8,12},{9,13},{1... | collective-permute-start | bytes 196616 | tf_op jit(solution)/shard_map/ppermute | solution.py:205
  44.1 8.6 %collective-permute-start.27 = (bf16[128,256]{1,0:T(8,128)(2,1)S(1)}, bf16[128,256]{1,0:T(8,128)(2,1)S(1)}, u32[]{:S(2)}, u32[]{:S(2)}) collective-permute-start(bf16[128,256]{1,0:T(8,128)(2,1)S(1)} %get-tuple-element.69), channel_id=1, source_target_pairs={{0,8},{1,9},{2,10},{3,11},{4,12},{5,13},{6,14},{7,15},{8,0},{9,1},... | collective-permute-start | bytes 196616 | tf_op jit(solution)/shard_map/ppermute | solution.py:205
  46.5 6.2 %collective-permute-start.28 = (bf16[128,256]{1,0:T(8,128)(2,1)S(1)}, bf16[128,256]{1,0:T(8,128)(2,1)S(1)}, u32[]{:S(2)}, u32[]{:S(2)}) collective-permute-start(bf16[128,256]{1,0:T(8,128)(2,1)S(1)} %get-tuple-element.70), channel_id=1, source_target_pairs={{0,12},{1,13},{2,14},{3,15},{4,0},{5,1},{6,2},{7,3},{8,4},{9,5},{1... | collective-permute-start | bytes 196616 | tf_op jit(solution)/shard_map/ppermute | solution.py:205
  50.8 5.7 %collective-permute-start.12 = (bf16[128,512]{1,0:T(8,128)(2,1)S(1)}, bf16[128,512]{1,0:T(8,128)(2,1)S(1)}, u32[]{:S(2)}, u32[]{:S(2)}) collective-permute-start(bf16[128,512]{1,0:T(8,128)(2,1)S(1)} %get-tuple-element.48), channel_id=1, source_target_pairs={{0,3},{1,2},{2,1},{3,0},{4,7},{5,6},{6,5},{7,4},{8,11},{9,10},{10,... | collective-permute-start | bytes 393224 | tf_op jit(solution)/shard_map/ppermute | solution.py:200
  52.7 3.9 %collective-permute-start.20 = (bf16[128,512]{1,0:T(8,128)(2,1)S(1)}, bf16[128,512]{1,0:T(8,128)(2,1)S(1)}, u32[]{:S(2)}, u32[]{:S(2)}) collective-permute-start(bf16[128,512]{1,0:T(8,128)(2,1)S(1)} %get-tuple-element.58), channel_id=1, source_target_pairs={{0,1},{1,0},{2,3},{3,2},{4,5},{5,4},{6,7},{7,6},{8,9},{9,8},{10,11... | collective-permute-start | bytes 393224 | tf_op jit(solution)/shard_map/ppermute | solution.py:200
  52.7 6.8 %collective-permute-start.21 = (bf16[128,512]{1,0:T(8,128)(2,1)S(1)}, bf16[128,512]{1,0:T(8,128)(2,1)S(1)}, u32[]{:S(2)}, u32[]{:S(2)}) collective-permute-start(bf16[128,512]{1,0:T(8,128)(2,1)S(1)} %get-tuple-element.59), channel_id=1, source_target_pairs={{0,2},{1,3},{2,0},{3,1},{4,6},{5,7},{6,4},{7,5},{8,10},{9,11},{10,... | collective-permute-start | bytes 393224 | tf_op jit(solution)/shard_map/ppermute | solution.py:200
  54.2 7.9 %collective-permute-start.22 = (bf16[128,512]{1,0:T(8,128)(2,1)S(1)}, bf16[128,512]{1,0:T(8,128)(2,1)S(1)}, u32[]{:S(2)}, u32[]{:S(2)}) collective-permute-start(bf16[128,512]{1,0:T(8,128)(2,1)S(1)} %get-tuple-element.60), channel_id=1, source_target_pairs={{0,3},{1,2},{2,1},{3,0},{4,7},{5,6},{6,5},{7,4},{8,11},{9,10},{10,... | collective-permute-start | bytes 393224 | tf_op jit(solution)/shard_map/ppermute | solution.py:200

commit v2 on v1

v2 whole, which is shorter than its diff:
```python
import math
from functools import partial

import jax
import jax.numpy as jnp
import ml_dtypes
import numpy as np
from jax import lax
from jax.experimental import pallas as pl
from jax.experimental.pallas import tpu as pltpu
from jax.sharding import PartitionSpec as P

QUAD = 4
CHUNKS = 2
REACH = 2
TILE = 256
F32 = jnp.float32
BF16 = jnp.bfloat16
SMEM = pl.BlockSpec(memory_space=pltpu.SMEM)
VMEM = pl.BlockSpec(memory_space=pltpu.VMEM)
HBM = pl.BlockSpec(memory_space=pltpu.HBM)
ANY = pl.BlockSpec(memory_space=pl.ANY)
PARAMS = pltpu.CompilerParams(vmem_limit_bytes=40 * 1024 * 1024)


def halving_order(count):
    order = [0]
    while len(order) < count:
        order = [2 * n for n in order] + [2 * n + 1 for n in order]
    return order


def split_bf16(table):
    high = table.astype(ml_dtypes.bfloat16)
    low = (table - high.astype(np.float64)).astype(ml_dtypes.bfloat16)
    return high, low


def tables(rows):
    length = 2 * rows
    omega = 2.0 * math.pi * (np.arange(rows) + 0.5) / length
    angle = omega[:, None] * np.arange(length)[None, :]
    forward = np.concatenate([np.cos(angle), -np.sin(angle)], axis=0)
    high, low = split_bf16(forward)
    half = np.concatenate([high[:, :rows], low[:, :rows]], axis=1)
    back_high, back_low = split_bf16(forward[:, :rows].T / rows)
    back = np.concatenate([back_high, back_low], axis=0)
    return np.concatenate([high, low, half, back], axis=0)


def dot(left, right):
    return jnp.dot(left, right, preferred_element_type=F32)


def conj_product(left, right):
    (lr, li), (rr, ri) = left, right
    return lr * rr + li * ri, li * rr - lr * ri


def halves(spectrum):
    rows = spectrum.shape[0] // 2
    return spectrum[:rows], spectrum[rows:]


def add(left, right):
    return left[0] + right[0], left[1] + right[1]


def invert(back, real, imag):
    rows = real.shape[0]
    spectrum = jnp.concatenate([real, imag], axis=0)
    high = spectrum.astype(BF16)
    low = (spectrum - high.astype(F32)).astype(BF16)
    both = dot(back, high)
    return both[:rows] + both[rows:] + dot(back[:rows], low)


def cut_products(pieces, offset, sources, held, sems, outs):
    count, width = pieces
    section = held[0].shape[1] // count
    copies = []
    for i in range(count):
        lanes = pl.ds(i * section, section)
        for n, (source, target) in enumerate(zip(sources, held)):
            copies.append(pltpu.make_async_copy(source.at[:, lanes], target.at[:, lanes], sems.at[n, i]))
            copies[-1].start()
    for i in range(count):
        copies[2 * i].wait()
        copies[2 * i + 1].wait()
        for out, side, pair, chunks in outs:
            for n, chunk in enumerate(chunks):
                lanes = pl.ds(pl.multiple_of(offset(chunk, i, pair, side), 128), width)
                first = (n * count + i) * width
                out[:, first : first + width] = held[0][:, lanes] * held[1][:, lanes]


def grad_kernel(pieces, offset, pos_ref, left_hbm, right_hbm, own, near, same, other, left_ref, right_ref, sems):
    place = pos_ref[0] % QUAD
    core, chip = place % 2, place // 2
    every = range(CHUNKS)
    outs = [(same, core, 1 - chip, every), (other, 1 - core, 1 - chip, every)]
    outs += [(near, 1 - core, chip, every), (own, core, chip, every)]
    cut_products(pieces, offset, (left_hbm, right_hbm), (left_ref, right_ref), sems, outs)


def input_kernel(pieces, offset, pos_ref, left_hbm, right_hbm, own, near, *refs):
    far, (left_ref, right_ref, sems) = refs[:-3], refs[-3:]
    rows = own.shape[0]
    place = pos_ref[0] % QUAD
    core, chip = place % 2, place // 2
    outs = [(near, 1 - core, chip, range(CHUNKS)), (own, core, chip, range(CHUNKS))]
    for chunk, out in enumerate(far):
        outs += [(out.at[:rows, :], core, 1 - chip, [chunk]), (out.at[rows:, :], 1 - core, 1 - chip, [chunk])]
    cut_products(pieces, offset, (left_hbm, right_hbm), (left_ref, right_ref), sems, outs)


def pack_kernel(near_ref, came_ref, _, out):
    rows = near_ref.shape[0]
    out[:rows, :] = near_ref[...]
    out[rows:, :] = came_ref[rows:, :]


def filter_kernel(quads, pos_ref, table_ref, *refs):
    parts, out, taps_all = refs[:-2], refs[-2], refs[-1]
    quad = pos_ref[0] // QUAD
    channels, lags = taps_all.shape
    rows = lags // REACH
    half = table_ref[2 * lags : 3 * lags]
    width = channels // CHUNKS
    piece = width // quads
    held = [(part, at) for part in parts for at in range(0, part.shape[0], CHUNKS * piece)]
    for s, (part, first) in zip(halving_order(quads), held):
        for chunk in range(CHUNKS):
            at = pl.ds(pl.multiple_of(chunk * width + lax.bitwise_xor(quad, s) * piece, piece), piece)
            taps_all[at, :] = part[first + chunk * piece : first + (chunk + 1) * piece, :]
    for first in range(0, channels, TILE):
        for segment in range(REACH):
            taps = taps_all[first : first + TILE, segment * rows : (segment + 1) * rows]
            twice = jnp.concatenate([taps, taps], axis=1)
            spectrum = lax.dot_general(half, twice, (((1,), (1,)), ((), ())), preferred_element_type=F32)
            out[segment * lags : (segment + 1) * lags, first : first + TILE] = spectrum


def gate_kernel(*refs):
    del refs


def halo_kernel(chunks, pos_ref, *refs):
    place = pos_ref[0] % QUAD
    held, outs = refs[:QUAD], refs[-chunks:]
    rows, width = held[0].shape[0], outs[0].shape[1]
    for block in range(REACH):
        for k in range(QUAD):

            @pl.when(lax.bitwise_xor(place, k) == block)
            def _():
                for chunk, out in enumerate(outs):
                    out[block * rows : (block + 1) * rows, :] = held[k][:rows, chunk * width : (chunk + 1) * width]


def conv_kernel(chunk, quads, docs, pos_ref, docs_ref, table_ref, halo_ref, filter_ref, *refs):
    grads, (own_ref, far_ref, came_ref) = refs[:QUAD], refs[QUAD : QUAD + 3]
    outs, terms = refs[-6 - QUAD : -6], refs[-6:-4]
    grad_all, input_all, out_all, terms_all = refs[-4:]
    rows, width = grads[0].shape
    length = 2 * rows
    piece = width // quads
    place, quad = pos_ref[0] % QUAD, pos_ref[0] // QUAD
    joined = []
    for j in range(QUAD + 1):
        same, end = jnp.int32(1), jnp.int32(0)
        for d in range(docs):
            end = end + docs_ref[d]
            same = jnp.where(end == quad * QUAD + j + 1, 0, same)
        joined.append(same.astype(F32))
    for k in range(QUAD):
        at = pl.ds(pl.multiple_of(lax.bitwise_xor(place, k) * rows, rows), rows)
        grad_all[at, :] = grads[k][...]
        held = (own_ref, came_ref, far_ref, came_ref)[k]
        input_all[at, :] = held[(k // 3) * rows : (k // 3 + 1) * rows, :]
    grad_all[QUAD * rows :, :] = halo_ref[...]
    high, low = table_ref[:length], table_ref[length : 2 * length]
    half, back = table_ref[2 * length : 3 * length], table_ref[3 * length :]
    for first in range(0, width, TILE):
        lanes = slice(first, min(first + TILE, width))
        filters = [halves(filter_ref[n * length : (n + 1) * length, lanes]) for n in range(REACH)]
        windows = []
        for j in range(QUAD + 1):
            ahead = grad_all[(j + 1) * rows : (j + 2) * rows, lanes].astype(F32) * joined[j]
            window = jnp.concatenate([grad_all[j * rows : (j + 1) * rows, lanes], ahead.astype(BF16)], axis=0)
            windows.append(dot(high, window) + dot(low, window))
        sums = [None] * REACH
        for j in range(QUAD):
            held = input_all[j * rows : (j + 1) * rows, lanes]
            source = halves(dot(half, jnp.concatenate([held, held], axis=0)))
            near, far = halves(windows[j]), halves(windows[j + 1] * joined[j])
            real, imag = add(conj_product(near, filters[0]), conj_product(far, filters[1]))
            out_all[j * rows : (j + 1) * rows, lanes] = invert(back, real, imag).astype(BF16)
            for segment, window in enumerate((near, far)):
                term = conj_product(window, source)
                sums[segment] = term if j == 0 else add(sums[segment], term)
        for segment in range(REACH):
            lags = invert(back, *sums[segment])
            terms_all[lanes, segment * rows : (segment + 1) * rows] = lags.T
    for k in range(QUAD):
        at = pl.ds(pl.multiple_of(lax.bitwise_xor(place, k) * rows, rows), rows)
        outs[k][...] = out_all[at, :]
    for n, s in enumerate(halving_order(quads)):
        at = pl.ds(pl.multiple_of(lax.bitwise_xor(quad, s) * piece, piece), piece)
        sent, n = divmod(n, quads // 2)
        terms[sent][n * piece : (n + 1) * piece, :] = terms_all[at, :].astype(terms[sent].dtype)


def fold_kernel(kept_ref, came_ref, *refs):
    keep_ref, send_ref = refs[-2:]
    half = keep_ref.shape[0]
    keep_ref[...] = kept_ref[:half, :] + came_ref[:half, :].astype(F32)
    send_ref[...] = (kept_ref[half:, :] + came_ref[half:, :].astype(F32)).astype(BF16)


def final_kernel(chunk, pieces, offset, scale, terms, pos_ref, key_ref, value_ref, *refs):
    grads, filters = refs[:QUAD], refs[QUAD : QUAD + terms]
    filter_all, filter_sem, key_all, value_all, sems = refs[-5:]
    key_out, value_out, *filter_out = refs[-8 if terms else -7 : -5]
    place = pos_ref[0] % QUAD
    count, width = pieces
    copies = []
    for n in range(terms // 2):
        kept, came = filters[2 * n], filters[2 * n + 1]
        rows = kept.shape[0]
        filter_all[n * rows : (n + 1) * rows, :] = (kept[...] + came[...].astype(F32)) * scale
    for out in filter_out:
        copies.append(pltpu.make_async_copy(filter_all, out, filter_sem))
        copies[-1].start()
    for k in range(QUAD):
        member = lax.bitwise_xor(place, k)
        for i in range(count):
            n = k * count + i
            lanes = pl.ds(pl.multiple_of(offset(chunk, i, member // 2, member % 2), 128), width)
            held = slice(n * width, (n + 1) * width)
            grad = grads[k][:, i * width : (i + 1) * width]
            key_all[:, held] = grad * value_ref[:, lanes]
            value_all[:, held] = grad * key_ref[:, lanes]
            copies.append(pltpu.make_async_copy(key_all.at[:, held], key_out.at[:, lanes], sems.at[0, n]))
            copies.append(pltpu.make_async_copy(value_all.at[:, held], value_out.at[:, lanes], sems.at[1, n]))
            copies[-2].start()
            copies[-1].start()
    for copy in copies:
        copy.wait()


def shards(query_gate, key_branch, value_branch, out_grad, filter_taps, doc_blocks):
    blocks = lax.axis_size("ctx")
    quads = blocks // QUAD
    rows, channels = query_gate.shape
    lags = filter_taps.shape[1]
    piece = channels // (QUAD * quads * CHUNKS)
    width = quads * piece
    pos = lax.axis_index("ctx").astype(jnp.int32).reshape(1)
    table = jnp.asarray(tables(rows))
    aligned = piece % 128 == 0

    def grouped(array):
        if aligned:
            return array
        parts = array.reshape(rows, quads, QUAD, CHUNKS, piece)
        return parts.transpose(0, 2, 3, 1, 4).reshape(rows, channels)

    def ungrouped(array):
        if aligned:
            return array
        parts = array.reshape(rows, QUAD, CHUNKS, quads, piece)
        return parts.transpose(0, 3, 1, 2, 4).reshape(rows, channels)

    if aligned:
        pieces = (quads, piece)
        offset = lambda chunk, i, pair, side: (((2 * i + pair) * 2 + side) * CHUNKS + chunk) * piece
    else:
        pieces = (1, width)
        offset = lambda chunk, i, pair, side: ((2 * pair + side) * CHUNKS + chunk) * width

    def to_member(value, k):
        return lax.ppermute(value, "ctx", [(i, i ^ k) for i in range(blocks)]) if k else value

    def gate(values, *after):
        return pl.pallas_call(
            gate_kernel,
            out_shape=[jax.ShapeDtypeStruct(value.shape, value.dtype) for value in values],
            in_specs=[ANY] * (len(values) + len(after)),
            out_specs=[ANY] * len(values),
            input_output_aliases={n: n for n in range(len(values))},
            compiler_params=PARAMS,
            name="gate",
        )(*values, *after)

    def to_quad(value, s):
        return to_member(value, QUAD * s)

    key_branch, value_branch = grouped(key_branch), grouped(value_branch)
    out_grad, query_gate = grouped(out_grad), grouped(query_gate)
    parts, step = [filter_taps], quads // 2
    while step:
        held = parts[0] if len(parts) == 1 else jnp.concatenate(parts, axis=0)
        parts, step = [held, to_quad(held, step)], step // 2

    alone, both = jax.ShapeDtypeStruct((rows, width), BF16), jax.ShapeDtypeStruct((rows, CHUNKS * width), BF16)
    def products(kernel, left, right, types, limit, name):
        return pl.pallas_call(
            partial(kernel, pieces, offset),
            out_shape=types,
            in_specs=[SMEM] + [HBM] * 2,
            out_specs=[VMEM] * len(types),
            scratch_shapes=[pltpu.VMEM((rows, channels), BF16)] * 2 + [pltpu.SemaphoreType.DMA((2, pieces[0]))],
            compiler_params=pltpu.CompilerParams(vmem_limit_bytes=limit * 1024 * 1024),
            name=name,
        )(pos, left, right)

    own, near, same, other = products(grad_kernel, out_grad, query_gate, [both] * 4, 60, "gated_grad")
    grads = [own, to_member(near, 1), to_member(same, 2), to_member(other, 3)]
    pair = jax.ShapeDtypeStruct((2 * rows, width), BF16)
    own, near, *far_inputs = products(input_kernel, key_branch, value_branch, [both] * 2 + [pair] * CHUNKS, 40, "conv_input")
    own_input, near_input = own, near
    far_inputs = [to_member(value, 2) for value in far_inputs]
    spectra = pl.pallas_call(
        partial(filter_kernel, quads),
        out_shape=jax.ShapeDtypeStruct((REACH * lags, CHUNKS * width), F32),
        in_specs=[SMEM, VMEM] + [VMEM] * len(parts),
        out_specs=VMEM,
        scratch_shapes=[pltpu.VMEM((CHUNKS * width, lags), BF16)],
        compiler_params=PARAMS,
        name="filter_spectra",
    )(pos, table, *parts)
    first_blocks = pl.pallas_call(
        partial(halo_kernel, CHUNKS),
        out_shape=[jax.ShapeDtypeStruct((REACH * rows, width), BF16)] * CHUNKS,
        in_specs=[SMEM] + [VMEM] * QUAD,
        out_specs=[VMEM] * CHUNKS,
        compiler_params=PARAMS,
        name="halo",
    )(pos, *grads)
    before = first_blocks[0]
    results, chunk_grads, chunk_terms = [], [], []
    whole = lambda *shape: pl.BlockSpec(shape, lambda _: (0,) * len(shape))
    nearest = []
    for chunk in range(CHUNKS):
        halo = lax.ppermute(first_blocks[chunk], "ctx", [(i, i - QUAD) for i in range(QUAD, blocks)])
        share = pl.BlockSpec((rows, width), lambda _, chunk=chunk: (0, chunk))
        forward = pl.pallas_call(
            pack_kernel,
            grid=(1,),
            out_shape=jax.ShapeDtypeStruct((2 * rows, width), BF16),
            in_specs=[share, whole(2 * rows, width), ANY],
            out_specs=whole(2 * rows, width),
            compiler_params=PARAMS,
            name=f"pack_{chunk}",
        )(near_input, far_inputs[chunk], before)
        forward = to_member(forward, 1)
        done = pl.pallas_call(
            partial(conv_kernel, chunk, quads, doc_blocks.shape[0]),
            grid=(1,),
            out_shape=[alone] * QUAD
            + [jax.ShapeDtypeStruct((width // 2, lags), kind) for kind in (F32, BF16)],
            in_specs=[SMEM, SMEM, whole(*table.shape), whole(REACH * rows, width)]
            + [pl.BlockSpec((REACH * lags, width), lambda _, chunk=chunk: (0, chunk))]
            + [share] * (QUAD + 1)
            + [whole(2 * rows, width)] * 2,
            out_specs=[whole(rows, width)] * QUAD + [whole(width // 2, lags)] * 2,
            scratch_shapes=[
                pltpu.VMEM(((QUAD + REACH) * rows, width), BF16),
                pltpu.VMEM((QUAD * rows, width), BF16),
                pltpu.VMEM((QUAD * rows, width), BF16),
                pltpu.VMEM((width, lags), F32),
            ],
            compiler_params=PARAMS,
            name=f"conv_{chunk}",
        )(pos, doc_blocks, table, halo, spectra, *grads, own_input, far_inputs[chunk], forward)
        own, *sent, kept, send = done
        before = kept
        if chunk:
            *sent, send = gate([*sent, send], *chunk_grads[-1][2:], chunk_terms[-1][1])
        chunk_grads.append([own, *[to_member(value, k + 1) for k, value in enumerate(sent)]])
        chunk_terms.append((kept, to_quad(send, 1)))
    filter_grads = []
    for chunk in range(CHUNKS):
        gradients, (kept, came) = chunk_grads[chunk], chunk_terms[chunk]
        step = 1
        while 2 * step < quads:
            step *= 2
            half = kept.shape[0] // 2
            kept, send = pl.pallas_call(
                fold_kernel,
                out_shape=[jax.ShapeDtypeStruct((half, lags), kind) for kind in (F32, BF16)],
                in_specs=[VMEM] * 2 + [ANY] * len(filter_grads[-1:]),
                out_specs=[VMEM] * 2,
                compiler_params=PARAMS,
                name=f"fold_{chunk}_{step}",
            )(kept, came, *filter_grads[-1:])
            came = to_quad(send, step)
        filter_grads += [kept, came]
        last = filter_grads if chunk == CHUNKS - 1 else []
        results = pl.pallas_call(
            partial(final_kernel, chunk, pieces, offset, 1.0 / math.sqrt(rows * blocks), len(last)),
            out_shape=[jax.ShapeDtypeStruct((rows, channels), BF16)] * 2
            + [jax.ShapeDtypeStruct((CHUNKS * piece, lags), F32)] * (len(last) > 0),
            in_specs=[SMEM] + [VMEM] * (2 + QUAD + len(last)) + [HBM] * len(results),
            out_specs=[HBM] * (3 if last else 2),
            scratch_shapes=[
                pltpu.VMEM((CHUNKS * piece, lags), F32),
                pltpu.SemaphoreType.DMA,
                pltpu.VMEM((rows, QUAD * width), BF16),
                pltpu.VMEM((rows, QUAD * width), BF16),
                pltpu.SemaphoreType.DMA((2, QUAD * pieces[0])),
            ],
            input_output_aliases={3 + QUAD + len(last) + n: n for n in range(len(results))},
            compiler_params=PARAMS,
            name=f"gate_products_{chunk}",
        )(pos, key_branch, value_branch, *gradients, *last, *results)
    key_grad, value_grad, filter_grad = results
    return (ungrouped(key_grad), ungrouped(value_grad), filter_grad)


def solution(mesh):
    in_specs = (
        P(("groups", "ctx"), None),
        P(("groups", "ctx"), None),
        P(("groups", "ctx"), None),
        P(("groups", "ctx"), None),
        P("ctx", None),
        P("groups"),
    )
    out_specs = (P(("groups", "ctx"), None), P(("groups", "ctx"), None), P(("groups", "ctx"), None))
    return jax.shard_map(shards, mesh=mesh, in_specs=in_specs, out_specs=out_specs, check_vma=False)
```

time: 64.8 us -> 59.9 us (0.924); the launches traced: 64.6 us -> 59 us
  starting transfers between devices: 32.3 us -> 22.6 us
  waiting for transfers between devices: 16.3 us -> 20.7 us
  Pallas kernels: 11.9 us -> 14.8 us
  local copies, waits for them, and re-layouts: 2.47 us -> 0.05 us
  other arithmetic: 0.79 us -> 0 us
    ppermute x29 -> x21, starting transfers between devices: 32.3 us -> 22.6 us  [the longest x19 20.1 us: to_member(): lax.ppermute(value, 'ctx', [(i, i ^ k) for i in range(blocks)])]
    ppermute x29 -> x21, waiting for transfers between devices: 16.3 us -> 20.7 us  [the longest x19 17.8 us: to_member(): lax.ppermute(value, 'ctx', [(i, i ^ k) for i in range(blocks)])]
    pallas_call x9 -> x13, Pallas kernels: 11.9 us -> 14.8 us  [the longest x2 7.75 us: shards(): pl.pallas_call(partial(conv_kernel, chunk, quads, doc_blocks.shape[0]), g...]
    unnamed x14 -> x13, local copies, waits for them, and re-layouts: 2.47 us -> 0.04 us
    mul x1 -> x0, other arithmetic: 0.73 us -> none  [shards(): jnp.concatenate(terms, axis=0) * (1.0 / math.sqrt(rows * blocks))]
  transfers between devices with their start and end apart: 29 -> 21, of which waited for: 9 -> 7; matrix products, arithmetic and copies ran while one was open for 1% -> 0% of each run, Pallas kernels for 15% -> 18%
where the time goes in v2:
time: 59.9 us; the launch traced here: 59 us
  starting transfers between devices  22.6 us (38%)
  waiting for transfers between devices  20.7 us (35%)
  Pallas kernels  14.8 us (25%)
  between operations  0.88 us (1%)
    ppermute x19, starting transfers between devices, to_member(): lax.ppermute(value, 'ctx', [(i, i ^ k) for i in range(blocks)])  20.1 us
    ppermute x19, waiting for transfers between devices, to_member(): lax.ppermute(value, 'ctx', [(i, i ^ k) for i in range(blocks)])  17.8 us
    pallas_call x2, Pallas kernels, shards(): pl.pallas_call(partial(conv_kernel, chunk, quads, doc_blocks.shape[0]), g...  7.75 us
    pallas_call x2, Pallas kernels, products(): pl.pallas_call(partial(kernel, pieces, offset), out_shape=types, in_specs...  3.61 us
    ppermute x2, waiting for transfers between devices, shards(): lax.ppermute(first_blocks[chunk], 'ctx', [(i, i - QUAD) for i in range(QU...  2.87 us
    pallas_call x2, Pallas kernels, shards(): pl.pallas_call(partial(final_kernel, chunk, pieces, offset, 1.0 / math.sq...  2.69 us
    ppermute x2, starting transfers between devices, shards(): lax.ppermute(first_blocks[chunk], 'ctx', [(i, i - QUAD) for i in range(QU...  2.57 us
  transfers between devices with their start and end apart: 21, of which 7 were waited for; matrix products, arithmetic and copies ran while one was open for 0% of the time, Pallas kernels for 18%

profile of v2, /device:TPU:0, one launch (start us, length us, event | category | flops | bytes accessed | tf_op | source)
XLA Modules:
  0.0 59.0 jit_solution(15750501345844311028)
XLA Ops:
  0.7 2.8 %gated_grad.1 = (bf16[128,1024]{1,0:T(8,128)(2,1)}, bf16[128,1024]{1,0:T(8,128)(2,1)}, bf16[128,1024]{1,0:T(8,128)(2,1)}, bf16[128,1024]{1,0:T(8,128)(2,1)}) custom-call(s32[1]{0:T(128)} %bitcast.pos_ref, bf16[128,4096]{1,0:T(8,128)(2,1)} %left_hbm.2, bf16[128,4096]{1,0:T(8,128)(2,1)} %right_hbm.2), custom_call_target="tpu_custom_call" | custom-call | tf_op jit(solution)/shard_map/gated_grad/pallas_call | solution.py:308
  3.5 0.0 copy-start.3
  3.5 0.5 collective-permute-start
  4.0 2.6 %collective-permute-start.1 = (bf16[128,1024]{1,0:T(8,128)(2,1)}, bf16[128,1024]{1,0:T(8,128)(2,1)S(1)}, u32[]{:S(2)}, u32[]{:S(2)}) collective-permute-start(bf16[128,1024]{1,0:T(8,128)(2,1)} %get-tuple-element.37), channel_id=1, source_target_pairs={{0,2},{1,3},{2,0},{3,1},{4,6},{5,7},{6,4},{7,5},{8,10},{9,11},{10,... | collective-permute-start | bytes 786440 | tf_op jit(solution)/shard_map/ppermute | solution.py:283
  6.6 0.1 collective-permute-start.2
  6.7 0.8 %conv_input.1 = (bf16[128,1024]{1,0:T(8,128)(2,1)S(1)}, bf16[128,1024]{1,0:T(8,128)(2,1)S(1)}, bf16[256,512]{1,0:T(8,128)(2,1)S(1)}, bf16[256,512]{1,0:T(8,128)(2,1)S(1)}) custom-call(s32[1]{0:T(128)} %bitcast.pos_ref, bf16[128,4096]{1,0:T(8,128)(2,1)S(1)} %copy-done, bf16[128,4096]{1,0:T(8,128)(2,1)S(1)} %copy-done.1), custom_call_target="tpu_custom_call" | custom-call | tf_op jit(solution)/shard_map/conv_input/pallas_call | solution.py:308
  7.5 1.8 %collective-permute-start.8 = (bf16[256,512]{1,0:T(8,128)(2,1)S(1)}, bf16[256,512]{1,0:T(8,128)(2,1)S(1)}, u32[]{:S(2)}, u32[]{:S(2)}) collective-permute-start(bf16[256,512]{1,0:T(8,128)(2,1)S(1)} %get-tuple-element.44), channel_id=1, source_target_pairs={{0,2},{1,3},{2,0},{3,1},{4,6},{5,7},{6,4},{7,5},{8,10},{9,11},{10,... | collective-permute-start | bytes 786440 | tf_op jit(solution)/shard_map/ppermute | solution.py:283
  9.3 2.6 %collective-permute-start.4 = (bf16[256,256]{1,0:T(8,128)(2,1)S(1)}, bf16[256,256]{1,0:T(8,128)(2,1)S(1)}, u32[]{:S(2)}, u32[]{:S(2)}) collective-permute-start(bf16[256,256]{1,0:T(8,128)(2,1)S(1)} %copy-done.5), channel_id=1, source_target_pairs={{0,8},{1,9},{2,10},{3,11},{4,12},{5,13},{6,14},{7,15},{8,0},{9,1},... | collective-permute-start | bytes 393224 | tf_op jit(solution)/shard_map/ppermute | solution.py:283
  11.9 6.6 %collective-permute-done.4 = bf16[256,256]{1,0:T(8,128)(2,1)S(1)} collective-permute-done((bf16[256,256]{1,0:T(8,128)(2,1)S(1)}, bf16[256,256]{1,0:T(8,128)(2,1)S(1)}, u32[]{:S(2)}, u32[]{:S(2)}) %collective-permute-start.4) | collective-permute-done | bytes 131104 | tf_op jit(solution)/shard_map/ppermute | solution.py:283
  18.5 0.7 %collective-permute-start.5 = (bf16[512,256]{1,0:T(8,128)(2,1)S(1)}, bf16[512,256]{1,0:T(8,128)(2,1)S(1)}, u32[]{:S(2)}, u32[]{:S(2)}) collective-permute-start(bf16[512,256]{1,0:T(8,128)(2,1)S(1)} %constant_dynamic-update-slice_fusion.refs_0_), channel_id=1, source_target_pairs={{0,4},{1,5},{2,6},{3,7},{4,0},{5,1},{6,2},{7,3},{8,12},{9,13},{10,... | collective-permute-start | bytes 786440 | tf_op jit(solution)/shard_map/ppermute | solution.py:283
  19.2 0.0 collective-permute-done.refs_1_
  19.2 0.0 collective-permute-done.1.refs_2_
  19.2 0.0 collective-permute-done.2.refs_3_
  19.2 0.1 halo.1
  19.3 1.3 %collective-permute-start.7 = (bf16[256,512]{1,0:T(8,128)(2,1)S(1)}, bf16[256,512]{1,0:T(8,128)(2,1)S(1)}, u32[]{:S(2)}, u32[]{:S(2)}) collective-permute-start(bf16[256,512]{1,0:T(8,128)(2,1)S(1)} %get-tuple-element.43._), channel_id=1, source_target_pairs={{4,0},{5,1},{6,2},{7,3},{8,4},{9,5},{10,6},{11,7},{12,8},{13,9},{1... | collective-permute-start | bytes 786440 | tf_op jit(solution)/shard_map/ppermute | solution.py:346
  20.6 4.4 %collective-permute-done.8.came_ref.refs_5_ = bf16[256,512]{1,0:T(8,128)(2,1)S(1)} collective-permute-done((bf16[256,512]{1,0:T(8,128)(2,1)S(1)}, bf16[256,512]{1,0:T(8,128)(2,1)S(1)}, u32[]{:S(2)}, u32[]{:S(2)}) %collective-permute-start.8) | collective-permute-done | bytes 262176 | tf_op jit(solution)/shard_map/ppermute | solution.py:283
  25.0 0.1 collective-permute-start.9
  25.1 1.8 %collective-permute-start.6 = (bf16[256,512]{1,0:T(8,128)(2,1)S(1)}, bf16[256,512]{1,0:T(8,128)(2,1)S(1)}, u32[]{:S(2)}, u32[]{:S(2)}) collective-permute-start(bf16[256,512]{1,0:T(8,128)(2,1)S(1)} %get-tuple-element.41), channel_id=1, source_target_pairs={{0,2},{1,3},{2,0},{3,1},{4,6},{5,7},{6,4},{7,5},{8,10},{9,11},{10,... | collective-permute-start | bytes 786440 | tf_op jit(solution)/shard_map/ppermute | solution.py:283
  26.9 1.3 %collective-permute-start.3 = (bf16[256,512]{1,0:T(8,128)(2,1)S(1)}, bf16[256,512]{1,0:T(8,128)(2,1)S(1)}, u32[]{:S(2)}, u32[]{:S(2)}) collective-permute-start(bf16[256,512]{1,0:T(8,128)(2,1)S(1)} %get-tuple-element.39), channel_id=1, source_target_pairs={{4,0},{5,1},{6,2},{7,3},{8,4},{9,5},{10,6},{11,7},{12,8},{13,9},{1... | collective-permute-start | bytes 786440 | tf_op jit(solution)/shard_map/ppermute | solution.py:346
  28.2 0.0 collective-permute-done.5.refs_1_
  28.2 0.5 filter_spectra.1.filter_ref
  28.7 2.9 %collective-permute-done.7.halo_ref = bf16[256,512]{1,0:T(8,128)(2,1)S(1)} collective-permute-done((bf16[256,512]{1,0:T(8,128)(2,1)S(1)}, bf16[256,512]{1,0:T(8,128)(2,1)S(1)}, u32[]{:S(2)}, u32[]{:S(2)}) %collective-permute-start.7) | collective-permute-done | bytes 262176 | tf_op jit(solution)/shard_map/ppermute | solution.py:346
  31.6 0.0 collective-permute-done.9.refs_6_
  31.6 3.9 %conv_0.1 = (bf16[128,512]{1,0:T(8,128)(2,1)S(1)}, bf16[128,512]{1,0:T(8,128)(2,1)S(1)}, bf16[128,512]{1,0:T(8,128)(2,1)S(1)}, bf16[128,512]{1,0:T(8,128)(2,1)S(...) custom-call(s32[1]{0:T(128)} %bitcast.pos_ref, s32[4]{0:T(128)S(1)} %copy-done.4, ...), custom_call_target="tpu_custom_call" | custom-call | tf_op jit(solution)/shard_map/conv_0/pallas_call | solution.py:358
  35.5 0.0 collective-permute-done.6.came_ref.refs_5_
  35.5 0.1 collective-permute-start.10
  35.6 0.2 collective-permute-start.13
  35.8 1.5 %collective-permute-start.11 = (bf16[128,512]{1,0:T(8,128)(2,1)S(1)}, bf16[128,512]{1,0:T(8,128)(2,1)S(1)}, u32[]{:S(2)}, u32[]{:S(2)}) collective-permute-start(bf16[128,512]{1,0:T(8,128)(2,1)S(1)} %get-tuple-element.51), channel_id=1, source_target_pairs={{0,2},{1,3},{2,0},{3,1},{4,6},{5,7},{6,4},{7,5},{8,10},{9,11},{10,... | collective-permute-start | bytes 393224 | tf_op jit(solution)/shard_map/ppermute | solution.py:283
  37.3 0.1 collective-permute-start.12
  37.4 4.1 %collective-permute-done.13.refs_6_.came_ref = bf16[256,256]{1,0:T(8,128)(2,1)S(1)} collective-permute-done((bf16[256,256]{1,0:T(8,128)(2,1)S(1)}, bf16[256,256]{1,0:T(8,128)(2,1)S(1)}, u32[]{:S(2)}, u32[]{:S(2)}) %collective-permute-start.13) | collective-permute-done | bytes 131104 | tf_op jit(solution)/shard_map/ppermute | solution.py:283
  41.5 0.0 collective-permute-done.3.halo_ref
  41.6 0.0 collective-permute-done.10.refs_6_
  41.6 3.9 %conv_1.1 = (bf16[128,512]{1,0:T(8,128)(2,1)S(1)}, bf16[128,512]{1,0:T(8,128)(2,1)S(1)}, bf16[128,512]{1,0:T(8,128)(2,1)S(1)}, bf16[128,512]{1,0:T(8,128)(2,1)S(...) custom-call(s32[1]{0:T(128)} %bitcast.pos_ref, s32[4]{0:T(128)S(1)} %copy-done.4, ...), custom_call_target="tpu_custom_call" | custom-call | tf_op jit(solution)/shard_map/conv_1/pallas_call | solution.py:358
  45.5 0.0 collective-permute-done.11.refs_4_.refs_2_
  45.5 0.3 collective-permute-start.18
  45.8 3.6 %collective-permute-start.17 = (bf16[128,256]{1,0:T(8,128)(2,1)S(1)}, bf16[128,256]{1,0:T(8,128)(2,1)S(1)}, u32[]{:S(2)}, u32[]{:S(2)}) collective-permute-start(bf16[128,256]{1,0:T(8,128)(2,1)S(1)} %get-tuple-element.58), channel_id=1, source_target_pairs={{0,8},{1,9},{2,10},{3,11},{4,12},{5,13},{6,14},{7,15},{8,0},{9,1},... | collective-permute-start | bytes 196616 | tf_op jit(solution)/shard_map/ppermute | solution.py:283
  49.4 0.0 collective-permute-start.20
  49.4 0.5 collective-permute-start.14
  50.0 0.5 collective-permute-start.15
  50.4 1.3 %collective-permute-done.17.refs_0_.refs_5_ = bf16[128,256]{1,0:T(8,128)(2,1)S(1)} collective-permute-done((bf16[128,256]{1,0:T(8,128)(2,1)S(1)}, bf16[128,256]{1,0:T(8,128)(2,1)S(1)}, u32[]{:S(2)}, u32[]{:S(2)}) %collective-permute-start.17) | collective-permute-done | bytes 65568 | tf_op jit(solution)/shard_map/ppermute | solution.py:283
  51.7 0.0 collective-permute-start.16
  51.7 0.3 collective-permute-done.18.came_ref
  52.0 3.0 %collective-permute-start.19 = (bf16[128,256]{1,0:T(8,128)(2,1)S(1)}, bf16[128,256]{1,0:T(8,128)(2,1)S(1)}, u32[]{:S(2)}, u32[]{:S(2)}) collective-permute-start(bf16[128,256]{1,0:T(8,128)(2,1)S(1)} %get-tuple-element.62), channel_id=1, source_target_pairs={{0,8},{1,9},{2,10},{3,11},{4,12},{5,13},{6,14},{7,15},{8,0},{9,1},... | collective-permute-start | bytes 196616 | tf_op jit(solution)/shard_map/ppermute | solution.py:283
  55.0 0.0 collective-permute-done.20.refs_1_
  55.0 1.3 %gate_products_0.1 = (bf16[128,4096]{1,0:T(8,128)(2,1)}, bf16[128,4096]{1,0:T(8,128)(2,1)}) custom-call(s32[1]{0:T(128)} %bitcast.pos_ref, bf16[128,4096]{1,0:T(8,128)(2,1)S(1)} %copy-done, bf16[128,4096]{1,0:T(8,128)(2,1)S(1)} %copy-done.1, bf16[128,512]{1,0:T(8,128)(2,1)S(1)} %get-tuple-element.63.refs_0_, ...), custom_call_target="tpu_custom_call" | custom-call | tf_op jit(solution)/shard_map/gate_products_0/pallas_call | solution.py:401
  56.3 1.2 %collective-permute-done.16.refs_3_ = bf16[128,512]{1,0:T(8,128)(2,1)S(1)} collective-permute-done((bf16[128,512]{1,0:T(8,128)(2,1)S(1)}, bf16[128,512]{1,0:T(8,128)(2,1)S(1)}, u32[]{:S(2)}, u32[]{:S(2)}) %collective-permute-start.16) | collective-permute-done | bytes 131104 | tf_op jit(solution)/shard_map/ppermute | solution.py:283
  57.6 0.0 collective-permute-done.19.refs_7_
  57.6 1.4 %gate_products_1.1 = (bf16[128,4096]{1,0:T(8,128)(2,1)}, bf16[128,4096]{1,0:T(8,128)(2,1)}, f32[256,256]{1,0:T(8,128)}) custom-call(s32[1]{0:T(128)} %bitcast.pos_ref, bf16[128,4096]{1,0:T(8,128)(2,1)S(1)} %copy-done, bf16[128,4096]{1,0:T(8,128)(2,1)S(1)} %copy-done.1, ...), custom_call_target="tpu_custom_call", output_to_operand_aliasing={{0}: (11, {}), {1}: (12, {})} | custom-call | tf_op jit(solution)/shard_map/gate_products_1/pallas_call | solution.py:401
  (21 shorter events, 0.1 us)
Async XLA Ops:
  0.6 6.1 %copy-start.1 = (bf16[128,4096]{1,0:T(8,128)(2,1)S(1)}, bf16[128,4096]{1,0:T(8,128)(2,1)}, u32[]{:S(2)}) copy-start(bf16[128,4096]{1,0:T(8,128)(2,1)} %value_ref.3) | copy-start | bytes 3145732
  0.6 6.1 %copy-start = (bf16[128,4096]{1,0:T(8,128)(2,1)S(1)}, bf16[128,4096]{1,0:T(8,128)(2,1)}, u32[]{:S(2)}) copy-start(bf16[128,4096]{1,0:T(8,128)(2,1)} %key_ref.3) | copy-start | bytes 3145732
  0.7 8.6 %copy-start.5 = (bf16[256,256]{1,0:T(8,128)(2,1)S(1)}, bf16[256,256]{1,0:T(8,128)(2,1)}, u32[]{:S(2)}) copy-start(bf16[256,256]{1,0:T(8,128)(2,1)} %param.11) | copy-start | bytes 393220
  3.5 15.7 %copy-start.3 = (bf16[128,1024]{1,0:T(8,128)(2,1)S(1)}, bf16[128,1024]{1,0:T(8,128)(2,1)}, u32[]{:S(2)}) copy-start(bf16[128,1024]{1,0:T(8,128)(2,1)} %get-tuple-element.35.refs_0_) | copy-start | bytes 786436
  3.5 15.7 %collective-permute-start = (bf16[128,1024]{1,0:T(8,128)(2,1)}, bf16[128,1024]{1,0:T(8,128)(2,1)S(1)}, u32[]{:S(2)}, u32[]{:S(2)}) collective-permute-start(bf16[128,1024]{1,0:T(8,128)(2,1)} %get-tuple-element.36), channel_id=1, source_target_pairs={{0,1},{1,0},{2,3},{3,2},{4,5},{5,4},{6,7},{7,6},{8,9},{9,8},{10,11... | collective-permute-start | bytes 786440 | tf_op jit(solution)/shard_map/ppermute | solution.py:283
  4.0 15.2 %collective-permute-start.1 = (bf16[128,1024]{1,0:T(8,128)(2,1)}, bf16[128,1024]{1,0:T(8,128)(2,1)S(1)}, u32[]{:S(2)}, u32[]{:S(2)}) collective-permute-start(bf16[128,1024]{1,0:T(8,128)(2,1)} %get-tuple-element.37), channel_id=1, source_target_pairs={{0,2},{1,3},{2,0},{3,1},{4,6},{5,7},{6,4},{7,5},{8,10},{9,11},{10,... | collective-permute-start | bytes 786440 | tf_op jit(solution)/shard_map/ppermute | solution.py:283
  6.6 21.6 %copy-start.2 = (bf16[1024,256]{1,0:T(8,128)(2,1)S(1)}, bf16[1024,256]{1,0:T(8,128)(2,1)}, u32[]{:S(2)}) copy-start(bf16[1024,256]{1,0:T(8,128)(2,1)} %constant.6.clone.table_ref) | copy-start | bytes 1572868
  6.6 12.6 %collective-permute-start.2 = (bf16[128,1024]{1,0:T(8,128)(2,1)}, bf16[128,1024]{1,0:T(8,128)(2,1)S(1)}, u32[]{:S(2)}, u32[]{:S(2)}) collective-permute-start(bf16[128,1024]{1,0:T(8,128)(2,1)} %get-tuple-element.38), channel_id=1, source_target_pairs={{0,3},{1,2},{2,1},{3,0},{4,7},{5,6},{6,5},{7,4},{8,11},{9,10},{10,... | collective-permute-start | bytes 786440 | tf_op jit(solution)/shard_map/ppermute | solution.py:283
  7.5 17.5 %collective-permute-start.8 = (bf16[256,512]{1,0:T(8,128)(2,1)S(1)}, bf16[256,512]{1,0:T(8,128)(2,1)S(1)}, u32[]{:S(2)}, u32[]{:S(2)}) collective-permute-start(bf16[256,512]{1,0:T(8,128)(2,1)S(1)} %get-tuple-element.44), channel_id=1, source_target_pairs={{0,2},{1,3},{2,0},{3,1},{4,6},{5,7},{6,4},{7,5},{8,10},{9,11},{10,... | collective-permute-start | bytes 786440 | tf_op jit(solution)/shard_map/ppermute | solution.py:283
  9.3 9.2 %collective-permute-start.4 = (bf16[256,256]{1,0:T(8,128)(2,1)S(1)}, bf16[256,256]{1,0:T(8,128)(2,1)S(1)}, u32[]{:S(2)}, u32[]{:S(2)}) collective-permute-start(bf16[256,256]{1,0:T(8,128)(2,1)S(1)} %copy-done.5), channel_id=1, source_target_pairs={{0,8},{1,9},{2,10},{3,11},{4,12},{5,13},{6,14},{7,15},{8,0},{9,1},... | collective-permute-start | bytes 393224 | tf_op jit(solution)/shard_map/ppermute | solution.py:283
  18.5 9.7 %collective-permute-start.5 = (bf16[512,256]{1,0:T(8,128)(2,1)S(1)}, bf16[512,256]{1,0:T(8,128)(2,1)S(1)}, u32[]{:S(2)}, u32[]{:S(2)}) collective-permute-start(bf16[512,256]{1,0:T(8,128)(2,1)S(1)} %constant_dynamic-update-slice_fusion.refs_0_), channel_id=1, source_target_pairs={{0,4},{1,5},{2,6},{3,7},{4,0},{5,1},{6,2},{7,3},{8,12},{9,13},{10,... | collective-permute-start | bytes 786440 | tf_op jit(solution)/shard_map/ppermute | solution.py:283
  19.3 12.3 %collective-permute-start.7 = (bf16[256,512]{1,0:T(8,128)(2,1)S(1)}, bf16[256,512]{1,0:T(8,128)(2,1)S(1)}, u32[]{:S(2)}, u32[]{:S(2)}) collective-permute-start(bf16[256,512]{1,0:T(8,128)(2,1)S(1)} %get-tuple-element.43._), channel_id=1, source_target_pairs={{4,0},{5,1},{6,2},{7,3},{8,4},{9,5},{10,6},{11,7},{12,8},{13,9},{1... | collective-permute-start | bytes 786440 | tf_op jit(solution)/shard_map/ppermute | solution.py:346
  25.0 6.6 %copy-start.4 = (s32[4]{0:T(128)S(1)}, s32[4]{0:T(128)}, u32[]{:S(2)}) copy-start(s32[4]{0:T(128)} %docs_ref.3) | copy-start | bytes 52
  25.0 6.6 %collective-permute-start.9 = (bf16[256,512]{1,0:T(8,128)(2,1)S(1)}, bf16[256,512]{1,0:T(8,128)(2,1)S(1)}, u32[]{:S(2)}, u32[]{:S(2)}) collective-permute-start(bf16[256,512]{1,0:T(8,128)(2,1)S(1)} %pack_0.1), channel_id=1, source_target_pairs={{0,1},{1,0},{2,3},{3,2},{4,5},{5,4},{6,7},{7,6},{8,9},{9,8},{10,11... | collective-permute-start | bytes 786440 | tf_op jit(solution)/shard_map/ppermute | solution.py:283
  25.1 10.4 %collective-permute-start.6 = (bf16[256,512]{1,0:T(8,128)(2,1)S(1)}, bf16[256,512]{1,0:T(8,128)(2,1)S(1)}, u32[]{:S(2)}, u32[]{:S(2)}) collective-permute-start(bf16[256,512]{1,0:T(8,128)(2,1)S(1)} %get-tuple-element.41), channel_id=1, source_target_pairs={{0,2},{1,3},{2,0},{3,1},{4,6},{5,7},{6,4},{7,5},{8,10},{9,11},{10,... | collective-permute-start | bytes 786440 | tf_op jit(solution)/shard_map/ppermute | solution.py:283
  26.9 14.6 %collective-permute-start.3 = (bf16[256,512]{1,0:T(8,128)(2,1)S(1)}, bf16[256,512]{1,0:T(8,128)(2,1)S(1)}, u32[]{:S(2)}, u32[]{:S(2)}) collective-permute-start(bf16[256,512]{1,0:T(8,128)(2,1)S(1)} %get-tuple-element.39), channel_id=1, source_target_pairs={{4,0},{5,1},{6,2},{7,3},{8,4},{9,5},{10,6},{11,7},{12,8},{13,9},{1... | collective-permute-start | bytes 786440 | tf_op jit(solution)/shard_map/ppermute | solution.py:346
  35.5 6.0 %collective-permute-start.10 = (bf16[256,512]{1,0:T(8,128)(2,1)S(1)}, bf16[256,512]{1,0:T(8,128)(2,1)S(1)}, u32[]{:S(2)}, u32[]{:S(2)}) collective-permute-start(bf16[256,512]{1,0:T(8,128)(2,1)S(1)} %pack_1.1), channel_id=1, source_target_pairs={{0,1},{1,0},{2,3},{3,2},{4,5},{5,4},{6,7},{7,6},{8,9},{9,8},{10,11... | collective-permute-start | bytes 786440 | tf_op jit(solution)/shard_map/ppermute | solution.py:283
  35.6 5.9 %collective-permute-start.13 = (bf16[256,256]{1,0:T(8,128)(2,1)S(1)}, bf16[256,256]{1,0:T(8,128)(2,1)S(1)}, u32[]{:S(2)}, u32[]{:S(2)}) collective-permute-start(bf16[256,256]{1,0:T(8,128)(2,1)S(1)} %get-tuple-element.53), channel_id=1, source_target_pairs={{0,4},{1,5},{2,6},{3,7},{4,0},{5,1},{6,2},{7,3},{8,12},{9,13},{10,... | collective-permute-start | bytes 393224 | tf_op jit(solution)/shard_map/ppermute | solution.py:283
  35.8 9.7 %collective-permute-start.11 = (bf16[128,512]{1,0:T(8,128)(2,1)S(1)}, bf16[128,512]{1,0:T(8,128)(2,1)S(1)}, u32[]{:S(2)}, u32[]{:S(2)}) collective-permute-start(bf16[128,512]{1,0:T(8,128)(2,1)S(1)} %get-tuple-element.51), channel_id=1, source_target_pairs={{0,2},{1,3},{2,0},{3,1},{4,6},{5,7},{6,4},{7,5},{8,10},{9,11},{10,... | collective-permute-start | bytes 393224 | tf_op jit(solution)/shard_map/ppermute | solution.py:283
  37.3 8.2 %collective-permute-start.12 = (bf16[128,512]{1,0:T(8,128)(2,1)S(1)}, bf16[128,512]{1,0:T(8,128)(2,1)S(1)}, u32[]{:S(2)}, u32[]{:S(2)}) collective-permute-start(bf16[128,512]{1,0:T(8,128)(2,1)S(1)} %get-tuple-element.52), channel_id=1, source_target_pairs={{0,3},{1,2},{2,1},{3,0},{4,7},{5,6},{6,5},{7,4},{8,11},{9,10},{10,... | collective-permute-start | bytes 393224 | tf_op jit(solution)/shard_map/ppermute | solution.py:283
  45.5 6.5 %collective-permute-start.18 = (bf16[256,256]{1,0:T(8,128)(2,1)S(1)}, bf16[256,256]{1,0:T(8,128)(2,1)S(1)}, u32[]{:S(2)}, u32[]{:S(2)}) collective-permute-start(bf16[256,256]{1,0:T(8,128)(2,1)S(1)} %get-tuple-element.60), channel_id=1, source_target_pairs={{0,4},{1,5},{2,6},{3,7},{4,0},{5,1},{6,2},{7,3},{8,12},{9,13},{10,... | collective-permute-start | bytes 393224 | tf_op jit(solution)/shard_map/ppermute | solution.py:283
  45.8 5.9 %collective-permute-start.17 = (bf16[128,256]{1,0:T(8,128)(2,1)S(1)}, bf16[128,256]{1,0:T(8,128)(2,1)S(1)}, u32[]{:S(2)}, u32[]{:S(2)}) collective-permute-start(bf16[128,256]{1,0:T(8,128)(2,1)S(1)} %get-tuple-element.58), channel_id=1, source_target_pairs={{0,8},{1,9},{2,10},{3,11},{4,12},{5,13},{6,14},{7,15},{8,0},{9,1},... | collective-permute-start | bytes 196616 | tf_op jit(solution)/shard_map/ppermute | solution.py:283
  49.4 5.6 %collective-permute-start.20 = (bf16[128,512]{1,0:T(8,128)(2,1)S(1)}, bf16[128,512]{1,0:T(8,128)(2,1)S(1)}, u32[]{:S(2)}, u32[]{:S(2)}) collective-permute-start(bf16[128,512]{1,0:T(8,128)(2,1)S(1)} %get-tuple-element.64), channel_id=1, source_target_pairs={{0,1},{1,0},{2,3},{3,2},{4,5},{5,4},{6,7},{7,6},{8,9},{9,8},{10,11... | collective-permute-start | bytes 393224 | tf_op jit(solution)/shard_map/ppermute | solution.py:283
  49.4 6.9 %collective-permute-start.14 = (bf16[128,512]{1,0:T(8,128)(2,1)S(1)}, bf16[128,512]{1,0:T(8,128)(2,1)S(1)}, u32[]{:S(2)}, u32[]{:S(2)}) collective-permute-start(bf16[128,512]{1,0:T(8,128)(2,1)S(1)} %get-tuple-element.54), channel_id=1, source_target_pairs={{0,1},{1,0},{2,3},{3,2},{4,5},{5,4},{6,7},{7,6},{8,9},{9,8},{10,11... | collective-permute-start | bytes 393224 | tf_op jit(solution)/shard_map/ppermute | solution.py:283
  50.0 6.4 %collective-permute-start.15 = (bf16[128,512]{1,0:T(8,128)(2,1)S(1)}, bf16[128,512]{1,0:T(8,128)(2,1)S(1)}, u32[]{:S(2)}, u32[]{:S(2)}) collective-permute-start(bf16[128,512]{1,0:T(8,128)(2,1)S(1)} %get-tuple-element.55), channel_id=1, source_target_pairs={{0,2},{1,3},{2,0},{3,1},{4,6},{5,7},{6,4},{7,5},{8,10},{9,11},{10,... | collective-permute-start | bytes 393224 | tf_op jit(solution)/shard_map/ppermute | solution.py:283
  51.7 5.8 %collective-permute-start.16 = (bf16[128,512]{1,0:T(8,128)(2,1)S(1)}, bf16[128,512]{1,0:T(8,128)(2,1)S(1)}, u32[]{:S(2)}, u32[]{:S(2)}) collective-permute-start(bf16[128,512]{1,0:T(8,128)(2,1)S(1)} %get-tuple-element.56), channel_id=1, source_target_pairs={{0,3},{1,2},{2,1},{3,0},{4,7},{5,6},{6,5},{7,4},{8,11},{9,10},{10,... | collective-permute-start | bytes 393224 | tf_op jit(solution)/shard_map/ppermute | solution.py:283
  52.0 5.5 %collective-permute-start.19 = (bf16[128,256]{1,0:T(8,128)(2,1)S(1)}, bf16[128,256]{1,0:T(8,128)(2,1)S(1)}, u32[]{:S(2)}, u32[]{:S(2)}) collective-permute-start(bf16[128,256]{1,0:T(8,128)(2,1)S(1)} %get-tuple-element.62), channel_id=1, source_target_pairs={{0,8},{1,9},{2,10},{3,11},{4,12},{5,13},{6,14},{7,15},{8,0},{9,1},... | collective-permute-start | bytes 196616 | tf_op jit(solution)/shard_map/ppermute | solution.py:283

commit v3 on v2

--- a/solution.py
+++ b/solution.py
@@ -69,10 +69,8 @@
 def invert(back, real, imag):
     rows = real.shape[0]
     spectrum = jnp.concatenate([real, imag], axis=0)
-    high = spectrum.astype(BF16)
-    low = (spectrum - high.astype(F32)).astype(BF16)
-    both = dot(back, high)
-    return both[:rows] + both[rows:] + dot(back[:rows], low)
+    both = dot(back, spectrum.astype(BF16))
+    return both[:rows] + both[rows:]
 
 
 def cut_products(pieces, offset, sources, held, sems, outs):
@@ -114,9 +112,10 @@
     cut_products(pieces, offset, (left_hbm, right_hbm), (left_ref, right_ref), sems, outs)
 
 
-def pack_kernel(near_ref, came_ref, _, out):
-    rows = near_ref.shape[0]
-    out[:rows, :] = near_ref[...]
+def pack_kernel(chunk, near_ref, came_ref, *refs):
+    out = refs[-1]
+    rows, width = near_ref.shape[0], out.shape[1]
+    out[:rows, :] = near_ref[:, chunk * width : (chunk + 1) * width]
     out[rows:, :] = came_ref[rows:, :]
 
 
@@ -158,61 +157,86 @@
                     out[block * rows : (block + 1) * rows, :] = held[k][:rows, chunk * width : (chunk + 1) * width]
 
 
-def conv_kernel(chunk, quads, docs, pos_ref, docs_ref, table_ref, halo_ref, filter_ref, *refs):
-    grads, (own_ref, far_ref, came_ref) = refs[:QUAD], refs[QUAD : QUAD + 3]
-    outs, terms = refs[-6 - QUAD : -6], refs[-6:-4]
-    grad_all, input_all, out_all, terms_all = refs[-4:]
-    rows, width = grads[0].shape
-    length = 2 * rows
-    piece = width // quads
-    place, quad = pos_ref[0] % QUAD, pos_ref[0] // QUAD
+def joined_blocks(pos_ref, docs_ref, docs):
     joined = []
     for j in range(QUAD + 1):
         same, end = jnp.int32(1), jnp.int32(0)
         for d in range(docs):
             end = end + docs_ref[d]
-            same = jnp.where(end == quad * QUAD + j + 1, 0, same)
+            same = jnp.where(end == pos_ref[0] // QUAD * QUAD + j + 1, 0, same)
         joined.append(same.astype(F32))
+    return joined
+
+
+def convolve(joined, table_ref, filters, grad_of, input_of, put):
+    length = table_ref.shape[1]
+    half, back = table_ref[2 * length : 3 * length], table_ref[3 * length :]
+    windows = []
+    for j in range(QUAD + 1):
+        both = jnp.concatenate([grad_of(j), grad_of(j + 1) * joined[j].astype(BF16)], axis=0)
+        parts = dot(table_ref[: 2 * length], both)
+        windows.append(parts[:length] + parts[length:])
+    sums = None
+    for j in range(QUAD):
+        near, far = halves(windows[j]), halves(windows[j + 1] * joined[j])
+        real, imag = add(conj_product(near, filters[0]), conj_product(far, filters[1]))
+        put(j, invert(back, real, imag).astype(BF16))
+        held = input_of(j)
+        source = halves(dot(half, jnp.concatenate([held, held], axis=0)))
+        terms = [conj_product(near, source), conj_product(far, source)]
+        sums = [add(*pair) for pair in zip(sums, terms)] if sums else terms
+    return sums
+
+
+def tiles(width):
+    return [slice(first, min(first + TILE, width)) for first in range(0, width, TILE)]
+
+
+def conv_kernel(chunk, quads, docs, pos_ref, docs_ref, table_ref, filter_ref, halo_ref, *refs):
+    grads, (own_ref, far_ref, came_ref) = refs[:QUAD], refs[QUAD : QUAD + 3]
+    outs, terms = refs[-6 - QUAD : -6], refs[-6:-4]
+    grad_all, input_all, out_all, terms_all = refs[-4:]
+    rows, width = outs[0].shape
+    length = 2 * rows
+    piece = width // quads
+    place, quad = pos_ref[0] % QUAD, pos_ref[0] // QUAD
+    share = slice(chunk * width, (chunk + 1) * width)
+    joined = joined_blocks(pos_ref, docs_ref, docs)
     for k in range(QUAD):
         at = pl.ds(pl.multiple_of(lax.bitwise_xor(place, k) * rows, rows), rows)
-        grad_all[at, :] = grads[k][...]
-        held = (own_ref, came_ref, far_ref, came_ref)[k]
-        input_all[at, :] = held[(k // 3) * rows : (k // 3 + 1) * rows, :]
+        grad_all[at, :] = grads[k][:, share]
+        if k:
+            held = (far_ref if k == 2 else came_ref)[k // 3 * rows : (k // 3 + 1) * rows, :]
+        else:
+            held = own_ref[:, share]
+        input_all[at, :] = held
     grad_all[QUAD * rows :, :] = halo_ref[...]
-    high, low = table_ref[:length], table_ref[length : 2 * length]
-    half, back = table_ref[2 * length : 3 * length], table_ref[3 * length :]
-    for first in range(0, width, TILE):
-        lanes = slice(first, min(first + TILE, width))
-        filters = [halves(filter_ref[n * length : (n + 1) * length, lanes]) for n in range(REACH)]
-        windows = []
-        for j in range(QUAD + 1):
-            ahead = grad_all[(j + 1) * rows : (j + 2) * rows, lanes].astype(F32) * joined[j]
-            window = jnp.concatenate([grad_all[j * rows : (j + 1) * rows, lanes], ahead.astype(BF16)], axis=0)
-            windows.append(dot(high, window) + dot(low, window))
-        sums = [None] * REACH
-        for j in range(QUAD):
-            held = input_all[j * rows : (j + 1) * rows, lanes]
-            source = halves(dot(half, jnp.concatenate([held, held], axis=0)))
-            near, far = halves(windows[j]), halves(windows[j + 1] * joined[j])
-            real, imag = add(conj_product(near, filters[0]), conj_product(far, filters[1]))
-            out_all[j * rows : (j + 1) * rows, lanes] = invert(back, real, imag).astype(BF16)
-            for segment, window in enumerate((near, far)):
-                term = conj_product(window, source)
-                sums[segment] = term if j == 0 else add(sums[segment], term)
+    for lanes in tiles(width):
+
+        def put(j, value, lanes=lanes):
+            out_all[j * rows : (j + 1) * rows, lanes] = value
+
+        of_chunk = slice(chunk * width + lanes.start, chunk * width + lanes.stop)
+        filters = [halves(filter_ref[n * length : (n + 1) * length, of_chunk]) for n in range(REACH)]
+        block = lambda ref, j, lanes=lanes: ref[j * rows : (j + 1) * rows, lanes]
+        sums = convolve(joined, table_ref, filters, partial(block, grad_all), partial(block, input_all), put)
         for segment in range(REACH):
-            lags = invert(back, *sums[segment])
+            lags = invert(table_ref[3 * length :], *sums[segment])
             terms_all[lanes, segment * rows : (segment + 1) * rows] = lags.T
     for k in range(QUAD):
         at = pl.ds(pl.multiple_of(lax.bitwise_xor(place, k) * rows, rows), rows)
-        outs[k][...] = out_all[at, :]
+        if k == 1 and chunk:
+            outs[k][:, : chunk * width] = refs[QUAD + 3][...]
+            outs[k][:, chunk * width :] = out_all[at, :]
+        else:
+            outs[k][...] = out_all[at, :]
     for n, s in enumerate(halving_order(quads)):
         at = pl.ds(pl.multiple_of(lax.bitwise_xor(quad, s) * piece, piece), piece)
         sent, n = divmod(n, quads // 2)
         terms[sent][n * piece : (n + 1) * piece, :] = terms_all[at, :].astype(terms[sent].dtype)
 
 
-def fold_kernel(kept_ref, came_ref, *refs):
-    keep_ref, send_ref = refs[-2:]
+def fold_kernel(kept_ref, came_ref, keep_ref, send_ref):
     half = keep_ref.shape[0]
     keep_ref[...] = kept_ref[:half, :] + came_ref[:half, :].astype(F32)
     send_ref[...] = (kept_ref[half:, :] + came_ref[half:, :].astype(F32)).astype(BF16)
@@ -238,7 +262,8 @@
             n = k * count + i
             lanes = pl.ds(pl.multiple_of(offset(chunk, i, member // 2, member % 2), 128), width)
             held = slice(n * width, (n + 1) * width)
-            grad = grads[k][:, i * width : (i + 1) * width]
+            first = ((chunk * count if k == 1 else 0) + i) * width
+            grad = grads[k][:, first : first + width]
             key_all[:, held] = grad * value_ref[:, lanes]
             value_all[:, held] = grad * key_ref[:, lanes]
             copies.append(pltpu.make_async_copy(key_all.at[:, held], key_out.at[:, lanes], sems.at[0, n]))
@@ -317,8 +342,8 @@
 
     own, near, same, other = products(grad_kernel, out_grad, query_gate, [both] * 4, 60, "gated_grad")
     grads = [own, to_member(near, 1), to_member(same, 2), to_member(other, 3)]
-    pair = jax.ShapeDtypeStruct((2 * rows, width), BF16)
-    own, near, *far_inputs = products(input_kernel, key_branch, value_branch, [both] * 2 + [pair] * CHUNKS, 40, "conv_input")
+    pair_type = jax.ShapeDtypeStruct((2 * rows, width), BF16)
+    own, near, *far_inputs = products(input_kernel, key_branch, value_branch, [both] * 2 + [pair_type] * CHUNKS, 40, "conv_input")
     own_input, near_input = own, near
     far_inputs = [to_member(value, 2) for value in far_inputs]
     spectra = pl.pallas_call(
@@ -338,33 +363,26 @@
         compiler_params=PARAMS,
         name="halo",
     )(pos, *grads)
-    before = first_blocks[0]
+    before = [first_blocks[0]]
     results, chunk_grads, chunk_terms = [], [], []
-    whole = lambda *shape: pl.BlockSpec(shape, lambda _: (0,) * len(shape))
     nearest = []
     for chunk in range(CHUNKS):
         halo = lax.ppermute(first_blocks[chunk], "ctx", [(i, i - QUAD) for i in range(QUAD, blocks)])
-        share = pl.BlockSpec((rows, width), lambda _, chunk=chunk: (0, chunk))
         forward = pl.pallas_call(
-            pack_kernel,
-            grid=(1,),
-            out_shape=jax.ShapeDtypeStruct((2 * rows, width), BF16),
-            in_specs=[share, whole(2 * rows, width), ANY],
-            out_specs=whole(2 * rows, width),
+            partial(pack_kernel, chunk),
+            out_shape=pair_type,
+            in_specs=[VMEM, VMEM] + [ANY] * len(before),
+            out_specs=VMEM,
             compiler_params=PARAMS,
             name=f"pack_{chunk}",
-        )(near_input, far_inputs[chunk], before)
+        )(near_input, far_inputs[chunk], *before)
         forward = to_member(forward, 1)
         done = pl.pallas_call(
             partial(conv_kernel, chunk, quads, doc_blocks.shape[0]),
-            grid=(1,),
-            out_shape=[alone] * QUAD
+            out_shape=[alone, jax.ShapeDtypeStruct((rows, (chunk + 1) * width), BF16), alone, alone]
             + [jax.ShapeDtypeStruct((width // 2, lags), kind) for kind in (F32, BF16)],
-            in_specs=[SMEM, SMEM, whole(*table.shape), whole(REACH * rows, width)]
-            + [pl.BlockSpec((REACH * lags, width), lambda _, chunk=chunk: (0, chunk))]
-            + [share] * (QUAD + 1)
-            + [whole(2 * rows, width)] * 2,
-            out_specs=[whole(rows, width)] * QUAD + [whole(width // 2, lags)] * 2,
+            in_specs=[SMEM, SMEM] + [VMEM] * (6 + QUAD + len(nearest)),
+            out_specs=[VMEM] * (QUAD + 2),
             scratch_shapes=[
                 pltpu.VMEM(((QUAD + REACH) * rows, width), BF16),
                 pltpu.VMEM((QUAD * rows, width), BF16),
@@ -373,16 +391,18 @@
             ],
             compiler_params=PARAMS,
             name=f"conv_{chunk}",
-        )(pos, doc_blocks, table, halo, spectra, *grads, own_input, far_inputs[chunk], forward)
-        own, *sent, kept, send = done
-        before = kept
+        )(pos, doc_blocks, table, spectra, halo, *grads, own_input, far_inputs[chunk], forward, *nearest)
+        own, pair, *sent, kept, send = done
+        before, nearest = [kept], [pair]
         if chunk:
-            *sent, send = gate([*sent, send], *chunk_grads[-1][2:], chunk_terms[-1][1])
-        chunk_grads.append([own, *[to_member(value, k + 1) for k, value in enumerate(sent)]])
+            *sent, pair, send = gate([*sent, pair, send], *chunk_grads[-1][2:], chunk_terms[-1][1])
+        chunk_grads.append([own, pair, *[to_member(value, 2 + k) for k, value in enumerate(sent)]])
         chunk_terms.append((kept, to_quad(send, 1)))
+    nearest = to_member(pair, 1)
     filter_grads = []
     for chunk in range(CHUNKS):
         gradients, (kept, came) = chunk_grads[chunk], chunk_terms[chunk]
+        gradients[1] = nearest
         step = 1
         while 2 * step < quads:
             step *= 2
@@ -390,11 +410,11 @@
             kept, send = pl.pallas_call(
                 fold_kernel,
                 out_shape=[jax.ShapeDtypeStruct((half, lags), kind) for kind in (F32, BF16)],
-                in_specs=[VMEM] * 2 + [ANY] * len(filter_grads[-1:]),
+                in_specs=[VMEM] * 2,
                 out_specs=[VMEM] * 2,
                 compiler_params=PARAMS,
                 name=f"fold_{chunk}_{step}",
-            )(kept, came, *filter_grads[-1:])
+            )(kept, came)
             came = to_quad(send, step)
         filter_grads += [kept, came]
         last = filter_grads if chunk == CHUNKS - 1 else []

time: 59.9 us -> 58.5 us (0.977); the launches traced: 59 us -> 58.3 us
  waiting for transfers between devices: 20.7 us -> 18.3 us
  starting transfers between devices: 22.6 us -> 24.7 us
    ppermute x19 -> x18, waiting for transfers between devices: 17.8 us -> 15.5 us  [to_member(): lax.ppermute(value, 'ctx', [(i, i ^ k) for i in range(blocks)])]
    ppermute x19 -> x18, starting transfers between devices: 20.1 us -> 22.1 us  [to_member(): lax.ppermute(value, 'ctx', [(i, i ^ k) for i in range(blocks)])]
  transfers between devices with their start and end apart: 21 -> 20, of which waited for: 7 -> 7; matrix products, arithmetic and copies ran while one was open for 0% -> 0% of each run, Pallas kernels for 18% -> 17%
where the time goes in v3:
time: 58.5 us; the launch traced here: 58.3 us
  starting transfers between devices  24.7 us (42%)
  waiting for transfers between devices  18.3 us (31%)
  Pallas kernels  14.5 us (25%)
  between operations  0.85 us (1%)
    ppermute x18, starting transfers between devices, to_member(): lax.ppermute(value, 'ctx', [(i, i ^ k) for i in range(blocks)])  22.1 us
    ppermute x18, waiting for transfers between devices, to_member(): lax.ppermute(value, 'ctx', [(i, i ^ k) for i in range(blocks)])  15.5 us
    pallas_call x2, Pallas kernels, shards(): pl.pallas_call(partial(conv_kernel, chunk, quads, doc_blocks.shape[0]), o...  7.45 us
    pallas_call x2, Pallas kernels, products(): pl.pallas_call(partial(kernel, pieces, offset), out_shape=types, in_specs...  3.61 us
    ppermute x2, waiting for transfers between devices, shards(): lax.ppermute(first_blocks[chunk], 'ctx', [(i, i - QUAD) for i in range(QU...  2.87 us
    pallas_call x2, Pallas kernels, shards(): pl.pallas_call(partial(final_kernel, chunk, pieces, offset, 1.0 / math.sq...  2.7 us
    ppermute x2, starting transfers between devices, shards(): lax.ppermute(first_blocks[chunk], 'ctx', [(i, i - QUAD) for i in range(QU...  2.57 us
  transfers between devices with their start and end apart: 20, of which 7 were waited for; matrix products, arithmetic and copies ran while one was open for 0% of the time, Pallas kernels for 17%

profile of v3, /device:TPU:0, one launch (start us, length us, event | category | flops | bytes accessed | tf_op | source)
XLA Modules:
  0.0 58.3 jit_solution(8533429289734590948)
XLA Ops:
  0.7 2.8 %gated_grad.1 = (bf16[128,1024]{1,0:T(8,128)(2,1)}, bf16[128,1024]{1,0:T(8,128)(2,1)}, bf16[128,1024]{1,0:T(8,128)(2,1)}, bf16[128,1024]{1,0:T(8,128)(2,1)}) custom-call(s32[1]{0:T(128)} %bitcast.pos_ref, bf16[128,4096]{1,0:T(8,128)(2,1)} %left_hbm.2, bf16[128,4096]{1,0:T(8,128)(2,1)} %right_hbm.2), custom_call_target="tpu_custom_call" | custom-call | tf_op jit(solution)/shard_map/gated_grad/pallas_call | solution.py:333
  3.5 0.0 copy-start.3
  3.5 0.5 collective-permute-start.2
  4.0 2.6 %collective-permute-start.3 = (bf16[128,1024]{1,0:T(8,128)(2,1)}, bf16[128,1024]{1,0:T(8,128)(2,1)S(1)}, u32[]{:S(2)}, u32[]{:S(2)}) collective-permute-start(bf16[128,1024]{1,0:T(8,128)(2,1)} %get-tuple-element.37), channel_id=1, source_target_pairs={{0,2},{1,3},{2,0},{3,1},{4,6},{5,7},{6,4},{7,5},{8,10},{9,11},{10,... | collective-permute-start | bytes 786440 | tf_op jit(solution)/shard_map/ppermute | solution.py:308
  6.6 0.1 collective-permute-start.4
  6.7 0.8 %conv_input.1 = (bf16[128,1024]{1,0:T(8,128)(2,1)S(1)}, bf16[128,1024]{1,0:T(8,128)(2,1)S(1)}, bf16[256,512]{1,0:T(8,128)(2,1)S(1)}, bf16[256,512]{1,0:T(8,128)(2,1)S(1)}) custom-call(s32[1]{0:T(128)} %bitcast.pos_ref, bf16[128,4096]{1,0:T(8,128)(2,1)S(1)} %copy-done, bf16[128,4096]{1,0:T(8,128)(2,1)S(1)} %copy-done.1), custom_call_target="tpu_custom_call" | custom-call | tf_op jit(solution)/shard_map/conv_input/pallas_call | solution.py:333
  7.5 1.8 %collective-permute-start.8 = (bf16[256,512]{1,0:T(8,128)(2,1)S(1)}, bf16[256,512]{1,0:T(8,128)(2,1)S(1)}, u32[]{:S(2)}, u32[]{:S(2)}) collective-permute-start(bf16[256,512]{1,0:T(8,128)(2,1)S(1)} %get-tuple-element.44), channel_id=1, source_target_pairs={{0,2},{1,3},{2,0},{3,1},{4,6},{5,7},{6,4},{7,5},{8,10},{9,11},{10,... | collective-permute-start | bytes 786440 | tf_op jit(solution)/shard_map/ppermute | solution.py:308
  9.3 2.6 %collective-permute-start = (bf16[256,256]{1,0:T(8,128)(2,1)S(1)}, bf16[256,256]{1,0:T(8,128)(2,1)S(1)}, u32[]{:S(2)}, u32[]{:S(2)}) collective-permute-start(bf16[256,256]{1,0:T(8,128)(2,1)S(1)} %copy-done.5), channel_id=1, source_target_pairs={{0,8},{1,9},{2,10},{3,11},{4,12},{5,13},{6,14},{7,15},{8,0},{9,1},... | collective-permute-start | bytes 393224 | tf_op jit(solution)/shard_map/ppermute | solution.py:308
  11.9 6.6 %collective-permute-done = bf16[256,256]{1,0:T(8,128)(2,1)S(1)} collective-permute-done((bf16[256,256]{1,0:T(8,128)(2,1)S(1)}, bf16[256,256]{1,0:T(8,128)(2,1)S(1)}, u32[]{:S(2)}, u32[]{:S(2)}) %collective-permute-start) | collective-permute-done | bytes 131104 | tf_op jit(solution)/shard_map/ppermute | solution.py:308
  18.5 0.7 %collective-permute-start.1 = (bf16[512,256]{1,0:T(8,128)(2,1)S(1)}, bf16[512,256]{1,0:T(8,128)(2,1)S(1)}, u32[]{:S(2)}, u32[]{:S(2)}) collective-permute-start(bf16[512,256]{1,0:T(8,128)(2,1)S(1)} %constant_dynamic-update-slice_fusion.refs_0_), channel_id=1, source_target_pairs={{0,4},{1,5},{2,6},{3,7},{4,0},{5,1},{6,2},{7,3},{8,12},{9,13},{10,... | collective-permute-start | bytes 786440 | tf_op jit(solution)/shard_map/ppermute | solution.py:308
  19.2 0.0 collective-permute-done.2.refs_1_
  19.2 0.0 collective-permute-done.3.refs_2_
  19.2 0.0 collective-permute-done.4.refs_3_
  19.2 0.1 halo.1
  19.3 1.3 %collective-permute-start.7 = (bf16[256,512]{1,0:T(8,128)(2,1)S(1)}, bf16[256,512]{1,0:T(8,128)(2,1)S(1)}, u32[]{:S(2)}, u32[]{:S(2)}) collective-permute-start(bf16[256,512]{1,0:T(8,128)(2,1)S(1)} %get-tuple-element.43.refs_0_), channel_id=1, source_target_pairs={{4,0},{5,1},{6,2},{7,3},{8,4},{9,5},{10,6},{11,7},{12,8},{13,9},{1... | collective-permute-start | bytes 786440 | tf_op jit(solution)/shard_map/ppermute | solution.py:370
  20.6 4.4 %collective-permute-done.8.came_ref.refs_5_ = bf16[256,512]{1,0:T(8,128)(2,1)S(1)} collective-permute-done((bf16[256,512]{1,0:T(8,128)(2,1)S(1)}, bf16[256,512]{1,0:T(8,128)(2,1)S(1)}, u32[]{:S(2)}, u32[]{:S(2)}) %collective-permute-start.8) | collective-permute-done | bytes 262176 | tf_op jit(solution)/shard_map/ppermute | solution.py:308
  25.0 0.1 collective-permute-start.9
  25.1 1.8 %collective-permute-start.6 = (bf16[256,512]{1,0:T(8,128)(2,1)S(1)}, bf16[256,512]{1,0:T(8,128)(2,1)S(1)}, u32[]{:S(2)}, u32[]{:S(2)}) collective-permute-start(bf16[256,512]{1,0:T(8,128)(2,1)S(1)} %get-tuple-element.41), channel_id=1, source_target_pairs={{0,2},{1,3},{2,0},{3,1},{4,6},{5,7},{6,4},{7,5},{8,10},{9,11},{10,... | collective-permute-start | bytes 786440 | tf_op jit(solution)/shard_map/ppermute | solution.py:308
  26.9 1.3 %collective-permute-start.5 = (bf16[256,512]{1,0:T(8,128)(2,1)S(1)}, bf16[256,512]{1,0:T(8,128)(2,1)S(1)}, u32[]{:S(2)}, u32[]{:S(2)}) collective-permute-start(bf16[256,512]{1,0:T(8,128)(2,1)S(1)} %get-tuple-element.39), channel_id=1, source_target_pairs={{4,0},{5,1},{6,2},{7,3},{8,4},{9,5},{10,6},{11,7},{12,8},{13,9},{1... | collective-permute-start | bytes 786440 | tf_op jit(solution)/shard_map/ppermute | solution.py:370
  28.2 0.0 collective-permute-done.1.refs_1_
  28.2 0.5 filter_spectra.1.filter_ref
  28.7 2.9 %collective-permute-done.7.halo_ref = bf16[256,512]{1,0:T(8,128)(2,1)S(1)} collective-permute-done((bf16[256,512]{1,0:T(8,128)(2,1)S(1)}, bf16[256,512]{1,0:T(8,128)(2,1)S(1)}, u32[]{:S(2)}, u32[]{:S(2)}) %collective-permute-start.7) | collective-permute-done | bytes 262176 | tf_op jit(solution)/shard_map/ppermute | solution.py:370
  31.6 0.0 collective-permute-done.9.refs_6_
  31.6 3.7 %conv_0.1 = (bf16[128,512]{1,0:T(8,128)(2,1)S(1)}, bf16[128,512]{1,0:T(8,128)(2,1)S(1)}, bf16[128,512]{1,0:T(8,128)(2,1)S(1)}, bf16[128,512]{1,0:T(8,128)(2,1)S(...) custom-call(s32[1]{0:T(128)} %bitcast.pos_ref, s32[4]{0:T(128)S(1)} %copy-done.4, ...), custom_call_target="tpu_custom_call" | custom-call | tf_op jit(solution)/shard_map/conv_0/pallas_call | solution.py:380
  35.3 0.0 collective-permute-done.6.came_ref.refs_5_
  35.4 0.1 collective-permute-start.10
  35.4 1.0 %collective-permute-start.11 = (bf16[128,512]{1,0:T(8,128)(2,1)S(1)}, bf16[128,512]{1,0:T(8,128)(2,1)S(1)}, u32[]{:S(2)}, u32[]{:S(2)}) collective-permute-start(bf16[128,512]{1,0:T(8,128)(2,1)S(1)} %get-tuple-element.52), channel_id=1, source_target_pairs={{0,2},{1,3},{2,0},{3,1},{4,6},{5,7},{6,4},{7,5},{8,10},{9,11},{10,... | collective-permute-start | bytes 393224 | tf_op jit(solution)/shard_map/ppermute | solution.py:308
  36.4 0.9 %collective-permute-start.12 = (bf16[128,512]{1,0:T(8,128)(2,1)S(1)}, bf16[128,512]{1,0:T(8,128)(2,1)S(1)}, u32[]{:S(2)}, u32[]{:S(2)}) collective-permute-start(bf16[128,512]{1,0:T(8,128)(2,1)S(1)} %get-tuple-element.53), channel_id=1, source_target_pairs={{0,3},{1,2},{2,1},{3,0},{4,7},{5,6},{6,5},{7,4},{8,11},{9,10},{10,... | collective-permute-start | bytes 393224 | tf_op jit(solution)/shard_map/ppermute | solution.py:308
  37.3 0.3 collective-permute-start.13
  37.6 0.0 collective-permute-done.5.halo_ref
  37.6 0.0 collective-permute-done.10.refs_6_
  37.6 3.7 %conv_1.1 = (bf16[128,512]{1,0:T(8,128)(2,1)S(1)}, bf16[128,1024]{1,0:T(8,128)(2,1)S(1)}, bf16[128,512]{1,0:T(8,128)(2,1)S(1)}, bf16[128,512]{1,0:T(8,128)(2,1)S...) custom-call(s32[1]{0:T(128)} %bitcast.pos_ref, s32[4]{0:T(128)S(1)} %copy-done.4, ...), custom_call_target="tpu_custom_call" | custom-call | tf_op jit(solution)/shard_map/conv_1/pallas_call | solution.py:380
  41.3 0.5 collective-permute-done.11.refs_4_.refs_2_
  41.8 1.9 %collective-permute-done.12.refs_5_.refs_3_ = bf16[128,512]{1,0:T(8,128)(2,1)S(1)} collective-permute-done((bf16[128,512]{1,0:T(8,128)(2,1)S(1)}, bf16[128,512]{1,0:T(8,128)(2,1)S(1)}, u32[]{:S(2)}, u32[]{:S(2)}) %collective-permute-start.12) | collective-permute-done | bytes 131104 | tf_op jit(solution)/shard_map/ppermute | solution.py:308
  43.7 0.0 collective-permute-done.13.refs_6_.came_ref
  43.7 0.3 collective-permute-start.14
  44.0 0.3 collective-permute-start.18
  44.3 1.5 %collective-permute-start.15 = (bf16[128,512]{1,0:T(8,128)(2,1)S(1)}, bf16[128,512]{1,0:T(8,128)(2,1)S(1)}, u32[]{:S(2)}, u32[]{:S(2)}) collective-permute-start(bf16[128,512]{1,0:T(8,128)(2,1)S(1)} %get-tuple-element.56), channel_id=1, source_target_pairs={{0,2},{1,3},{2,0},{3,1},{4,6},{5,7},{6,4},{7,5},{8,10},{9,11},{10,... | collective-permute-start | bytes 393224 | tf_op jit(solution)/shard_map/ppermute | solution.py:308
  45.8 0.0 collective-permute-start.16
  45.8 3.5 %collective-permute-start.17 = (bf16[128,256]{1,0:T(8,128)(2,1)S(1)}, bf16[128,256]{1,0:T(8,128)(2,1)S(1)}, u32[]{:S(2)}, u32[]{:S(2)}) collective-permute-start(bf16[128,256]{1,0:T(8,128)(2,1)S(1)} %get-tuple-element.59), channel_id=1, source_target_pairs={{0,8},{1,9},{2,10},{3,11},{4,12},{5,13},{6,14},{7,15},{8,0},{9,1},... | collective-permute-start | bytes 196616 | tf_op jit(solution)/shard_map/ppermute | solution.py:308
  49.3 0.3 collective-permute-done.18.came_ref
  49.7 4.1 %collective-permute-start.19 = (bf16[128,256]{1,0:T(8,128)(2,1)S(1)}, bf16[128,256]{1,0:T(8,128)(2,1)S(1)}, u32[]{:S(2)}, u32[]{:S(2)}) collective-permute-start(bf16[128,256]{1,0:T(8,128)(2,1)S(1)} %get-tuple-element.63), channel_id=1, source_target_pairs={{0,8},{1,9},{2,10},{3,11},{4,12},{5,13},{6,14},{7,15},{8,0},{9,1},... | collective-permute-start | bytes 196616 | tf_op jit(solution)/shard_map/ppermute | solution.py:308
  53.8 0.0 collective-permute-done.14.refs_1_
  53.8 1.3 %gate_products_0.1 = (bf16[128,4096]{1,0:T(8,128)(2,1)}, bf16[128,4096]{1,0:T(8,128)(2,1)}) custom-call(s32[1]{0:T(128)} %bitcast.pos_ref, bf16[128,4096]{1,0:T(8,128)(2,1)S(1)} %copy-done, bf16[128,4096]{1,0:T(8,128)(2,1)S(1)} %copy-done.1, bf16[128,512]{1,0:T(8,128)(2,1)S(1)} %get-tuple-element.64.refs_0_, ...), custom_call_target="tpu_custom_call" | custom-call | tf_op jit(solution)/shard_map/gate_products_0/pallas_call | solution.py:421
  55.1 0.0 collective-permute-done.17.refs_5_
  55.1 0.0 collective-permute-done.15.refs_2_
  55.1 1.8 %collective-permute-done.19.refs_7_ = bf16[128,256]{1,0:T(8,128)(2,1)S(1)} collective-permute-done((bf16[128,256]{1,0:T(8,128)(2,1)S(1)}, bf16[128,256]{1,0:T(8,128)(2,1)S(1)}, u32[]{:S(2)}, u32[]{:S(2)}) %collective-permute-start.19) | collective-permute-done | bytes 65568 | tf_op jit(solution)/shard_map/ppermute | solution.py:308
  56.9 1.4 %gate_products_1.1 = (bf16[128,4096]{1,0:T(8,128)(2,1)}, bf16[128,4096]{1,0:T(8,128)(2,1)}, f32[256,256]{1,0:T(8,128)}) custom-call(s32[1]{0:T(128)} %bitcast.pos_ref, bf16[128,4096]{1,0:T(8,128)(2,1)S(1)} %copy-done, bf16[128,4096]{1,0:T(8,128)(2,1)S(1)} %copy-done.1, ...), custom_call_target="tpu_custom_call", output_to_operand_aliasing={{0}: (11, {}), {1}: (12, {})} | custom-call | tf_op jit(solution)/shard_map/gate_products_1/pallas_call | solution.py:421
  (19 shorter events, 0.1 us)
Async XLA Ops:
  0.6 6.1 %copy-start.1 = (bf16[128,4096]{1,0:T(8,128)(2,1)S(1)}, bf16[128,4096]{1,0:T(8,128)(2,1)}, u32[]{:S(2)}) copy-start(bf16[128,4096]{1,0:T(8,128)(2,1)} %value_ref.3) | copy-start | bytes 3145732
  0.6 6.1 %copy-start = (bf16[128,4096]{1,0:T(8,128)(2,1)S(1)}, bf16[128,4096]{1,0:T(8,128)(2,1)}, u32[]{:S(2)}) copy-start(bf16[128,4096]{1,0:T(8,128)(2,1)} %key_ref.3) | copy-start | bytes 3145732
  0.7 8.6 %copy-start.5 = (bf16[256,256]{1,0:T(8,128)(2,1)S(1)}, bf16[256,256]{1,0:T(8,128)(2,1)}, u32[]{:S(2)}) copy-start(bf16[256,256]{1,0:T(8,128)(2,1)} %param.11) | copy-start | bytes 393220
  3.5 15.7 %copy-start.3 = (bf16[128,1024]{1,0:T(8,128)(2,1)S(1)}, bf16[128,1024]{1,0:T(8,128)(2,1)}, u32[]{:S(2)}) copy-start(bf16[128,1024]{1,0:T(8,128)(2,1)} %get-tuple-element.35.refs_0_) | copy-start | bytes 786436
  3.5 15.7 %collective-permute-start.2 = (bf16[128,1024]{1,0:T(8,128)(2,1)}, bf16[128,1024]{1,0:T(8,128)(2,1)S(1)}, u32[]{:S(2)}, u32[]{:S(2)}) collective-permute-start(bf16[128,1024]{1,0:T(8,128)(2,1)} %get-tuple-element.36), channel_id=1, source_target_pairs={{0,1},{1,0},{2,3},{3,2},{4,5},{5,4},{6,7},{7,6},{8,9},{9,8},{10,11... | collective-permute-start | bytes 786440 | tf_op jit(solution)/shard_map/ppermute | solution.py:308
  4.0 15.2 %collective-permute-start.3 = (bf16[128,1024]{1,0:T(8,128)(2,1)}, bf16[128,1024]{1,0:T(8,128)(2,1)S(1)}, u32[]{:S(2)}, u32[]{:S(2)}) collective-permute-start(bf16[128,1024]{1,0:T(8,128)(2,1)} %get-tuple-element.37), channel_id=1, source_target_pairs={{0,2},{1,3},{2,0},{3,1},{4,6},{5,7},{6,4},{7,5},{8,10},{9,11},{10,... | collective-permute-start | bytes 786440 | tf_op jit(solution)/shard_map/ppermute | solution.py:308
  6.6 21.6 %copy-start.2 = (bf16[1024,256]{1,0:T(8,128)(2,1)S(1)}, bf16[1024,256]{1,0:T(8,128)(2,1)}, u32[]{:S(2)}) copy-start(bf16[1024,256]{1,0:T(8,128)(2,1)} %constant.6.clone.table_ref) | copy-start | bytes 1572868
  6.6 12.6 %collective-permute-start.4 = (bf16[128,1024]{1,0:T(8,128)(2,1)}, bf16[128,1024]{1,0:T(8,128)(2,1)S(1)}, u32[]{:S(2)}, u32[]{:S(2)}) collective-permute-start(bf16[128,1024]{1,0:T(8,128)(2,1)} %get-tuple-element.38), channel_id=1, source_target_pairs={{0,3},{1,2},{2,1},{3,0},{4,7},{5,6},{6,5},{7,4},{8,11},{9,10},{10,... | collective-permute-start | bytes 786440 | tf_op jit(solution)/shard_map/ppermute | solution.py:308
  7.5 17.5 %collective-permute-start.8 = (bf16[256,512]{1,0:T(8,128)(2,1)S(1)}, bf16[256,512]{1,0:T(8,128)(2,1)S(1)}, u32[]{:S(2)}, u32[]{:S(2)}) collective-permute-start(bf16[256,512]{1,0:T(8,128)(2,1)S(1)} %get-tuple-element.44), channel_id=1, source_target_pairs={{0,2},{1,3},{2,0},{3,1},{4,6},{5,7},{6,4},{7,5},{8,10},{9,11},{10,... | collective-permute-start | bytes 786440 | tf_op jit(solution)/shard_map/ppermute | solution.py:308
  9.3 9.2 %collective-permute-start = (bf16[256,256]{1,0:T(8,128)(2,1)S(1)}, bf16[256,256]{1,0:T(8,128)(2,1)S(1)}, u32[]{:S(2)}, u32[]{:S(2)}) collective-permute-start(bf16[256,256]{1,0:T(8,128)(2,1)S(1)} %copy-done.5), channel_id=1, source_target_pairs={{0,8},{1,9},{2,10},{3,11},{4,12},{5,13},{6,14},{7,15},{8,0},{9,1},... | collective-permute-start | bytes 393224 | tf_op jit(solution)/shard_map/ppermute | solution.py:308
  18.5 9.7 %collective-permute-start.1 = (bf16[512,256]{1,0:T(8,128)(2,1)S(1)}, bf16[512,256]{1,0:T(8,128)(2,1)S(1)}, u32[]{:S(2)}, u32[]{:S(2)}) collective-permute-start(bf16[512,256]{1,0:T(8,128)(2,1)S(1)} %constant_dynamic-update-slice_fusion.refs_0_), channel_id=1, source_target_pairs={{0,4},{1,5},{2,6},{3,7},{4,0},{5,1},{6,2},{7,3},{8,12},{9,13},{10,... | collective-permute-start | bytes 786440 | tf_op jit(solution)/shard_map/ppermute | solution.py:308
  19.3 12.3 %collective-permute-start.7 = (bf16[256,512]{1,0:T(8,128)(2,1)S(1)}, bf16[256,512]{1,0:T(8,128)(2,1)S(1)}, u32[]{:S(2)}, u32[]{:S(2)}) collective-permute-start(bf16[256,512]{1,0:T(8,128)(2,1)S(1)} %get-tuple-element.43.refs_0_), channel_id=1, source_target_pairs={{4,0},{5,1},{6,2},{7,3},{8,4},{9,5},{10,6},{11,7},{12,8},{13,9},{1... | collective-permute-start | bytes 786440 | tf_op jit(solution)/shard_map/ppermute | solution.py:370
  25.0 6.6 %copy-start.4 = (s32[4]{0:T(128)S(1)}, s32[4]{0:T(128)}, u32[]{:S(2)}) copy-start(s32[4]{0:T(128)} %docs_ref.3) | copy-start | bytes 52
  25.0 6.6 %collective-permute-start.9 = (bf16[256,512]{1,0:T(8,128)(2,1)S(1)}, bf16[256,512]{1,0:T(8,128)(2,1)S(1)}, u32[]{:S(2)}, u32[]{:S(2)}) collective-permute-start(bf16[256,512]{1,0:T(8,128)(2,1)S(1)} %pack_0.1), channel_id=1, source_target_pairs={{0,1},{1,0},{2,3},{3,2},{4,5},{5,4},{6,7},{7,6},{8,9},{9,8},{10,11... | collective-permute-start | bytes 786440 | tf_op jit(solution)/shard_map/ppermute | solution.py:308
  25.1 10.3 %collective-permute-start.6 = (bf16[256,512]{1,0:T(8,128)(2,1)S(1)}, bf16[256,512]{1,0:T(8,128)(2,1)S(1)}, u32[]{:S(2)}, u32[]{:S(2)}) collective-permute-start(bf16[256,512]{1,0:T(8,128)(2,1)S(1)} %get-tuple-element.41), channel_id=1, source_target_pairs={{0,2},{1,3},{2,0},{3,1},{4,6},{5,7},{6,4},{7,5},{8,10},{9,11},{10,... | collective-permute-start | bytes 786440 | tf_op jit(solution)/shard_map/ppermute | solution.py:308
  26.9 10.7 %collective-permute-start.5 = (bf16[256,512]{1,0:T(8,128)(2,1)S(1)}, bf16[256,512]{1,0:T(8,128)(2,1)S(1)}, u32[]{:S(2)}, u32[]{:S(2)}) collective-permute-start(bf16[256,512]{1,0:T(8,128)(2,1)S(1)} %get-tuple-element.39), channel_id=1, source_target_pairs={{4,0},{5,1},{6,2},{7,3},{8,4},{9,5},{10,6},{11,7},{12,8},{13,9},{1... | collective-permute-start | bytes 786440 | tf_op jit(solution)/shard_map/ppermute | solution.py:370
  35.4 2.2 %collective-permute-start.10 = (bf16[256,512]{1,0:T(8,128)(2,1)S(1)}, bf16[256,512]{1,0:T(8,128)(2,1)S(1)}, u32[]{:S(2)}, u32[]{:S(2)}) collective-permute-start(bf16[256,512]{1,0:T(8,128)(2,1)S(1)} %pack_1.1), channel_id=1, source_target_pairs={{0,1},{1,0},{2,3},{3,2},{4,5},{5,4},{6,7},{7,6},{8,9},{9,8},{10,11... | collective-permute-start | bytes 786440 | tf_op jit(solution)/shard_map/ppermute | solution.py:308
  35.4 6.4 %collective-permute-start.11 = (bf16[128,512]{1,0:T(8,128)(2,1)S(1)}, bf16[128,512]{1,0:T(8,128)(2,1)S(1)}, u32[]{:S(2)}, u32[]{:S(2)}) collective-permute-start(bf16[128,512]{1,0:T(8,128)(2,1)S(1)} %get-tuple-element.52), channel_id=1, source_target_pairs={{0,2},{1,3},{2,0},{3,1},{4,6},{5,7},{6,4},{7,5},{8,10},{9,11},{10,... | collective-permute-start | bytes 393224 | tf_op jit(solution)/shard_map/ppermute | solution.py:308
  36.4 7.3 %collective-permute-start.12 = (bf16[128,512]{1,0:T(8,128)(2,1)S(1)}, bf16[128,512]{1,0:T(8,128)(2,1)S(1)}, u32[]{:S(2)}, u32[]{:S(2)}) collective-permute-start(bf16[128,512]{1,0:T(8,128)(2,1)S(1)} %get-tuple-element.53), channel_id=1, source_target_pairs={{0,3},{1,2},{2,1},{3,0},{4,7},{5,6},{6,5},{7,4},{8,11},{9,10},{10,... | collective-permute-start | bytes 393224 | tf_op jit(solution)/shard_map/ppermute | solution.py:308
  37.3 6.4 %collective-permute-start.13 = (bf16[256,256]{1,0:T(8,128)(2,1)S(1)}, bf16[256,256]{1,0:T(8,128)(2,1)S(1)}, u32[]{:S(2)}, u32[]{:S(2)}) collective-permute-start(bf16[256,256]{1,0:T(8,128)(2,1)S(1)} %get-tuple-element.54), channel_id=1, source_target_pairs={{0,4},{1,5},{2,6},{3,7},{4,0},{5,1},{6,2},{7,3},{8,12},{9,13},{10,... | collective-permute-start | bytes 393224 | tf_op jit(solution)/shard_map/ppermute | solution.py:308
  43.7 10.1 %collective-permute-start.14 = (bf16[128,1024]{1,0:T(8,128)(2,1)S(1)}, bf16[128,1024]{1,0:T(8,128)(2,1)S(1)}, u32[]{:S(2)}, u32[]{:S(2)}) collective-permute-start(bf16[128,1024]{1,0:T(8,128)(2,1)S(1)} %get-tuple-element.55), channel_id=1, source_target_pairs={{0,1},{1,0},{2,3},{3,2},{4,5},{5,4},{6,7},{7,6},{8,9},{9,8},{10,11... | collective-permute-start | bytes 786440 | tf_op jit(solution)/shard_map/ppermute | solution.py:308
  44.0 5.6 %collective-permute-start.18 = (bf16[256,256]{1,0:T(8,128)(2,1)S(1)}, bf16[256,256]{1,0:T(8,128)(2,1)S(1)}, u32[]{:S(2)}, u32[]{:S(2)}) collective-permute-start(bf16[256,256]{1,0:T(8,128)(2,1)S(1)} %get-tuple-element.61), channel_id=1, source_target_pairs={{0,4},{1,5},{2,6},{3,7},{4,0},{5,1},{6,2},{7,3},{8,12},{9,13},{10,... | collective-permute-start | bytes 393224 | tf_op jit(solution)/shard_map/ppermute | solution.py:308
  44.3 10.8 %collective-permute-start.15 = (bf16[128,512]{1,0:T(8,128)(2,1)S(1)}, bf16[128,512]{1,0:T(8,128)(2,1)S(1)}, u32[]{:S(2)}, u32[]{:S(2)}) collective-permute-start(bf16[128,512]{1,0:T(8,128)(2,1)S(1)} %get-tuple-element.56), channel_id=1, source_target_pairs={{0,2},{1,3},{2,0},{3,1},{4,6},{5,7},{6,4},{7,5},{8,10},{9,11},{10,... | collective-permute-start | bytes 393224 | tf_op jit(solution)/shard_map/ppermute | solution.py:308
  45.8 9.3 %collective-permute-start.16 = (bf16[128,512]{1,0:T(8,128)(2,1)S(1)}, bf16[128,512]{1,0:T(8,128)(2,1)S(1)}, u32[]{:S(2)}, u32[]{:S(2)}) collective-permute-start(bf16[128,512]{1,0:T(8,128)(2,1)S(1)} %get-tuple-element.57), channel_id=1, source_target_pairs={{0,3},{1,2},{2,1},{3,0},{4,7},{5,6},{6,5},{7,4},{8,11},{9,10},{10,... | collective-permute-start | bytes 393224 | tf_op jit(solution)/shard_map/ppermute | solution.py:308
  45.8 9.3 %collective-permute-start.17 = (bf16[128,256]{1,0:T(8,128)(2,1)S(1)}, bf16[128,256]{1,0:T(8,128)(2,1)S(1)}, u32[]{:S(2)}, u32[]{:S(2)}) collective-permute-start(bf16[128,256]{1,0:T(8,128)(2,1)S(1)} %get-tuple-element.59), channel_id=1, source_target_pairs={{0,8},{1,9},{2,10},{3,11},{4,12},{5,13},{6,14},{7,15},{8,0},{9,1},... | collective-permute-start | bytes 196616 | tf_op jit(solution)/shard_map/ppermute | solution.py:308
  49.7 7.3 %collective-permute-start.19 = (bf16[128,256]{1,0:T(8,128)(2,1)S(1)}, bf16[128,256]{1,0:T(8,128)(2,1)S(1)}, u32[]{:S(2)}, u32[]{:S(2)}) collective-permute-start(bf16[128,256]{1,0:T(8,128)(2,1)S(1)} %get-tuple-element.63), channel_id=1, source_target_pairs={{0,8},{1,9},{2,10},{3,11},{4,12},{5,13},{6,14},{7,15},{8,0},{9,1},... | collective-permute-start | bytes 196616 | tf_op jit(solution)/shard_map/ppermute | solution.py:308

commit v4 on v3

--- a/solution.py
+++ b/solution.py
@@ -101,7 +101,7 @@
     cut_products(pieces, offset, (left_hbm, right_hbm), (left_ref, right_ref), sems, outs)
 
 
-def input_kernel(pieces, offset, pos_ref, left_hbm, right_hbm, own, near, *refs):
+def input_kernel(pieces, offset, pos_ref, left_hbm, right_hbm, _, own, near, *refs):
     far, (left_ref, right_ref, sems) = refs[:-3], refs[-3:]
     rows = own.shape[0]
     place = pos_ref[0] % QUAD
@@ -324,26 +324,29 @@
     key_branch, value_branch = grouped(key_branch), grouped(value_branch)
     out_grad, query_gate = grouped(out_grad), grouped(query_gate)
     parts, step = [filter_taps], quads // 2
-    while step:
+    while step > 1:
         held = parts[0] if len(parts) == 1 else jnp.concatenate(parts, axis=0)
         parts, step = [held, to_quad(held, step)], step // 2
+    if quads > 1:
+        first = to_quad(parts[0], 1)
+        parts += [first, *[to_quad(gate([part], first)[0], 1) for part in parts[1:]]]
 
     alone, both = jax.ShapeDtypeStruct((rows, width), BF16), jax.ShapeDtypeStruct((rows, CHUNKS * width), BF16)
-    def products(kernel, left, right, types, limit, name):
+    def products(kernel, left, right, types, limit, name, *after):
         return pl.pallas_call(
             partial(kernel, pieces, offset),
             out_shape=types,
-            in_specs=[SMEM] + [HBM] * 2,
+            in_specs=[SMEM] + [HBM] * 2 + [ANY] * len(after),
             out_specs=[VMEM] * len(types),
             scratch_shapes=[pltpu.VMEM((rows, channels), BF16)] * 2 + [pltpu.SemaphoreType.DMA((2, pieces[0]))],
             compiler_params=pltpu.CompilerParams(vmem_limit_bytes=limit * 1024 * 1024),
             name=name,
-        )(pos, left, right)
+        )(pos, left, right, *after)
 
     own, near, same, other = products(grad_kernel, out_grad, query_gate, [both] * 4, 60, "gated_grad")
     grads = [own, to_member(near, 1), to_member(same, 2), to_member(other, 3)]
     pair_type = jax.ShapeDtypeStruct((2 * rows, width), BF16)
-    own, near, *far_inputs = products(input_kernel, key_branch, value_branch, [both] * 2 + [pair_type] * CHUNKS, 40, "conv_input")
+    own, near, *far_inputs = products(input_kernel, key_branch, value_branch, [both] * 2 + [pair_type] * CHUNKS, 40, "conv_input", grads[1])
     own_input, near_input = own, near
     far_inputs = [to_member(value, 2) for value in far_inputs]
     spectra = pl.pallas_call(
@@ -363,7 +366,7 @@
         compiler_params=PARAMS,
         name="halo",
     )(pos, *grads)
-    before = [first_blocks[0]]
+    before = [first_blocks[0], spectra]
     results, chunk_grads, chunk_terms = [], [], []
     nearest = []
     for chunk in range(CHUNKS):

time: 58.5 us -> 57.2 us (0.978)
  waiting for transfers between devices: 18.3 us -> 13.5 us
  starting transfers between devices: 24.7 us -> 28.1 us
    ppermute x18 -> x19, waiting for transfers between devices: 15.5 us -> 11.8 us  [to_member(): lax.ppermute(value, 'ctx', [(i, i ^ k) for i in range(blocks)])]
    ppermute x18 -> x19, starting transfers between devices: 22.1 us -> 25.5 us  [to_member(): lax.ppermute(value, 'ctx', [(i, i ^ k) for i in range(blocks)])]
    ppermute x2, waiting for transfers between devices: 2.87 us -> 1.7 us  [shards(): lax.ppermute(first_blocks[chunk], 'ctx', [(i, i - QUAD) for i in range(QU...]
  transfers between devices with their start and end apart: 20 -> 21, of which waited for: 7 -> 10; matrix products, arithmetic and copies ran while one was open for 0% -> 0% of each run, Pallas kernels for 17% -> 18%
where the time goes in v4:
time: 57.2 us; the launch traced here: 57.1 us
  starting transfers between devices  28.1 us (49%)
  Pallas kernels  14.5 us (25%)
  waiting for transfers between devices  13.5 us (24%)
  between operations  0.82 us (1%)
    ppermute x19, starting transfers between devices, to_member(): lax.ppermute(value, 'ctx', [(i, i ^ k) for i in range(blocks)])  25.5 us
    ppermute x19, waiting for transfers between devices, to_member(): lax.ppermute(value, 'ctx', [(i, i ^ k) for i in range(blocks)])  11.8 us
    pallas_call x2, Pallas kernels, shards(): pl.pallas_call(partial(conv_kernel, chunk, quads, doc_blocks.shape[0]), o...  7.55 us
    pallas_call x2, Pallas kernels, products(): pl.pallas_call(partial(kernel, pieces, offset), out_shape=types, in_specs...  3.63 us
    pallas_call x2, Pallas kernels, shards(): pl.pallas_call(partial(final_kernel, chunk, pieces, offset, 1.0 / math.sq...  2.7 us
    ppermute x2, starting transfers between devices, shards(): lax.ppermute(first_blocks[chunk], 'ctx', [(i, i - QUAD) for i in range(QU...  2.57 us
    ppermute x2, waiting for transfers between devices, shards(): lax.ppermute(first_blocks[chunk], 'ctx', [(i, i - QUAD) for i in range(QU...  1.7 us
  transfers between devices with their start and end apart: 21, of which 10 were waited for; matrix products, arithmetic and copies ran while one was open for 0% of the time, Pallas kernels for 18%

profile of v4, /device:TPU:0, one launch (start us, length us, event | category | flops | bytes accessed | tf_op | source)
XLA Modules:
  0.0 57.1 jit_solution(1939423074550597095)
XLA Ops:
  0.7 2.8 %gated_grad.1 = (bf16[128,1024]{1,0:T(8,128)(2,1)}, bf16[128,1024]{1,0:T(8,128)(2,1)}, bf16[128,1024]{1,0:T(8,128)(2,1)}, bf16[128,1024]{1,0:T(8,128)(2,1)}) custom-call(s32[1]{0:T(128)} %bitcast.pos_ref, bf16[128,4096]{1,0:T(8,128)(2,1)} %left_hbm.2, bf16[128,4096]{1,0:T(8,128)(2,1)} %right_hbm.2), custom_call_target="tpu_custom_call" | custom-call | tf_op jit(solution)/shard_map/gated_grad/pallas_call | solution.py:336
  3.5 0.0 copy-start.3
  3.5 0.0 copy-start.2
  3.5 0.0 copy-start.4
  3.5 0.5 collective-permute-start.3
  4.0 2.6 %collective-permute-start.4 = (bf16[128,1024]{1,0:T(8,128)(2,1)}, bf16[128,1024]{1,0:T(8,128)(2,1)S(1)}, u32[]{:S(2)}, u32[]{:S(2)}) collective-permute-start(bf16[128,1024]{1,0:T(8,128)(2,1)} %get-tuple-element.37), channel_id=1, source_target_pairs={{0,2},{1,3},{2,0},{3,1},{4,6},{5,7},{6,4},{7,5},{8,10},{9,11},{10,... | collective-permute-start | bytes 786440 | tf_op jit(solution)/shard_map/ppermute | solution.py:308
  6.6 0.1 collective-permute-start.5
  6.7 2.8 %collective-permute-start = (bf16[256,256]{1,0:T(8,128)(2,1)}, bf16[256,256]{1,0:T(8,128)(2,1)S(1)}, u32[]{:S(2)}, u32[]{:S(2)}) collective-permute-start(bf16[256,256]{1,0:T(8,128)(2,1)} %refs_0_.1), channel_id=1, source_target_pairs={{0,8},{1,9},{2,10},{3,11},{4,12},{5,13},{6,14},{7,15},{8,0},{9,1},... | collective-permute-start | bytes 393224 | tf_op jit(solution)/shard_map/ppermute | solution.py:308
  9.5 1.6 %collective-permute-start.1 = (bf16[256,256]{1,0:T(8,128)(2,1)}, bf16[256,256]{1,0:T(8,128)(2,1)S(1)}, u32[]{:S(2)}, u32[]{:S(2)}) collective-permute-start(bf16[256,256]{1,0:T(8,128)(2,1)} %refs_0_.1), channel_id=1, source_target_pairs={{0,4},{1,5},{2,6},{3,7},{4,0},{5,1},{6,2},{7,3},{8,12},{9,13},{10,... | collective-permute-start | bytes 393224 | tf_op jit(solution)/shard_map/ppermute | solution.py:308
  11.1 0.0 collective-permute-done.3.refs_1_._
  11.1 0.8 %conv_input.1 = (bf16[128,1024]{1,0:T(8,128)(2,1)S(1)}, bf16[128,1024]{1,0:T(8,128)(2,1)S(1)}, bf16[256,512]{1,0:T(8,128)(2,1)S(1)}, bf16[256,512]{1,0:T(8,128)(2,1)S(1)}) custom-call(s32[1]{0:T(128)} %bitcast.pos_ref, bf16[128,4096]{1,0:T(8,128)(2,1)S(1)} %copy-done, bf16[128,4096]{1,0:T(8,128)(2,1)S(1)} %copy-done.1, ...), custom_call_target="tpu_custom_call" | custom-call | tf_op jit(solution)/shard_map/conv_input/pallas_call | solution.py:336
  11.9 1.6 %collective-permute-start.9 = (bf16[256,512]{1,0:T(8,128)(2,1)S(1)}, bf16[256,512]{1,0:T(8,128)(2,1)S(1)}, u32[]{:S(2)}, u32[]{:S(2)}) collective-permute-start(bf16[256,512]{1,0:T(8,128)(2,1)S(1)} %get-tuple-element.44), channel_id=1, source_target_pairs={{0,2},{1,3},{2,0},{3,1},{4,6},{5,7},{6,4},{7,5},{8,10},{9,11},{10,... | collective-permute-start | bytes 786440 | tf_op jit(solution)/shard_map/ppermute | solution.py:308
  13.5 3.2 %collective-permute-done.refs_1_ = bf16[256,256]{1,0:T(8,128)(2,1)S(1)} collective-permute-done((bf16[256,256]{1,0:T(8,128)(2,1)}, bf16[256,256]{1,0:T(8,128)(2,1)S(1)}, u32[]{:S(2)}, u32[]{:S(2)}) %collective-permute-start) | collective-permute-done | bytes 131104 | tf_op jit(solution)/shard_map/ppermute | solution.py:308
  16.6 0.2 collective-permute-done.1.refs_1_.refs_2_
  16.8 1.5 %collective-permute-start.2 = (bf16[256,256]{1,0:T(8,128)(2,1)S(1)}, bf16[256,256]{1,0:T(8,128)(2,1)S(1)}, u32[]{:S(2)}, u32[]{:S(2)}) collective-permute-start(bf16[256,256]{1,0:T(8,128)(2,1)S(1)} %gate.2), channel_id=1, source_target_pairs={{0,4},{1,5},{2,6},{3,7},{4,0},{5,1},{6,2},{7,3},{8,12},{9,13},{10,... | collective-permute-start | bytes 393224 | tf_op jit(solution)/shard_map/ppermute | solution.py:308
  18.3 0.0 collective-permute-done.4.refs_2_
  18.3 0.9 %collective-permute-done.5.refs_3_ = bf16[128,1024]{1,0:T(8,128)(2,1)S(1)} collective-permute-done((bf16[128,1024]{1,0:T(8,128)(2,1)}, bf16[128,1024]{1,0:T(8,128)(2,1)S(1)}, u32[]{:S(2)}, u32[]{:S(2)}) %collective-permute-start.5) | collective-permute-done | bytes 262176 | tf_op jit(solution)/shard_map/ppermute | solution.py:308
  19.2 0.1 halo.1
  19.3 1.3 %collective-permute-start.8 = (bf16[256,512]{1,0:T(8,128)(2,1)S(1)}, bf16[256,512]{1,0:T(8,128)(2,1)S(1)}, u32[]{:S(2)}, u32[]{:S(2)}) collective-permute-start(bf16[256,512]{1,0:T(8,128)(2,1)S(1)} %get-tuple-element.43.refs_0_), channel_id=1, source_target_pairs={{4,0},{5,1},{6,2},{7,3},{8,4},{9,5},{10,6},{11,7},{12,8},{13,9},{1... | collective-permute-start | bytes 786440 | tf_op jit(solution)/shard_map/ppermute | solution.py:373
  20.6 1.2 %collective-permute-done.2.refs_3_ = bf16[256,256]{1,0:T(8,128)(2,1)S(1)} collective-permute-done((bf16[256,256]{1,0:T(8,128)(2,1)S(1)}, bf16[256,256]{1,0:T(8,128)(2,1)S(1)}, u32[]{:S(2)}, u32[]{:S(2)}) %collective-permute-start.2) | collective-permute-done | bytes 131104 | tf_op jit(solution)/shard_map/ppermute | solution.py:308
  21.8 0.5 filter_spectra.1.refs_1_.filter_ref
  22.3 0.0 copy-start.5
  22.3 2.7 %collective-permute-done.9.came_ref.refs_5_ = bf16[256,512]{1,0:T(8,128)(2,1)S(1)} collective-permute-done((bf16[256,512]{1,0:T(8,128)(2,1)S(1)}, bf16[256,512]{1,0:T(8,128)(2,1)S(1)}, u32[]{:S(2)}, u32[]{:S(2)}) %collective-permute-start.9) | collective-permute-done | bytes 262176 | tf_op jit(solution)/shard_map/ppermute | solution.py:308
  25.0 0.1 collective-permute-start.10
  25.1 1.8 %collective-permute-start.7 = (bf16[256,512]{1,0:T(8,128)(2,1)S(1)}, bf16[256,512]{1,0:T(8,128)(2,1)S(1)}, u32[]{:S(2)}, u32[]{:S(2)}) collective-permute-start(bf16[256,512]{1,0:T(8,128)(2,1)S(1)} %get-tuple-element.41), channel_id=1, source_target_pairs={{0,2},{1,3},{2,0},{3,1},{4,6},{5,7},{6,4},{7,5},{8,10},{9,11},{10,... | collective-permute-start | bytes 786440 | tf_op jit(solution)/shard_map/ppermute | solution.py:308
  26.9 1.3 %collective-permute-start.6 = (bf16[256,512]{1,0:T(8,128)(2,1)S(1)}, bf16[256,512]{1,0:T(8,128)(2,1)S(1)}, u32[]{:S(2)}, u32[]{:S(2)}) collective-permute-start(bf16[256,512]{1,0:T(8,128)(2,1)S(1)} %get-tuple-element.39), channel_id=1, source_target_pairs={{4,0},{5,1},{6,2},{7,3},{8,4},{9,5},{10,6},{11,7},{12,8},{13,9},{1... | collective-permute-start | bytes 786440 | tf_op jit(solution)/shard_map/ppermute | solution.py:373
  28.2 1.7 %collective-permute-done.8.halo_ref = bf16[256,512]{1,0:T(8,128)(2,1)S(1)} collective-permute-done((bf16[256,512]{1,0:T(8,128)(2,1)S(1)}, bf16[256,512]{1,0:T(8,128)(2,1)S(1)}, u32[]{:S(2)}, u32[]{:S(2)}) %collective-permute-start.8) | collective-permute-done | bytes 262176 | tf_op jit(solution)/shard_map/ppermute | solution.py:373
  29.9 0.0 collective-permute-done.10.refs_6_
  29.9 3.8 %conv_0.1 = (bf16[128,512]{1,0:T(8,128)(2,1)S(1)}, bf16[128,512]{1,0:T(8,128)(2,1)S(1)}, bf16[128,512]{1,0:T(8,128)(2,1)S(1)}, bf16[128,512]{1,0:T(8,128)(2,1)S(...) custom-call(s32[1]{0:T(128)} %bitcast.pos_ref, s32[4]{0:T(128)S(1)} %copy-done.5, ...), custom_call_target="tpu_custom_call" | custom-call | tf_op jit(solution)/shard_map/conv_0/pallas_call | solution.py:383
  33.7 0.1 collective-permute-done.7.came_ref.refs_5_
  33.8 0.1 collective-permute-start.11
  33.9 1.8 %collective-permute-start.12 = (bf16[128,512]{1,0:T(8,128)(2,1)S(1)}, bf16[128,512]{1,0:T(8,128)(2,1)S(1)}, u32[]{:S(2)}, u32[]{:S(2)}) collective-permute-start(bf16[128,512]{1,0:T(8,128)(2,1)S(1)} %get-tuple-element.52), channel_id=1, source_target_pairs={{0,2},{1,3},{2,0},{3,1},{4,6},{5,7},{6,4},{7,5},{8,10},{9,11},{10,... | collective-permute-start | bytes 393224 | tf_op jit(solution)/shard_map/ppermute | solution.py:308
  35.7 0.1 collective-permute-start.13
  35.8 1.8 %collective-permute-start.14 = (bf16[256,256]{1,0:T(8,128)(2,1)S(1)}, bf16[256,256]{1,0:T(8,128)(2,1)S(1)}, u32[]{:S(2)}, u32[]{:S(2)}) collective-permute-start(bf16[256,256]{1,0:T(8,128)(2,1)S(1)} %get-tuple-element.54), channel_id=1, source_target_pairs={{0,4},{1,5},{2,6},{3,7},{4,0},{5,1},{6,2},{7,3},{8,12},{9,13},{10,... | collective-permute-start | bytes 393224 | tf_op jit(solution)/shard_map/ppermute | solution.py:308
  37.6 3.8 %conv_1.1 = (bf16[128,512]{1,0:T(8,128)(2,1)S(1)}, bf16[128,1024]{1,0:T(8,128)(2,1)S(1)}, bf16[128,512]{1,0:T(8,128)(2,1)S(1)}, bf16[128,512]{1,0:T(8,128)(2,1)S...) custom-call(s32[1]{0:T(128)} %bitcast.pos_ref, s32[4]{0:T(128)S(1)} %copy-done.5, ...), custom_call_target="tpu_custom_call" | custom-call | tf_op jit(solution)/shard_map/conv_1/pallas_call | solution.py:383
  41.4 0.8 %collective-permute-done.13.refs_5_.refs_3_ = bf16[128,512]{1,0:T(8,128)(2,1)S(1)} collective-permute-done((bf16[128,512]{1,0:T(8,128)(2,1)S(1)}, bf16[128,512]{1,0:T(8,128)(2,1)S(1)}, u32[]{:S(2)}, u32[]{:S(2)}) %collective-permute-start.13) | collective-permute-done | bytes 131104 | tf_op jit(solution)/shard_map/ppermute | solution.py:308
  42.2 0.3 collective-permute-start.15
  42.5 1.8 %collective-permute-start.19 = (bf16[256,256]{1,0:T(8,128)(2,1)S(1)}, bf16[256,256]{1,0:T(8,128)(2,1)S(1)}, u32[]{:S(2)}, u32[]{:S(2)}) collective-permute-start(bf16[256,256]{1,0:T(8,128)(2,1)S(1)} %get-tuple-element.61), channel_id=1, source_target_pairs={{0,4},{1,5},{2,6},{3,7},{4,0},{5,1},{6,2},{7,3},{8,12},{9,13},{10,... | collective-permute-start | bytes 393224 | tf_op jit(solution)/shard_map/ppermute | solution.py:308
  44.3 1.5 %collective-permute-start.16 = (bf16[128,512]{1,0:T(8,128)(2,1)S(1)}, bf16[128,512]{1,0:T(8,128)(2,1)S(1)}, u32[]{:S(2)}, u32[]{:S(2)}) collective-permute-start(bf16[128,512]{1,0:T(8,128)(2,1)S(1)} %get-tuple-element.56), channel_id=1, source_target_pairs={{0,2},{1,3},{2,0},{3,1},{4,6},{5,7},{6,4},{7,5},{8,10},{9,11},{10,... | collective-permute-start | bytes 393224 | tf_op jit(solution)/shard_map/ppermute | solution.py:308
  45.8 2.7 %collective-permute-start.18 = (bf16[128,256]{1,0:T(8,128)(2,1)S(1)}, bf16[128,256]{1,0:T(8,128)(2,1)S(1)}, u32[]{:S(2)}, u32[]{:S(2)}) collective-permute-start(bf16[128,256]{1,0:T(8,128)(2,1)S(1)} %get-tuple-element.59), channel_id=1, source_target_pairs={{0,8},{1,9},{2,10},{3,11},{4,12},{5,13},{6,14},{7,15},{8,0},{9,1},... | collective-permute-start | bytes 196616 | tf_op jit(solution)/shard_map/ppermute | solution.py:308
  48.5 0.0 collective-permute-done.19.came_ref
  48.5 3.0 %collective-permute-start.20 = (bf16[128,256]{1,0:T(8,128)(2,1)S(1)}, bf16[128,256]{1,0:T(8,128)(2,1)S(1)}, u32[]{:S(2)}, u32[]{:S(2)}) collective-permute-start(bf16[128,256]{1,0:T(8,128)(2,1)S(1)} %get-tuple-element.63), channel_id=1, source_target_pairs={{0,8},{1,9},{2,10},{3,11},{4,12},{5,13},{6,14},{7,15},{8,0},{9,1},... | collective-permute-start | bytes 196616 | tf_op jit(solution)/shard_map/ppermute | solution.py:308
  51.5 0.0 collective-permute-done.15.refs_1_
  51.5 1.3 %gate_products_0.1 = (bf16[128,4096]{1,0:T(8,128)(2,1)}, bf16[128,4096]{1,0:T(8,128)(2,1)}) custom-call(s32[1]{0:T(128)} %bitcast.pos_ref, bf16[128,4096]{1,0:T(8,128)(2,1)S(1)} %copy-done, bf16[128,4096]{1,0:T(8,128)(2,1)S(1)} %copy-done.1, bf16[128,512]{1,0:T(8,128)(2,1)S(1)} %get-tuple-element.64.refs_0_, ...), custom_call_target="tpu_custom_call" | custom-call | tf_op jit(solution)/shard_map/gate_products_0/pallas_call | solution.py:424
  52.8 0.9 %collective-permute-done.18.refs_5_ = bf16[128,256]{1,0:T(8,128)(2,1)S(1)} collective-permute-done((bf16[128,256]{1,0:T(8,128)(2,1)S(1)}, bf16[128,256]{1,0:T(8,128)(2,1)S(1)}, u32[]{:S(2)}, u32[]{:S(2)}) %collective-permute-start.18) | collective-permute-done | bytes 65568 | tf_op jit(solution)/shard_map/ppermute | solution.py:308
  53.7 0.0 collective-permute-done.16.refs_2_
  53.7 1.9 %collective-permute-done.20.refs_7_ = bf16[128,256]{1,0:T(8,128)(2,1)S(1)} collective-permute-done((bf16[128,256]{1,0:T(8,128)(2,1)S(1)}, bf16[128,256]{1,0:T(8,128)(2,1)S(1)}, u32[]{:S(2)}, u32[]{:S(2)}) %collective-permute-start.20) | collective-permute-done | bytes 65568 | tf_op jit(solution)/shard_map/ppermute | solution.py:308
  55.6 1.4 %gate_products_1.1 = (bf16[128,4096]{1,0:T(8,128)(2,1)}, bf16[128,4096]{1,0:T(8,128)(2,1)}, f32[256,256]{1,0:T(8,128)}) custom-call(s32[1]{0:T(128)} %bitcast.pos_ref, bf16[128,4096]{1,0:T(8,128)(2,1)S(1)} %copy-done, bf16[128,4096]{1,0:T(8,128)(2,1)S(1)} %copy-done.1, ...), custom_call_target="tpu_custom_call", output_to_operand_aliasing={{0}: (11, {}), {1}: (12, {})} | custom-call | tf_op jit(solution)/shard_map/gate_products_1/pallas_call | solution.py:424
  (21 shorter events, 0.1 us)
Async XLA Ops:
  0.6 10.5 %copy-start.1 = (bf16[128,4096]{1,0:T(8,128)(2,1)S(1)}, bf16[128,4096]{1,0:T(8,128)(2,1)}, u32[]{:S(2)}) copy-start(bf16[128,4096]{1,0:T(8,128)(2,1)} %value_ref.3) | copy-start | bytes 3145732
  0.6 10.4 %copy-start = (bf16[128,4096]{1,0:T(8,128)(2,1)S(1)}, bf16[128,4096]{1,0:T(8,128)(2,1)}, u32[]{:S(2)}) copy-start(bf16[128,4096]{1,0:T(8,128)(2,1)} %key_ref.3) | copy-start | bytes 3145732
  3.5 15.7 %copy-start.3 = (bf16[128,1024]{1,0:T(8,128)(2,1)S(1)}, bf16[128,1024]{1,0:T(8,128)(2,1)}, u32[]{:S(2)}) copy-start(bf16[128,1024]{1,0:T(8,128)(2,1)} %get-tuple-element.35.refs_0_) | copy-start | bytes 786436
  3.5 18.3 %copy-start.2 = (bf16[1024,256]{1,0:T(8,128)(2,1)S(1)}, bf16[1024,256]{1,0:T(8,128)(2,1)}, u32[]{:S(2)}) copy-start(bf16[1024,256]{1,0:T(8,128)(2,1)} %constant.6.clone.table_ref) | copy-start | bytes 1572868
  3.5 18.3 %copy-start.4 = (bf16[256,256]{1,0:T(8,128)(2,1)S(1)}, bf16[256,256]{1,0:T(8,128)(2,1)}, u32[]{:S(2)}) copy-start(bf16[256,256]{1,0:T(8,128)(2,1)} %refs_0_.1) | copy-start | bytes 393220
  3.5 7.6 %collective-permute-start.3 = (bf16[128,1024]{1,0:T(8,128)(2,1)}, bf16[128,1024]{1,0:T(8,128)(2,1)S(1)}, u32[]{:S(2)}, u32[]{:S(2)}) collective-permute-start(bf16[128,1024]{1,0:T(8,128)(2,1)} %get-tuple-element.36), channel_id=1, source_target_pairs={{0,1},{1,0},{2,3},{3,2},{4,5},{5,4},{6,7},{7,6},{8,9},{9,8},{10,11... | collective-permute-start | bytes 786440 | tf_op jit(solution)/shard_map/ppermute | solution.py:308
  4.0 14.3 %collective-permute-start.4 = (bf16[128,1024]{1,0:T(8,128)(2,1)}, bf16[128,1024]{1,0:T(8,128)(2,1)S(1)}, u32[]{:S(2)}, u32[]{:S(2)}) collective-permute-start(bf16[128,1024]{1,0:T(8,128)(2,1)} %get-tuple-element.37), channel_id=1, source_target_pairs={{0,2},{1,3},{2,0},{3,1},{4,6},{5,7},{6,4},{7,5},{8,10},{9,11},{10,... | collective-permute-start | bytes 786440 | tf_op jit(solution)/shard_map/ppermute | solution.py:308
  6.6 12.6 %collective-permute-start.5 = (bf16[128,1024]{1,0:T(8,128)(2,1)}, bf16[128,1024]{1,0:T(8,128)(2,1)S(1)}, u32[]{:S(2)}, u32[]{:S(2)}) collective-permute-start(bf16[128,1024]{1,0:T(8,128)(2,1)} %get-tuple-element.38), channel_id=1, source_target_pairs={{0,3},{1,2},{2,1},{3,0},{4,7},{5,6},{6,5},{7,4},{8,11},{9,10},{10,... | collective-permute-start | bytes 786440 | tf_op jit(solution)/shard_map/ppermute | solution.py:308
  6.7 9.9 %collective-permute-start = (bf16[256,256]{1,0:T(8,128)(2,1)}, bf16[256,256]{1,0:T(8,128)(2,1)S(1)}, u32[]{:S(2)}, u32[]{:S(2)}) collective-permute-start(bf16[256,256]{1,0:T(8,128)(2,1)} %refs_0_.1), channel_id=1, source_target_pairs={{0,8},{1,9},{2,10},{3,11},{4,12},{5,13},{6,14},{7,15},{8,0},{9,1},... | collective-permute-start | bytes 393224 | tf_op jit(solution)/shard_map/ppermute | solution.py:308
  9.5 7.3 %collective-permute-start.1 = (bf16[256,256]{1,0:T(8,128)(2,1)}, bf16[256,256]{1,0:T(8,128)(2,1)S(1)}, u32[]{:S(2)}, u32[]{:S(2)}) collective-permute-start(bf16[256,256]{1,0:T(8,128)(2,1)} %refs_0_.1), channel_id=1, source_target_pairs={{0,4},{1,5},{2,6},{3,7},{4,0},{5,1},{6,2},{7,3},{8,12},{9,13},{10,... | collective-permute-start | bytes 393224 | tf_op jit(solution)/shard_map/ppermute | solution.py:308
  11.9 13.1 %collective-permute-start.9 = (bf16[256,512]{1,0:T(8,128)(2,1)S(1)}, bf16[256,512]{1,0:T(8,128)(2,1)S(1)}, u32[]{:S(2)}, u32[]{:S(2)}) collective-permute-start(bf16[256,512]{1,0:T(8,128)(2,1)S(1)} %get-tuple-element.44), channel_id=1, source_target_pairs={{0,2},{1,3},{2,0},{3,1},{4,6},{5,7},{6,4},{7,5},{8,10},{9,11},{10,... | collective-permute-start | bytes 786440 | tf_op jit(solution)/shard_map/ppermute | solution.py:308
  16.8 5.0 %collective-permute-start.2 = (bf16[256,256]{1,0:T(8,128)(2,1)S(1)}, bf16[256,256]{1,0:T(8,128)(2,1)S(1)}, u32[]{:S(2)}, u32[]{:S(2)}) collective-permute-start(bf16[256,256]{1,0:T(8,128)(2,1)S(1)} %gate.2), channel_id=1, source_target_pairs={{0,4},{1,5},{2,6},{3,7},{4,0},{5,1},{6,2},{7,3},{8,12},{9,13},{10,... | collective-permute-start | bytes 393224 | tf_op jit(solution)/shard_map/ppermute | solution.py:308
  19.3 10.6 %collective-permute-start.8 = (bf16[256,512]{1,0:T(8,128)(2,1)S(1)}, bf16[256,512]{1,0:T(8,128)(2,1)S(1)}, u32[]{:S(2)}, u32[]{:S(2)}) collective-permute-start(bf16[256,512]{1,0:T(8,128)(2,1)S(1)} %get-tuple-element.43.refs_0_), channel_id=1, source_target_pairs={{4,0},{5,1},{6,2},{7,3},{8,4},{9,5},{10,6},{11,7},{12,8},{13,9},{1... | collective-permute-start | bytes 786440 | tf_op jit(solution)/shard_map/ppermute | solution.py:373
  22.3 7.6 %copy-start.5 = (s32[4]{0:T(128)S(1)}, s32[4]{0:T(128)}, u32[]{:S(2)}) copy-start(s32[4]{0:T(128)} %docs_ref.3) | copy-start | bytes 52
  25.0 4.9 %collective-permute-start.10 = (bf16[256,512]{1,0:T(8,128)(2,1)S(1)}, bf16[256,512]{1,0:T(8,128)(2,1)S(1)}, u32[]{:S(2)}, u32[]{:S(2)}) collective-permute-start(bf16[256,512]{1,0:T(8,128)(2,1)S(1)} %pack_0.1), channel_id=1, source_target_pairs={{0,1},{1,0},{2,3},{3,2},{4,5},{5,4},{6,7},{7,6},{8,9},{9,8},{10,11... | collective-permute-start | bytes 786440 | tf_op jit(solution)/shard_map/ppermute | solution.py:308
  25.1 8.7 %collective-permute-start.7 = (bf16[256,512]{1,0:T(8,128)(2,1)S(1)}, bf16[256,512]{1,0:T(8,128)(2,1)S(1)}, u32[]{:S(2)}, u32[]{:S(2)}) collective-permute-start(bf16[256,512]{1,0:T(8,128)(2,1)S(1)} %get-tuple-element.41), channel_id=1, source_target_pairs={{0,2},{1,3},{2,0},{3,1},{4,6},{5,7},{6,4},{7,5},{8,10},{9,11},{10,... | collective-permute-start | bytes 786440 | tf_op jit(solution)/shard_map/ppermute | solution.py:308
  26.9 10.7 %collective-permute-start.6 = (bf16[256,512]{1,0:T(8,128)(2,1)S(1)}, bf16[256,512]{1,0:T(8,128)(2,1)S(1)}, u32[]{:S(2)}, u32[]{:S(2)}) collective-permute-start(bf16[256,512]{1,0:T(8,128)(2,1)S(1)} %get-tuple-element.39), channel_id=1, source_target_pairs={{4,0},{5,1},{6,2},{7,3},{8,4},{9,5},{10,6},{11,7},{12,8},{13,9},{1... | collective-permute-start | bytes 786440 | tf_op jit(solution)/shard_map/ppermute | solution.py:373
  33.8 3.8 %collective-permute-start.11 = (bf16[256,512]{1,0:T(8,128)(2,1)S(1)}, bf16[256,512]{1,0:T(8,128)(2,1)S(1)}, u32[]{:S(2)}, u32[]{:S(2)}) collective-permute-start(bf16[256,512]{1,0:T(8,128)(2,1)S(1)} %pack_1.1), channel_id=1, source_target_pairs={{0,1},{1,0},{2,3},{3,2},{4,5},{5,4},{6,7},{7,6},{8,9},{9,8},{10,11... | collective-permute-start | bytes 786440 | tf_op jit(solution)/shard_map/ppermute | solution.py:308
  33.9 7.5 %collective-permute-start.12 = (bf16[128,512]{1,0:T(8,128)(2,1)S(1)}, bf16[128,512]{1,0:T(8,128)(2,1)S(1)}, u32[]{:S(2)}, u32[]{:S(2)}) collective-permute-start(bf16[128,512]{1,0:T(8,128)(2,1)S(1)} %get-tuple-element.52), channel_id=1, source_target_pairs={{0,2},{1,3},{2,0},{3,1},{4,6},{5,7},{6,4},{7,5},{8,10},{9,11},{10,... | collective-permute-start | bytes 393224 | tf_op jit(solution)/shard_map/ppermute | solution.py:308
  35.7 6.4 %collective-permute-start.13 = (bf16[128,512]{1,0:T(8,128)(2,1)S(1)}, bf16[128,512]{1,0:T(8,128)(2,1)S(1)}, u32[]{:S(2)}, u32[]{:S(2)}) collective-permute-start(bf16[128,512]{1,0:T(8,128)(2,1)S(1)} %get-tuple-element.53), channel_id=1, source_target_pairs={{0,3},{1,2},{2,1},{3,0},{4,7},{5,6},{6,5},{7,4},{8,11},{9,10},{10,... | collective-permute-start | bytes 393224 | tf_op jit(solution)/shard_map/ppermute | solution.py:308
  35.8 6.4 %collective-permute-start.14 = (bf16[256,256]{1,0:T(8,128)(2,1)S(1)}, bf16[256,256]{1,0:T(8,128)(2,1)S(1)}, u32[]{:S(2)}, u32[]{:S(2)}) collective-permute-start(bf16[256,256]{1,0:T(8,128)(2,1)S(1)} %get-tuple-element.54), channel_id=1, source_target_pairs={{0,4},{1,5},{2,6},{3,7},{4,0},{5,1},{6,2},{7,3},{8,12},{9,13},{10,... | collective-permute-start | bytes 393224 | tf_op jit(solution)/shard_map/ppermute | solution.py:308
  42.2 9.4 %collective-permute-start.15 = (bf16[128,1024]{1,0:T(8,128)(2,1)S(1)}, bf16[128,1024]{1,0:T(8,128)(2,1)S(1)}, u32[]{:S(2)}, u32[]{:S(2)}) collective-permute-start(bf16[128,1024]{1,0:T(8,128)(2,1)S(1)} %get-tuple-element.55), channel_id=1, source_target_pairs={{0,1},{1,0},{2,3},{3,2},{4,5},{5,4},{6,7},{7,6},{8,9},{9,8},{10,11... | collective-permute-start | bytes 786440 | tf_op jit(solution)/shard_map/ppermute | solution.py:308
  42.5 6.0 %collective-permute-start.19 = (bf16[256,256]{1,0:T(8,128)(2,1)S(1)}, bf16[256,256]{1,0:T(8,128)(2,1)S(1)}, u32[]{:S(2)}, u32[]{:S(2)}) collective-permute-start(bf16[256,256]{1,0:T(8,128)(2,1)S(1)} %get-tuple-element.61), channel_id=1, source_target_pairs={{0,4},{1,5},{2,6},{3,7},{4,0},{5,1},{6,2},{7,3},{8,12},{9,13},{10,... | collective-permute-start | bytes 393224 | tf_op jit(solution)/shard_map/ppermute | solution.py:308
  44.3 9.4 %collective-permute-start.16 = (bf16[128,512]{1,0:T(8,128)(2,1)S(1)}, bf16[128,512]{1,0:T(8,128)(2,1)S(1)}, u32[]{:S(2)}, u32[]{:S(2)}) collective-permute-start(bf16[128,512]{1,0:T(8,128)(2,1)S(1)} %get-tuple-element.56), channel_id=1, source_target_pairs={{0,2},{1,3},{2,0},{3,1},{4,6},{5,7},{6,4},{7,5},{8,10},{9,11},{10,... | collective-permute-start | bytes 393224 | tf_op jit(solution)/shard_map/ppermute | solution.py:308
  45.8 7.9 %collective-permute-start.17 = (bf16[128,512]{1,0:T(8,128)(2,1)S(1)}, bf16[128,512]{1,0:T(8,128)(2,1)S(1)}, u32[]{:S(2)}, u32[]{:S(2)}) collective-permute-start(bf16[128,512]{1,0:T(8,128)(2,1)S(1)} %get-tuple-element.57), channel_id=1, source_target_pairs={{0,3},{1,2},{2,1},{3,0},{4,7},{5,6},{6,5},{7,4},{8,11},{9,10},{10,... | collective-permute-start | bytes 393224 | tf_op jit(solution)/shard_map/ppermute | solution.py:308
  45.8 7.9 %collective-permute-start.18 = (bf16[128,256]{1,0:T(8,128)(2,1)S(1)}, bf16[128,256]{1,0:T(8,128)(2,1)S(1)}, u32[]{:S(2)}, u32[]{:S(2)}) collective-permute-start(bf16[128,256]{1,0:T(8,128)(2,1)S(1)} %get-tuple-element.59), channel_id=1, source_target_pairs={{0,8},{1,9},{2,10},{3,11},{4,12},{5,13},{6,14},{7,15},{8,0},{9,1},... | collective-permute-start | bytes 196616 | tf_op jit(solution)/shard_map/ppermute | solution.py:308
  48.5 7.1 %collective-permute-start.20 = (bf16[128,256]{1,0:T(8,128)(2,1)S(1)}, bf16[128,256]{1,0:T(8,128)(2,1)S(1)}, u32[]{:S(2)}, u32[]{:S(2)}) collective-permute-start(bf16[128,256]{1,0:T(8,128)(2,1)S(1)} %get-tuple-element.63), channel_id=1, source_target_pairs={{0,8},{1,9},{2,10},{3,11},{4,12},{5,13},{6,14},{7,15},{8,0},{9,1},... | collective-permute-start | bytes 196616 | tf_op jit(solution)/shard_map/ppermute | solution.py:308

commit v5 on v4

--- a/solution.py
+++ b/solution.py
@@ -176,14 +176,13 @@
         both = jnp.concatenate([grad_of(j), grad_of(j + 1) * joined[j].astype(BF16)], axis=0)
         parts = dot(table_ref[: 2 * length], both)
         windows.append(parts[:length] + parts[length:])
+    sources = [halves(dot(half, jnp.concatenate([input_of(j)] * 2, axis=0))) for j in range(QUAD)]
     sums = None
     for j in range(QUAD):
         near, far = halves(windows[j]), halves(windows[j + 1] * joined[j])
         real, imag = add(conj_product(near, filters[0]), conj_product(far, filters[1]))
         put(j, invert(back, real, imag).astype(BF16))
-        held = input_of(j)
-        source = halves(dot(half, jnp.concatenate([held, held], axis=0)))
-        terms = [conj_product(near, source), conj_product(far, source)]
+        terms = [conj_product(near, sources[j]), conj_product(far, sources[j])]
         sums = [add(*pair) for pair in zip(sums, terms)] if sums else terms
     return sums
 
@@ -348,7 +347,8 @@
     pair_type = jax.ShapeDtypeStruct((2 * rows, width), BF16)
     own, near, *far_inputs = products(input_kernel, key_branch, value_branch, [both] * 2 + [pair_type] * CHUNKS, 40, "conv_input", grads[1])
     own_input, near_input = own, near
-    far_inputs = [to_member(value, 2) for value in far_inputs]
+    far_inputs[0] = to_member(far_inputs[0], 2)
+    far_inputs[1] = to_member(gate([far_inputs[1]], far_inputs[0])[0], 2)
     spectra = pl.pallas_call(
         partial(filter_kernel, quads),
         out_shape=jax.ShapeDtypeStruct((REACH * lags, CHUNKS * width), F32),
@@ -396,7 +396,7 @@
             name=f"conv_{chunk}",
         )(pos, doc_blocks, table, spectra, halo, *grads, own_input, far_inputs[chunk], forward, *nearest)
         own, pair, *sent, kept, send = done
-        before, nearest = [kept], [pair]
+        before, nearest = [pair], [pair]
         if chunk:
             *sent, pair, send = gate([*sent, pair, send], *chunk_grads[-1][2:], chunk_terms[-1][1])
         chunk_grads.append([own, pair, *[to_member(value, 2 + k) for k, value in enumerate(sent)]])

time: 57.2 us -> 57.2 us (level)
  no operation moved by 1% of the time
where the time goes in v5:
time: 57.2 us; the launch traced here: 57 us
  starting transfers between devices  28 us (49%)
  Pallas kernels  14.4 us (25%)
  waiting for transfers between devices  13.7 us (24%)
  between operations  0.82 us (1%)
    ppermute x19, starting transfers between devices, to_member(): lax.ppermute(value, 'ctx', [(i, i ^ k) for i in range(blocks)])  25.5 us
    ppermute x19, waiting for transfers between devices, to_member(): lax.ppermute(value, 'ctx', [(i, i ^ k) for i in range(blocks)])  12 us
    pallas_call x2, Pallas kernels, shards(): pl.pallas_call(partial(conv_kernel, chunk, quads, doc_blocks.shape[0]), o...  7.38 us
    pallas_call x2, Pallas kernels, products(): pl.pallas_call(partial(kernel, pieces, offset), out_shape=types, in_specs...  3.62 us
    pallas_call x2, Pallas kernels, shards(): pl.pallas_call(partial(final_kernel, chunk, pieces, offset, 1.0 / math.sq...  2.7 us
    ppermute x2, starting transfers between devices, shards(): lax.ppermute(first_blocks[chunk], 'ctx', [(i, i - QUAD) for i in range(QU...  2.57 us
    ppermute x2, waiting for transfers between devices, shards(): lax.ppermute(first_blocks[chunk], 'ctx', [(i, i - QUAD) for i in range(QU...  1.69 us
  transfers between devices with their start and end apart: 21, of which 10 were waited for; matrix products, arithmetic and copies ran while one was open for 0% of the time, Pallas kernels for 18%

profile of v5, /device:TPU:0, one launch (start us, length us, event | category | flops | bytes accessed | tf_op | source)
XLA Modules:
  0.0 57.0 jit_solution(6998882545094829)
XLA Ops:
  0.7 2.8 %gated_grad.1 = (bf16[128,1024]{1,0:T(8,128)(2,1)}, bf16[128,1024]{1,0:T(8,128)(2,1)}, bf16[128,1024]{1,0:T(8,128)(2,1)}, bf16[128,1024]{1,0:T(8,128)(2,1)}) custom-call(s32[1]{0:T(128)} %bitcast.pos_ref, bf16[128,4096]{1,0:T(8,128)(2,1)} %left_hbm.2, bf16[128,4096]{1,0:T(8,128)(2,1)} %right_hbm.2), custom_call_target="tpu_custom_call" | custom-call | tf_op jit(solution)/shard_map/gated_grad/pallas_call | solution.py:335
  3.5 0.0 copy-start.3
  3.5 0.0 copy-start.2
  3.5 0.0 copy-start.4
  3.5 0.5 collective-permute-start.3
  4.0 2.6 %collective-permute-start.4 = (bf16[128,1024]{1,0:T(8,128)(2,1)}, bf16[128,1024]{1,0:T(8,128)(2,1)S(1)}, u32[]{:S(2)}, u32[]{:S(2)}) collective-permute-start(bf16[128,1024]{1,0:T(8,128)(2,1)} %get-tuple-element.37), channel_id=1, source_target_pairs={{0,2},{1,3},{2,0},{3,1},{4,6},{5,7},{6,4},{7,5},{8,10},{9,11},{10,... | collective-permute-start | bytes 786440 | tf_op jit(solution)/shard_map/ppermute | solution.py:307
  6.6 0.1 collective-permute-start.5
  6.7 2.8 %collective-permute-start = (bf16[256,256]{1,0:T(8,128)(2,1)}, bf16[256,256]{1,0:T(8,128)(2,1)S(1)}, u32[]{:S(2)}, u32[]{:S(2)}) collective-permute-start(bf16[256,256]{1,0:T(8,128)(2,1)} %refs_0_.1), channel_id=1, source_target_pairs={{0,8},{1,9},{2,10},{3,11},{4,12},{5,13},{6,14},{7,15},{8,0},{9,1},... | collective-permute-start | bytes 393224 | tf_op jit(solution)/shard_map/ppermute | solution.py:307
  9.5 1.6 %collective-permute-start.1 = (bf16[256,256]{1,0:T(8,128)(2,1)}, bf16[256,256]{1,0:T(8,128)(2,1)S(1)}, u32[]{:S(2)}, u32[]{:S(2)}) collective-permute-start(bf16[256,256]{1,0:T(8,128)(2,1)} %refs_0_.1), channel_id=1, source_target_pairs={{0,4},{1,5},{2,6},{3,7},{4,0},{5,1},{6,2},{7,3},{8,12},{9,13},{10,... | collective-permute-start | bytes 393224 | tf_op jit(solution)/shard_map/ppermute | solution.py:307
  11.1 0.0 collective-permute-done.3.refs_1_._
  11.1 0.8 %conv_input.1 = (bf16[128,1024]{1,0:T(8,128)(2,1)S(1)}, bf16[128,1024]{1,0:T(8,128)(2,1)S(1)}, bf16[256,512]{1,0:T(8,128)(2,1)S(1)}, bf16[256,512]{1,0:T(8,128)(2,1)S(1)}) custom-call(s32[1]{0:T(128)} %bitcast.pos_ref, bf16[128,4096]{1,0:T(8,128)(2,1)S(1)} %copy-done, bf16[128,4096]{1,0:T(8,128)(2,1)S(1)} %copy-done.1, ...), custom_call_target="tpu_custom_call" | custom-call | tf_op jit(solution)/shard_map/conv_input/pallas_call | solution.py:335
  11.9 1.6 %collective-permute-start.7 = (bf16[256,512]{1,0:T(8,128)(2,1)S(1)}, bf16[256,512]{1,0:T(8,128)(2,1)S(1)}, u32[]{:S(2)}, u32[]{:S(2)}) collective-permute-start(bf16[256,512]{1,0:T(8,128)(2,1)S(1)} %get-tuple-element.42), channel_id=1, source_target_pairs={{0,2},{1,3},{2,0},{3,1},{4,6},{5,7},{6,4},{7,5},{8,10},{9,11},{10,... | collective-permute-start | bytes 786440 | tf_op jit(solution)/shard_map/ppermute | solution.py:307
  13.5 3.2 %collective-permute-done.refs_1_ = bf16[256,256]{1,0:T(8,128)(2,1)S(1)} collective-permute-done((bf16[256,256]{1,0:T(8,128)(2,1)}, bf16[256,256]{1,0:T(8,128)(2,1)S(1)}, u32[]{:S(2)}, u32[]{:S(2)}) %collective-permute-start) | collective-permute-done | bytes 131104 | tf_op jit(solution)/shard_map/ppermute | solution.py:307
  16.6 0.2 collective-permute-done.1.refs_1_.refs_2_
  16.8 1.5 %collective-permute-start.2 = (bf16[256,256]{1,0:T(8,128)(2,1)S(1)}, bf16[256,256]{1,0:T(8,128)(2,1)S(1)}, u32[]{:S(2)}, u32[]{:S(2)}) collective-permute-start(bf16[256,256]{1,0:T(8,128)(2,1)S(1)} %gate.3), channel_id=1, source_target_pairs={{0,4},{1,5},{2,6},{3,7},{4,0},{5,1},{6,2},{7,3},{8,12},{9,13},{10,... | collective-permute-start | bytes 393224 | tf_op jit(solution)/shard_map/ppermute | solution.py:307
  18.3 0.9 %collective-permute-done.5.refs_3_ = bf16[128,1024]{1,0:T(8,128)(2,1)S(1)} collective-permute-done((bf16[128,1024]{1,0:T(8,128)(2,1)}, bf16[128,1024]{1,0:T(8,128)(2,1)S(1)}, u32[]{:S(2)}, u32[]{:S(2)}) %collective-permute-start.5) | collective-permute-done | bytes 262176 | tf_op jit(solution)/shard_map/ppermute | solution.py:307
  19.2 0.1 halo.1
  19.3 1.3 %collective-permute-start.9 = (bf16[256,512]{1,0:T(8,128)(2,1)S(1)}, bf16[256,512]{1,0:T(8,128)(2,1)S(1)}, u32[]{:S(2)}, u32[]{:S(2)}) collective-permute-start(bf16[256,512]{1,0:T(8,128)(2,1)S(1)} %get-tuple-element.44.refs_0_), channel_id=1, source_target_pairs={{4,0},{5,1},{6,2},{7,3},{8,4},{9,5},{10,6},{11,7},{12,8},{13,9},{1... | collective-permute-start | bytes 786440 | tf_op jit(solution)/shard_map/ppermute | solution.py:373
  20.6 1.2 %collective-permute-done.2.refs_3_ = bf16[256,256]{1,0:T(8,128)(2,1)S(1)} collective-permute-done((bf16[256,256]{1,0:T(8,128)(2,1)S(1)}, bf16[256,256]{1,0:T(8,128)(2,1)S(1)}, u32[]{:S(2)}, u32[]{:S(2)}) %collective-permute-start.2) | collective-permute-done | bytes 131104 | tf_op jit(solution)/shard_map/ppermute | solution.py:307
  21.8 0.5 filter_spectra.1.refs_1_.filter_ref
  22.3 0.0 copy-start.5
  22.3 2.7 %collective-permute-done.7.refs_1_.came_ref.refs_5_ = bf16[256,512]{1,0:T(8,128)(2,1)S(1)} collective-permute-done((bf16[256,512]{1,0:T(8,128)(2,1)S(1)}, bf16[256,512]{1,0:T(8,128)(2,1)S(1)}, u32[]{:S(2)}, u32[]{:S(2)}) %collective-permute-start.7) | collective-permute-done | bytes 262176 | tf_op jit(solution)/shard_map/ppermute | solution.py:307
  25.0 0.1 collective-permute-start.10
  25.1 1.8 %collective-permute-start.8 = (bf16[256,512]{1,0:T(8,128)(2,1)S(1)}, bf16[256,512]{1,0:T(8,128)(2,1)S(1)}, u32[]{:S(2)}, u32[]{:S(2)}) collective-permute-start(bf16[256,512]{1,0:T(8,128)(2,1)S(1)} %gate.4), channel_id=1, source_target_pairs={{0,2},{1,3},{2,0},{3,1},{4,6},{5,7},{6,4},{7,5},{8,10},{9,11},{10,... | collective-permute-start | bytes 786440 | tf_op jit(solution)/shard_map/ppermute | solution.py:307
  26.9 1.3 %collective-permute-start.6 = (bf16[256,512]{1,0:T(8,128)(2,1)S(1)}, bf16[256,512]{1,0:T(8,128)(2,1)S(1)}, u32[]{:S(2)}, u32[]{:S(2)}) collective-permute-start(bf16[256,512]{1,0:T(8,128)(2,1)S(1)} %get-tuple-element.39), channel_id=1, source_target_pairs={{4,0},{5,1},{6,2},{7,3},{8,4},{9,5},{10,6},{11,7},{12,8},{13,9},{1... | collective-permute-start | bytes 786440 | tf_op jit(solution)/shard_map/ppermute | solution.py:373
  28.2 1.7 %collective-permute-done.9.halo_ref = bf16[256,512]{1,0:T(8,128)(2,1)S(1)} collective-permute-done((bf16[256,512]{1,0:T(8,128)(2,1)S(1)}, bf16[256,512]{1,0:T(8,128)(2,1)S(1)}, u32[]{:S(2)}, u32[]{:S(2)}) %collective-permute-start.9) | collective-permute-done | bytes 262176 | tf_op jit(solution)/shard_map/ppermute | solution.py:373
  29.9 0.0 collective-permute-done.10.refs_6_
  29.9 3.7 %conv_0.1 = (bf16[128,512]{1,0:T(8,128)(2,1)S(1)}, bf16[128,512]{1,0:T(8,128)(2,1)S(1)}, bf16[128,512]{1,0:T(8,128)(2,1)S(1)}, bf16[128,512]{1,0:T(8,128)(2,1)S(...) custom-call(s32[1]{0:T(128)} %bitcast.pos_ref, s32[4]{0:T(128)S(1)} %copy-done.5, ...), custom_call_target="tpu_custom_call" | custom-call | tf_op jit(solution)/shard_map/conv_0/pallas_call | solution.py:383
  33.6 0.2 collective-permute-done.8.came_ref.refs_5_
  33.8 0.1 collective-permute-start.11
  33.9 1.8 %collective-permute-start.12 = (bf16[128,512]{1,0:T(8,128)(2,1)S(1)}, bf16[128,512]{1,0:T(8,128)(2,1)S(1)}, u32[]{:S(2)}, u32[]{:S(2)}) collective-permute-start(bf16[128,512]{1,0:T(8,128)(2,1)S(1)} %get-tuple-element.51), channel_id=1, source_target_pairs={{0,2},{1,3},{2,0},{3,1},{4,6},{5,7},{6,4},{7,5},{8,10},{9,11},{10,... | collective-permute-start | bytes 393224 | tf_op jit(solution)/shard_map/ppermute | solution.py:307
  35.7 0.1 collective-permute-start.13
  35.8 1.8 %collective-permute-start.14 = (bf16[256,256]{1,0:T(8,128)(2,1)S(1)}, bf16[256,256]{1,0:T(8,128)(2,1)S(1)}, u32[]{:S(2)}, u32[]{:S(2)}) collective-permute-start(bf16[256,256]{1,0:T(8,128)(2,1)S(1)} %get-tuple-element.53), channel_id=1, source_target_pairs={{0,4},{1,5},{2,6},{3,7},{4,0},{5,1},{6,2},{7,3},{8,12},{9,13},{10,... | collective-permute-start | bytes 393224 | tf_op jit(solution)/shard_map/ppermute | solution.py:307
  37.6 3.7 %conv_1.1 = (bf16[128,512]{1,0:T(8,128)(2,1)S(1)}, bf16[128,1024]{1,0:T(8,128)(2,1)S(1)}, bf16[128,512]{1,0:T(8,128)(2,1)S(1)}, bf16[128,512]{1,0:T(8,128)(2,1)S...) custom-call(s32[1]{0:T(128)} %bitcast.pos_ref, s32[4]{0:T(128)S(1)} %copy-done.5, ...), custom_call_target="tpu_custom_call" | custom-call | tf_op jit(solution)/shard_map/conv_1/pallas_call | solution.py:383
  41.3 0.0 collective-permute-done.12.refs_4_.refs_2_
  41.3 0.9 %collective-permute-done.13.refs_5_.refs_3_ = bf16[128,512]{1,0:T(8,128)(2,1)S(1)} collective-permute-done((bf16[128,512]{1,0:T(8,128)(2,1)S(1)}, bf16[128,512]{1,0:T(8,128)(2,1)S(1)}, u32[]{:S(2)}, u32[]{:S(2)}) %collective-permute-start.13) | collective-permute-done | bytes 131104 | tf_op jit(solution)/shard_map/ppermute | solution.py:307
  42.2 0.3 collective-permute-start.15
  42.5 1.8 %collective-permute-start.19 = (bf16[256,256]{1,0:T(8,128)(2,1)S(1)}, bf16[256,256]{1,0:T(8,128)(2,1)S(1)}, u32[]{:S(2)}, u32[]{:S(2)}) collective-permute-start(bf16[256,256]{1,0:T(8,128)(2,1)S(1)} %get-tuple-element.61), channel_id=1, source_target_pairs={{0,4},{1,5},{2,6},{3,7},{4,0},{5,1},{6,2},{7,3},{8,12},{9,13},{10,... | collective-permute-start | bytes 393224 | tf_op jit(solution)/shard_map/ppermute | solution.py:307
  44.3 1.5 %collective-permute-start.16 = (bf16[128,512]{1,0:T(8,128)(2,1)S(1)}, bf16[128,512]{1,0:T(8,128)(2,1)S(1)}, u32[]{:S(2)}, u32[]{:S(2)}) collective-permute-start(bf16[128,512]{1,0:T(8,128)(2,1)S(1)} %get-tuple-element.55), channel_id=1, source_target_pairs={{0,2},{1,3},{2,0},{3,1},{4,6},{5,7},{6,4},{7,5},{8,10},{9,11},{10,... | collective-permute-start | bytes 393224 | tf_op jit(solution)/shard_map/ppermute | solution.py:307
  45.8 2.7 %collective-permute-start.18 = (bf16[128,256]{1,0:T(8,128)(2,1)S(1)}, bf16[128,256]{1,0:T(8,128)(2,1)S(1)}, u32[]{:S(2)}, u32[]{:S(2)}) collective-permute-start(bf16[128,256]{1,0:T(8,128)(2,1)S(1)} %get-tuple-element.59), channel_id=1, source_target_pairs={{0,8},{1,9},{2,10},{3,11},{4,12},{5,13},{6,14},{7,15},{8,0},{9,1},... | collective-permute-start | bytes 196616 | tf_op jit(solution)/shard_map/ppermute | solution.py:307
  48.5 0.0 collective-permute-done.19.came_ref
  48.5 2.9 %collective-permute-start.20 = (bf16[128,256]{1,0:T(8,128)(2,1)S(1)}, bf16[128,256]{1,0:T(8,128)(2,1)S(1)}, u32[]{:S(2)}, u32[]{:S(2)}) collective-permute-start(bf16[128,256]{1,0:T(8,128)(2,1)S(1)} %get-tuple-element.63), channel_id=1, source_target_pairs={{0,8},{1,9},{2,10},{3,11},{4,12},{5,13},{6,14},{7,15},{8,0},{9,1},... | collective-permute-start | bytes 196616 | tf_op jit(solution)/shard_map/ppermute | solution.py:307
  51.5 1.3 %gate_products_0.1 = (bf16[128,4096]{1,0:T(8,128)(2,1)}, bf16[128,4096]{1,0:T(8,128)(2,1)}) custom-call(s32[1]{0:T(128)} %bitcast.pos_ref, bf16[128,4096]{1,0:T(8,128)(2,1)S(1)} %copy-done, bf16[128,4096]{1,0:T(8,128)(2,1)S(1)} %copy-done.1, bf16[128,512]{1,0:T(8,128)(2,1)S(1)} %get-tuple-element.64.refs_0_, ...), custom_call_target="tpu_custom_call" | custom-call | tf_op jit(solution)/shard_map/gate_products_0/pallas_call | solution.py:424
  52.7 0.9 %collective-permute-done.18.refs_5_ = bf16[128,256]{1,0:T(8,128)(2,1)S(1)} collective-permute-done((bf16[128,256]{1,0:T(8,128)(2,1)S(1)}, bf16[128,256]{1,0:T(8,128)(2,1)S(1)}, u32[]{:S(2)}, u32[]{:S(2)}) %collective-permute-start.18) | collective-permute-done | bytes 65568 | tf_op jit(solution)/shard_map/ppermute | solution.py:307
  53.6 0.0 collective-permute-done.16.refs_2_
  53.7 0.0 collective-permute-done.17.refs_3_
  53.7 1.9 %collective-permute-done.20.refs_7_ = bf16[128,256]{1,0:T(8,128)(2,1)S(1)} collective-permute-done((bf16[128,256]{1,0:T(8,128)(2,1)S(1)}, bf16[128,256]{1,0:T(8,128)(2,1)S(1)}, u32[]{:S(2)}, u32[]{:S(2)}) %collective-permute-start.20) | collective-permute-done | bytes 65568 | tf_op jit(solution)/shard_map/ppermute | solution.py:307
  55.6 1.4 %gate_products_1.1 = (bf16[128,4096]{1,0:T(8,128)(2,1)}, bf16[128,4096]{1,0:T(8,128)(2,1)}, f32[256,256]{1,0:T(8,128)}) custom-call(s32[1]{0:T(128)} %bitcast.pos_ref, bf16[128,4096]{1,0:T(8,128)(2,1)S(1)} %copy-done, bf16[128,4096]{1,0:T(8,128)(2,1)S(1)} %copy-done.1, ...), custom_call_target="tpu_custom_call", output_to_operand_aliasing={{0}: (11, {}), {1}: (12, {})} | custom-call | tf_op jit(solution)/shard_map/gate_products_1/pallas_call | solution.py:424
  (22 shorter events, 0.1 us)
Async XLA Ops:
  0.6 10.5 %copy-start.1 = (bf16[128,4096]{1,0:T(8,128)(2,1)S(1)}, bf16[128,4096]{1,0:T(8,128)(2,1)}, u32[]{:S(2)}) copy-start(bf16[128,4096]{1,0:T(8,128)(2,1)} %value_ref.3) | copy-start | bytes 3145732
  0.6 10.4 %copy-start = (bf16[128,4096]{1,0:T(8,128)(2,1)S(1)}, bf16[128,4096]{1,0:T(8,128)(2,1)}, u32[]{:S(2)}) copy-start(bf16[128,4096]{1,0:T(8,128)(2,1)} %key_ref.3) | copy-start | bytes 3145732
  3.5 15.7 %copy-start.3 = (bf16[128,1024]{1,0:T(8,128)(2,1)S(1)}, bf16[128,1024]{1,0:T(8,128)(2,1)}, u32[]{:S(2)}) copy-start(bf16[128,1024]{1,0:T(8,128)(2,1)} %get-tuple-element.35.refs_0_) | copy-start | bytes 786436
  3.5 18.3 %copy-start.2 = (bf16[1024,256]{1,0:T(8,128)(2,1)S(1)}, bf16[1024,256]{1,0:T(8,128)(2,1)}, u32[]{:S(2)}) copy-start(bf16[1024,256]{1,0:T(8,128)(2,1)} %constant.6.clone.table_ref) | copy-start | bytes 1572868
  3.5 18.3 %copy-start.4 = (bf16[256,256]{1,0:T(8,128)(2,1)S(1)}, bf16[256,256]{1,0:T(8,128)(2,1)}, u32[]{:S(2)}) copy-start(bf16[256,256]{1,0:T(8,128)(2,1)} %refs_0_.1) | copy-start | bytes 393220
  3.5 7.6 %collective-permute-start.3 = (bf16[128,1024]{1,0:T(8,128)(2,1)}, bf16[128,1024]{1,0:T(8,128)(2,1)S(1)}, u32[]{:S(2)}, u32[]{:S(2)}) collective-permute-start(bf16[128,1024]{1,0:T(8,128)(2,1)} %get-tuple-element.36), channel_id=1, source_target_pairs={{0,1},{1,0},{2,3},{3,2},{4,5},{5,4},{6,7},{7,6},{8,9},{9,8},{10,11... | collective-permute-start | bytes 786440 | tf_op jit(solution)/shard_map/ppermute | solution.py:307
  4.0 14.3 %collective-permute-start.4 = (bf16[128,1024]{1,0:T(8,128)(2,1)}, bf16[128,1024]{1,0:T(8,128)(2,1)S(1)}, u32[]{:S(2)}, u32[]{:S(2)}) collective-permute-start(bf16[128,1024]{1,0:T(8,128)(2,1)} %get-tuple-element.37), channel_id=1, source_target_pairs={{0,2},{1,3},{2,0},{3,1},{4,6},{5,7},{6,4},{7,5},{8,10},{9,11},{10,... | collective-permute-start | bytes 786440 | tf_op jit(solution)/shard_map/ppermute | solution.py:307
  6.6 12.6 %collective-permute-start.5 = (bf16[128,1024]{1,0:T(8,128)(2,1)}, bf16[128,1024]{1,0:T(8,128)(2,1)S(1)}, u32[]{:S(2)}, u32[]{:S(2)}) collective-permute-start(bf16[128,1024]{1,0:T(8,128)(2,1)} %get-tuple-element.38), channel_id=1, source_target_pairs={{0,3},{1,2},{2,1},{3,0},{4,7},{5,6},{6,5},{7,4},{8,11},{9,10},{10,... | collective-permute-start | bytes 786440 | tf_op jit(solution)/shard_map/ppermute | solution.py:307
  6.7 9.9 %collective-permute-start = (bf16[256,256]{1,0:T(8,128)(2,1)}, bf16[256,256]{1,0:T(8,128)(2,1)S(1)}, u32[]{:S(2)}, u32[]{:S(2)}) collective-permute-start(bf16[256,256]{1,0:T(8,128)(2,1)} %refs_0_.1), channel_id=1, source_target_pairs={{0,8},{1,9},{2,10},{3,11},{4,12},{5,13},{6,14},{7,15},{8,0},{9,1},... | collective-permute-start | bytes 393224 | tf_op jit(solution)/shard_map/ppermute | solution.py:307
  9.5 7.3 %collective-permute-start.1 = (bf16[256,256]{1,0:T(8,128)(2,1)}, bf16[256,256]{1,0:T(8,128)(2,1)S(1)}, u32[]{:S(2)}, u32[]{:S(2)}) collective-permute-start(bf16[256,256]{1,0:T(8,128)(2,1)} %refs_0_.1), channel_id=1, source_target_pairs={{0,4},{1,5},{2,6},{3,7},{4,0},{5,1},{6,2},{7,3},{8,12},{9,13},{10,... | collective-permute-start | bytes 393224 | tf_op jit(solution)/shard_map/ppermute | solution.py:307
  11.9 13.1 %collective-permute-start.7 = (bf16[256,512]{1,0:T(8,128)(2,1)S(1)}, bf16[256,512]{1,0:T(8,128)(2,1)S(1)}, u32[]{:S(2)}, u32[]{:S(2)}) collective-permute-start(bf16[256,512]{1,0:T(8,128)(2,1)S(1)} %get-tuple-element.42), channel_id=1, source_target_pairs={{0,2},{1,3},{2,0},{3,1},{4,6},{5,7},{6,4},{7,5},{8,10},{9,11},{10,... | collective-permute-start | bytes 786440 | tf_op jit(solution)/shard_map/ppermute | solution.py:307
  16.8 5.0 %collective-permute-start.2 = (bf16[256,256]{1,0:T(8,128)(2,1)S(1)}, bf16[256,256]{1,0:T(8,128)(2,1)S(1)}, u32[]{:S(2)}, u32[]{:S(2)}) collective-permute-start(bf16[256,256]{1,0:T(8,128)(2,1)S(1)} %gate.3), channel_id=1, source_target_pairs={{0,4},{1,5},{2,6},{3,7},{4,0},{5,1},{6,2},{7,3},{8,12},{9,13},{10,... | collective-permute-start | bytes 393224 | tf_op jit(solution)/shard_map/ppermute | solution.py:307
  19.3 10.6 %collective-permute-start.9 = (bf16[256,512]{1,0:T(8,128)(2,1)S(1)}, bf16[256,512]{1,0:T(8,128)(2,1)S(1)}, u32[]{:S(2)}, u32[]{:S(2)}) collective-permute-start(bf16[256,512]{1,0:T(8,128)(2,1)S(1)} %get-tuple-element.44.refs_0_), channel_id=1, source_target_pairs={{4,0},{5,1},{6,2},{7,3},{8,4},{9,5},{10,6},{11,7},{12,8},{13,9},{1... | collective-permute-start | bytes 786440 | tf_op jit(solution)/shard_map/ppermute | solution.py:373
  22.3 7.6 %copy-start.5 = (s32[4]{0:T(128)S(1)}, s32[4]{0:T(128)}, u32[]{:S(2)}) copy-start(s32[4]{0:T(128)} %docs_ref.3) | copy-start | bytes 52
  25.0 4.9 %collective-permute-start.10 = (bf16[256,512]{1,0:T(8,128)(2,1)S(1)}, bf16[256,512]{1,0:T(8,128)(2,1)S(1)}, u32[]{:S(2)}, u32[]{:S(2)}) collective-permute-start(bf16[256,512]{1,0:T(8,128)(2,1)S(1)} %pack_0.1), channel_id=1, source_target_pairs={{0,1},{1,0},{2,3},{3,2},{4,5},{5,4},{6,7},{7,6},{8,9},{9,8},{10,11... | collective-permute-start | bytes 786440 | tf_op jit(solution)/shard_map/ppermute | solution.py:307
  25.1 8.7 %collective-permute-start.8 = (bf16[256,512]{1,0:T(8,128)(2,1)S(1)}, bf16[256,512]{1,0:T(8,128)(2,1)S(1)}, u32[]{:S(2)}, u32[]{:S(2)}) collective-permute-start(bf16[256,512]{1,0:T(8,128)(2,1)S(1)} %gate.4), channel_id=1, source_target_pairs={{0,2},{1,3},{2,0},{3,1},{4,6},{5,7},{6,4},{7,5},{8,10},{9,11},{10,... | collective-permute-start | bytes 786440 | tf_op jit(solution)/shard_map/ppermute | solution.py:307
  26.9 10.7 %collective-permute-start.6 = (bf16[256,512]{1,0:T(8,128)(2,1)S(1)}, bf16[256,512]{1,0:T(8,128)(2,1)S(1)}, u32[]{:S(2)}, u32[]{:S(2)}) collective-permute-start(bf16[256,512]{1,0:T(8,128)(2,1)S(1)} %get-tuple-element.39), channel_id=1, source_target_pairs={{4,0},{5,1},{6,2},{7,3},{8,4},{9,5},{10,6},{11,7},{12,8},{13,9},{1... | collective-permute-start | bytes 786440 | tf_op jit(solution)/shard_map/ppermute | solution.py:373
  33.8 3.8 %collective-permute-start.11 = (bf16[256,512]{1,0:T(8,128)(2,1)S(1)}, bf16[256,512]{1,0:T(8,128)(2,1)S(1)}, u32[]{:S(2)}, u32[]{:S(2)}) collective-permute-start(bf16[256,512]{1,0:T(8,128)(2,1)S(1)} %pack_1.1), channel_id=1, source_target_pairs={{0,1},{1,0},{2,3},{3,2},{4,5},{5,4},{6,7},{7,6},{8,9},{9,8},{10,11... | collective-permute-start | bytes 786440 | tf_op jit(solution)/shard_map/ppermute | solution.py:307
  33.9 7.4 %collective-permute-start.12 = (bf16[128,512]{1,0:T(8,128)(2,1)S(1)}, bf16[128,512]{1,0:T(8,128)(2,1)S(1)}, u32[]{:S(2)}, u32[]{:S(2)}) collective-permute-start(bf16[128,512]{1,0:T(8,128)(2,1)S(1)} %get-tuple-element.51), channel_id=1, source_target_pairs={{0,2},{1,3},{2,0},{3,1},{4,6},{5,7},{6,4},{7,5},{8,10},{9,11},{10,... | collective-permute-start | bytes 393224 | tf_op jit(solution)/shard_map/ppermute | solution.py:307
  35.7 6.4 %collective-permute-start.13 = (bf16[128,512]{1,0:T(8,128)(2,1)S(1)}, bf16[128,512]{1,0:T(8,128)(2,1)S(1)}, u32[]{:S(2)}, u32[]{:S(2)}) collective-permute-start(bf16[128,512]{1,0:T(8,128)(2,1)S(1)} %get-tuple-element.52), channel_id=1, source_target_pairs={{0,3},{1,2},{2,1},{3,0},{4,7},{5,6},{6,5},{7,4},{8,11},{9,10},{10,... | collective-permute-start | bytes 393224 | tf_op jit(solution)/shard_map/ppermute | solution.py:307
  35.8 6.4 %collective-permute-start.14 = (bf16[256,256]{1,0:T(8,128)(2,1)S(1)}, bf16[256,256]{1,0:T(8,128)(2,1)S(1)}, u32[]{:S(2)}, u32[]{:S(2)}) collective-permute-start(bf16[256,256]{1,0:T(8,128)(2,1)S(1)} %get-tuple-element.53), channel_id=1, source_target_pairs={{0,4},{1,5},{2,6},{3,7},{4,0},{5,1},{6,2},{7,3},{8,12},{9,13},{10,... | collective-permute-start | bytes 393224 | tf_op jit(solution)/shard_map/ppermute | solution.py:307
  42.2 9.3 %collective-permute-start.15 = (bf16[128,1024]{1,0:T(8,128)(2,1)S(1)}, bf16[128,1024]{1,0:T(8,128)(2,1)S(1)}, u32[]{:S(2)}, u32[]{:S(2)}) collective-permute-start(bf16[128,1024]{1,0:T(8,128)(2,1)S(1)} %get-tuple-element.54), channel_id=1, source_target_pairs={{0,1},{1,0},{2,3},{3,2},{4,5},{5,4},{6,7},{7,6},{8,9},{9,8},{10,11... | collective-permute-start | bytes 786440 | tf_op jit(solution)/shard_map/ppermute | solution.py:307
  42.5 6.0 %collective-permute-start.19 = (bf16[256,256]{1,0:T(8,128)(2,1)S(1)}, bf16[256,256]{1,0:T(8,128)(2,1)S(1)}, u32[]{:S(2)}, u32[]{:S(2)}) collective-permute-start(bf16[256,256]{1,0:T(8,128)(2,1)S(1)} %get-tuple-element.61), channel_id=1, source_target_pairs={{0,4},{1,5},{2,6},{3,7},{4,0},{5,1},{6,2},{7,3},{8,12},{9,13},{10,... | collective-permute-start | bytes 393224 | tf_op jit(solution)/shard_map/ppermute | solution.py:307
  44.3 9.4 %collective-permute-start.16 = (bf16[128,512]{1,0:T(8,128)(2,1)S(1)}, bf16[128,512]{1,0:T(8,128)(2,1)S(1)}, u32[]{:S(2)}, u32[]{:S(2)}) collective-permute-start(bf16[128,512]{1,0:T(8,128)(2,1)S(1)} %get-tuple-element.55), channel_id=1, source_target_pairs={{0,2},{1,3},{2,0},{3,1},{4,6},{5,7},{6,4},{7,5},{8,10},{9,11},{10,... | collective-permute-start | bytes 393224 | tf_op jit(solution)/shard_map/ppermute | solution.py:307
  45.8 7.9 %collective-permute-start.17 = (bf16[128,512]{1,0:T(8,128)(2,1)S(1)}, bf16[128,512]{1,0:T(8,128)(2,1)S(1)}, u32[]{:S(2)}, u32[]{:S(2)}) collective-permute-start(bf16[128,512]{1,0:T(8,128)(2,1)S(1)} %get-tuple-element.56), channel_id=1, source_target_pairs={{0,3},{1,2},{2,1},{3,0},{4,7},{5,6},{6,5},{7,4},{8,11},{9,10},{10,... | collective-permute-start | bytes 393224 | tf_op jit(solution)/shard_map/ppermute | solution.py:307
  45.8 7.8 %collective-permute-start.18 = (bf16[128,256]{1,0:T(8,128)(2,1)S(1)}, bf16[128,256]{1,0:T(8,128)(2,1)S(1)}, u32[]{:S(2)}, u32[]{:S(2)}) collective-permute-start(bf16[128,256]{1,0:T(8,128)(2,1)S(1)} %get-tuple-element.59), channel_id=1, source_target_pairs={{0,8},{1,9},{2,10},{3,11},{4,12},{5,13},{6,14},{7,15},{8,0},{9,1},... | collective-permute-start | bytes 196616 | tf_op jit(solution)/shard_map/ppermute | solution.py:307
  48.5 7.1 %collective-permute-start.20 = (bf16[128,256]{1,0:T(8,128)(2,1)S(1)}, bf16[128,256]{1,0:T(8,128)(2,1)S(1)}, u32[]{:S(2)}, u32[]{:S(2)}) collective-permute-start(bf16[128,256]{1,0:T(8,128)(2,1)S(1)} %get-tuple-element.63), channel_id=1, source_target_pairs={{0,8},{1,9},{2,10},{3,11},{4,12},{5,13},{6,14},{7,15},{8,0},{9,1},... | collective-permute-start | bytes 196616 | tf_op jit(solution)/shard_map/ppermute | solution.py:307

commit v6 on v5

--- a/solution.py
+++ b/solution.py
@@ -220,8 +220,9 @@
         block = lambda ref, j, lanes=lanes: ref[j * rows : (j + 1) * rows, lanes]
         sums = convolve(joined, table_ref, filters, partial(block, grad_all), partial(block, input_all), put)
         for segment in range(REACH):
-            lags = invert(table_ref[3 * length :], *sums[segment])
-            terms_all[lanes, segment * rows : (segment + 1) * rows] = lags.T
+            spectrum = jnp.concatenate(sums[segment], axis=0).astype(BF16)
+            both = lax.dot_general(spectrum, table_ref[3 * length :], (((0,), (1,)), ((), ())), preferred_element_type=F32)
+            terms_all[lanes, segment * rows : (segment + 1) * rows] = both[:, :rows] + both[:, rows:]
     for k in range(QUAD):
         at = pl.ds(pl.multiple_of(lax.bitwise_xor(place, k) * rows, rows), rows)
         if k == 1 and chunk:

time: 57.2 us -> 57.2 us (level)
  no operation moved by 1% of the time
where the time goes in v6:
time: 57.2 us; the launch traced here: 57 us
  starting transfers between devices  28.1 us (49%)
  Pallas kernels  14.3 us (25%)
  waiting for transfers between devices  13.8 us (24%)
  between operations  0.82 us (1%)
    ppermute x19, starting transfers between devices, to_member(): lax.ppermute(value, 'ctx', [(i, i ^ k) for i in range(blocks)])  25.5 us
    ppermute x19, waiting for transfers between devices, to_member(): lax.ppermute(value, 'ctx', [(i, i ^ k) for i in range(blocks)])  12.1 us
    pallas_call x2, Pallas kernels, shards(): pl.pallas_call(partial(conv_kernel, chunk, quads, doc_blocks.shape[0]), o...  7.27 us
    pallas_call x2, Pallas kernels, products(): pl.pallas_call(partial(kernel, pieces, offset), out_shape=types, in_specs...  3.62 us
    pallas_call x2, Pallas kernels, shards(): pl.pallas_call(partial(final_kernel, chunk, pieces, offset, 1.0 / math.sq...  2.7 us
    ppermute x2, starting transfers between devices, shards(): lax.ppermute(first_blocks[chunk], 'ctx', [(i, i - QUAD) for i in range(QU...  2.57 us
    ppermute x2, waiting for transfers between devices, shards(): lax.ppermute(first_blocks[chunk], 'ctx', [(i, i - QUAD) for i in range(QU...  1.69 us
  transfers between devices with their start and end apart: 21, of which 10 were waited for; matrix products, arithmetic and copies ran while one was open for 0% of the time, Pallas kernels for 18%

profile of v6, /device:TPU:0, one launch (start us, length us, event | category | flops | bytes accessed | tf_op | source)
XLA Modules:
  0.0 57.0 jit_solution(12381457269344058649)
XLA Ops:
  0.7 2.8 %gated_grad.1 = (bf16[128,1024]{1,0:T(8,128)(2,1)}, bf16[128,1024]{1,0:T(8,128)(2,1)}, bf16[128,1024]{1,0:T(8,128)(2,1)}, bf16[128,1024]{1,0:T(8,128)(2,1)}) custom-call(s32[1]{0:T(128)} %bitcast.pos_ref, bf16[128,4096]{1,0:T(8,128)(2,1)} %left_hbm.2, bf16[128,4096]{1,0:T(8,128)(2,1)} %right_hbm.2), custom_call_target="tpu_custom_call" | custom-call | tf_op jit(solution)/shard_map/gated_grad/pallas_call | solution.py:336
  3.5 0.0 copy-start.3
  3.5 0.0 copy-start.2
  3.5 0.0 copy-start.4
  3.5 0.5 collective-permute-start.3
  4.0 2.6 %collective-permute-start.4 = (bf16[128,1024]{1,0:T(8,128)(2,1)}, bf16[128,1024]{1,0:T(8,128)(2,1)S(1)}, u32[]{:S(2)}, u32[]{:S(2)}) collective-permute-start(bf16[128,1024]{1,0:T(8,128)(2,1)} %get-tuple-element.37), channel_id=1, source_target_pairs={{0,2},{1,3},{2,0},{3,1},{4,6},{5,7},{6,4},{7,5},{8,10},{9,11},{10,... | collective-permute-start | bytes 786440 | tf_op jit(solution)/shard_map/ppermute | solution.py:308
  6.6 0.1 collective-permute-start.5
  6.7 2.8 %collective-permute-start = (bf16[256,256]{1,0:T(8,128)(2,1)}, bf16[256,256]{1,0:T(8,128)(2,1)S(1)}, u32[]{:S(2)}, u32[]{:S(2)}) collective-permute-start(bf16[256,256]{1,0:T(8,128)(2,1)} %refs_0_.1), channel_id=1, source_target_pairs={{0,8},{1,9},{2,10},{3,11},{4,12},{5,13},{6,14},{7,15},{8,0},{9,1},... | collective-permute-start | bytes 393224 | tf_op jit(solution)/shard_map/ppermute | solution.py:308
  9.5 1.6 %collective-permute-start.1 = (bf16[256,256]{1,0:T(8,128)(2,1)}, bf16[256,256]{1,0:T(8,128)(2,1)S(1)}, u32[]{:S(2)}, u32[]{:S(2)}) collective-permute-start(bf16[256,256]{1,0:T(8,128)(2,1)} %refs_0_.1), channel_id=1, source_target_pairs={{0,4},{1,5},{2,6},{3,7},{4,0},{5,1},{6,2},{7,3},{8,12},{9,13},{10,... | collective-permute-start | bytes 393224 | tf_op jit(solution)/shard_map/ppermute | solution.py:308
  11.1 0.8 %conv_input.1 = (bf16[128,1024]{1,0:T(8,128)(2,1)S(1)}, bf16[128,1024]{1,0:T(8,128)(2,1)S(1)}, bf16[256,512]{1,0:T(8,128)(2,1)S(1)}, bf16[256,512]{1,0:T(8,128)(2,1)S(1)}) custom-call(s32[1]{0:T(128)} %bitcast.pos_ref, bf16[128,4096]{1,0:T(8,128)(2,1)S(1)} %copy-done, bf16[128,4096]{1,0:T(8,128)(2,1)S(1)} %copy-done.1, ...), custom_call_target="tpu_custom_call" | custom-call | tf_op jit(solution)/shard_map/conv_input/pallas_call | solution.py:336
  11.9 1.6 %collective-permute-start.7 = (bf16[256,512]{1,0:T(8,128)(2,1)S(1)}, bf16[256,512]{1,0:T(8,128)(2,1)S(1)}, u32[]{:S(2)}, u32[]{:S(2)}) collective-permute-start(bf16[256,512]{1,0:T(8,128)(2,1)S(1)} %get-tuple-element.42), channel_id=1, source_target_pairs={{0,2},{1,3},{2,0},{3,1},{4,6},{5,7},{6,4},{7,5},{8,10},{9,11},{10,... | collective-permute-start | bytes 786440 | tf_op jit(solution)/shard_map/ppermute | solution.py:308
  13.5 3.2 %collective-permute-done.refs_1_ = bf16[256,256]{1,0:T(8,128)(2,1)S(1)} collective-permute-done((bf16[256,256]{1,0:T(8,128)(2,1)}, bf16[256,256]{1,0:T(8,128)(2,1)S(1)}, u32[]{:S(2)}, u32[]{:S(2)}) %collective-permute-start) | collective-permute-done | bytes 131104 | tf_op jit(solution)/shard_map/ppermute | solution.py:308
  16.6 0.2 collective-permute-done.1.refs_1_.refs_2_
  16.8 1.5 %collective-permute-start.2 = (bf16[256,256]{1,0:T(8,128)(2,1)S(1)}, bf16[256,256]{1,0:T(8,128)(2,1)S(1)}, u32[]{:S(2)}, u32[]{:S(2)}) collective-permute-start(bf16[256,256]{1,0:T(8,128)(2,1)S(1)} %gate.3), channel_id=1, source_target_pairs={{0,4},{1,5},{2,6},{3,7},{4,0},{5,1},{6,2},{7,3},{8,12},{9,13},{10,... | collective-permute-start | bytes 393224 | tf_op jit(solution)/shard_map/ppermute | solution.py:308
  18.3 0.0 collective-permute-done.4.refs_2_
  18.3 0.9 %collective-permute-done.5.refs_3_ = bf16[128,1024]{1,0:T(8,128)(2,1)S(1)} collective-permute-done((bf16[128,1024]{1,0:T(8,128)(2,1)}, bf16[128,1024]{1,0:T(8,128)(2,1)S(1)}, u32[]{:S(2)}, u32[]{:S(2)}) %collective-permute-start.5) | collective-permute-done | bytes 262176 | tf_op jit(solution)/shard_map/ppermute | solution.py:308
  19.2 0.1 halo.1
  19.3 1.3 %collective-permute-start.9 = (bf16[256,512]{1,0:T(8,128)(2,1)S(1)}, bf16[256,512]{1,0:T(8,128)(2,1)S(1)}, u32[]{:S(2)}, u32[]{:S(2)}) collective-permute-start(bf16[256,512]{1,0:T(8,128)(2,1)S(1)} %get-tuple-element.44.refs_0_), channel_id=1, source_target_pairs={{4,0},{5,1},{6,2},{7,3},{8,4},{9,5},{10,6},{11,7},{12,8},{13,9},{1... | collective-permute-start | bytes 786440 | tf_op jit(solution)/shard_map/ppermute | solution.py:374
  20.6 1.2 %collective-permute-done.2.refs_3_ = bf16[256,256]{1,0:T(8,128)(2,1)S(1)} collective-permute-done((bf16[256,256]{1,0:T(8,128)(2,1)S(1)}, bf16[256,256]{1,0:T(8,128)(2,1)S(1)}, u32[]{:S(2)}, u32[]{:S(2)}) %collective-permute-start.2) | collective-permute-done | bytes 131104 | tf_op jit(solution)/shard_map/ppermute | solution.py:308
  21.8 0.5 filter_spectra.1.refs_1_.filter_ref
  22.3 0.0 copy-start.5
  22.3 2.7 %collective-permute-done.7.refs_1_.came_ref.refs_5_ = bf16[256,512]{1,0:T(8,128)(2,1)S(1)} collective-permute-done((bf16[256,512]{1,0:T(8,128)(2,1)S(1)}, bf16[256,512]{1,0:T(8,128)(2,1)S(1)}, u32[]{:S(2)}, u32[]{:S(2)}) %collective-permute-start.7) | collective-permute-done | bytes 262176 | tf_op jit(solution)/shard_map/ppermute | solution.py:308
  25.0 0.1 collective-permute-start.10
  25.1 1.8 %collective-permute-start.8 = (bf16[256,512]{1,0:T(8,128)(2,1)S(1)}, bf16[256,512]{1,0:T(8,128)(2,1)S(1)}, u32[]{:S(2)}, u32[]{:S(2)}) collective-permute-start(bf16[256,512]{1,0:T(8,128)(2,1)S(1)} %gate.4), channel_id=1, source_target_pairs={{0,2},{1,3},{2,0},{3,1},{4,6},{5,7},{6,4},{7,5},{8,10},{9,11},{10,... | collective-permute-start | bytes 786440 | tf_op jit(solution)/shard_map/ppermute | solution.py:308
  26.9 1.3 %collective-permute-start.6 = (bf16[256,512]{1,0:T(8,128)(2,1)S(1)}, bf16[256,512]{1,0:T(8,128)(2,1)S(1)}, u32[]{:S(2)}, u32[]{:S(2)}) collective-permute-start(bf16[256,512]{1,0:T(8,128)(2,1)S(1)} %get-tuple-element.39), channel_id=1, source_target_pairs={{4,0},{5,1},{6,2},{7,3},{8,4},{9,5},{10,6},{11,7},{12,8},{13,9},{1... | collective-permute-start | bytes 786440 | tf_op jit(solution)/shard_map/ppermute | solution.py:374
  28.2 1.7 %collective-permute-done.9.halo_ref = bf16[256,512]{1,0:T(8,128)(2,1)S(1)} collective-permute-done((bf16[256,512]{1,0:T(8,128)(2,1)S(1)}, bf16[256,512]{1,0:T(8,128)(2,1)S(1)}, u32[]{:S(2)}, u32[]{:S(2)}) %collective-permute-start.9) | collective-permute-done | bytes 262176 | tf_op jit(solution)/shard_map/ppermute | solution.py:374
  29.9 3.6 %conv_0.1 = (bf16[128,512]{1,0:T(8,128)(2,1)S(1)}, bf16[128,512]{1,0:T(8,128)(2,1)S(1)}, bf16[128,512]{1,0:T(8,128)(2,1)S(1)}, bf16[128,512]{1,0:T(8,128)(2,1)S(...) custom-call(s32[1]{0:T(128)} %bitcast.pos_ref, s32[4]{0:T(128)S(1)} %copy-done.5, ...), custom_call_target="tpu_custom_call" | custom-call | tf_op jit(solution)/shard_map/conv_0/pallas_call | solution.py:384
  33.5 0.3 collective-permute-done.8.came_ref.refs_5_
  33.8 0.1 collective-permute-start.11
  33.9 1.8 %collective-permute-start.12 = (bf16[128,512]{1,0:T(8,128)(2,1)S(1)}, bf16[128,512]{1,0:T(8,128)(2,1)S(1)}, u32[]{:S(2)}, u32[]{:S(2)}) collective-permute-start(bf16[128,512]{1,0:T(8,128)(2,1)S(1)} %get-tuple-element.51), channel_id=1, source_target_pairs={{0,2},{1,3},{2,0},{3,1},{4,6},{5,7},{6,4},{7,5},{8,10},{9,11},{10,... | collective-permute-start | bytes 393224 | tf_op jit(solution)/shard_map/ppermute | solution.py:308
  35.7 0.1 collective-permute-start.13
  35.8 1.8 %collective-permute-start.14 = (bf16[256,256]{1,0:T(8,128)(2,1)S(1)}, bf16[256,256]{1,0:T(8,128)(2,1)S(1)}, u32[]{:S(2)}, u32[]{:S(2)}) collective-permute-start(bf16[256,256]{1,0:T(8,128)(2,1)S(1)} %get-tuple-element.53), channel_id=1, source_target_pairs={{0,4},{1,5},{2,6},{3,7},{4,0},{5,1},{6,2},{7,3},{8,12},{9,13},{10,... | collective-permute-start | bytes 393224 | tf_op jit(solution)/shard_map/ppermute | solution.py:308
  37.6 0.0 collective-permute-done.6.halo_ref
  37.6 0.0 collective-permute-done.11.refs_6_
  37.6 3.6 %conv_1.1 = (bf16[128,512]{1,0:T(8,128)(2,1)S(1)}, bf16[128,1024]{1,0:T(8,128)(2,1)S(1)}, bf16[128,512]{1,0:T(8,128)(2,1)S(1)}, bf16[128,512]{1,0:T(8,128)(2,1)S...) custom-call(s32[1]{0:T(128)} %bitcast.pos_ref, s32[4]{0:T(128)S(1)} %copy-done.5, ...), custom_call_target="tpu_custom_call" | custom-call | tf_op jit(solution)/shard_map/conv_1/pallas_call | solution.py:384
  41.2 0.9 %collective-permute-done.13.refs_5_.refs_3_ = bf16[128,512]{1,0:T(8,128)(2,1)S(1)} collective-permute-done((bf16[128,512]{1,0:T(8,128)(2,1)S(1)}, bf16[128,512]{1,0:T(8,128)(2,1)S(1)}, u32[]{:S(2)}, u32[]{:S(2)}) %collective-permute-start.13) | collective-permute-done | bytes 131104 | tf_op jit(solution)/shard_map/ppermute | solution.py:308
  42.2 0.0 collective-permute-done.14.refs_6_.came_ref
  42.2 0.3 collective-permute-start.15
  42.5 1.8 %collective-permute-start.19 = (bf16[256,256]{1,0:T(8,128)(2,1)S(1)}, bf16[256,256]{1,0:T(8,128)(2,1)S(1)}, u32[]{:S(2)}, u32[]{:S(2)}) collective-permute-start(bf16[256,256]{1,0:T(8,128)(2,1)S(1)} %get-tuple-element.61), channel_id=1, source_target_pairs={{0,4},{1,5},{2,6},{3,7},{4,0},{5,1},{6,2},{7,3},{8,12},{9,13},{10,... | collective-permute-start | bytes 393224 | tf_op jit(solution)/shard_map/ppermute | solution.py:308
  44.3 1.5 %collective-permute-start.16 = (bf16[128,512]{1,0:T(8,128)(2,1)S(1)}, bf16[128,512]{1,0:T(8,128)(2,1)S(1)}, u32[]{:S(2)}, u32[]{:S(2)}) collective-permute-start(bf16[128,512]{1,0:T(8,128)(2,1)S(1)} %get-tuple-element.55), channel_id=1, source_target_pairs={{0,2},{1,3},{2,0},{3,1},{4,6},{5,7},{6,4},{7,5},{8,10},{9,11},{10,... | collective-permute-start | bytes 393224 | tf_op jit(solution)/shard_map/ppermute | solution.py:308
  45.8 2.7 %collective-permute-start.18 = (bf16[128,256]{1,0:T(8,128)(2,1)S(1)}, bf16[128,256]{1,0:T(8,128)(2,1)S(1)}, u32[]{:S(2)}, u32[]{:S(2)}) collective-permute-start(bf16[128,256]{1,0:T(8,128)(2,1)S(1)} %get-tuple-element.59), channel_id=1, source_target_pairs={{0,8},{1,9},{2,10},{3,11},{4,12},{5,13},{6,14},{7,15},{8,0},{9,1},... | collective-permute-start | bytes 196616 | tf_op jit(solution)/shard_map/ppermute | solution.py:308
  48.5 0.0 collective-permute-done.19.came_ref
  48.5 3.0 %collective-permute-start.20 = (bf16[128,256]{1,0:T(8,128)(2,1)S(1)}, bf16[128,256]{1,0:T(8,128)(2,1)S(1)}, u32[]{:S(2)}, u32[]{:S(2)}) collective-permute-start(bf16[128,256]{1,0:T(8,128)(2,1)S(1)} %get-tuple-element.63), channel_id=1, source_target_pairs={{0,8},{1,9},{2,10},{3,11},{4,12},{5,13},{6,14},{7,15},{8,0},{9,1},... | collective-permute-start | bytes 196616 | tf_op jit(solution)/shard_map/ppermute | solution.py:308
  51.5 0.0 collective-permute-done.15.refs_1_
  51.5 1.3 %gate_products_0.1 = (bf16[128,4096]{1,0:T(8,128)(2,1)}, bf16[128,4096]{1,0:T(8,128)(2,1)}) custom-call(s32[1]{0:T(128)} %bitcast.pos_ref, bf16[128,4096]{1,0:T(8,128)(2,1)S(1)} %copy-done, bf16[128,4096]{1,0:T(8,128)(2,1)S(1)} %copy-done.1, bf16[128,512]{1,0:T(8,128)(2,1)S(1)} %get-tuple-element.64.refs_0_, ...), custom_call_target="tpu_custom_call" | custom-call | tf_op jit(solution)/shard_map/gate_products_0/pallas_call | solution.py:425
  52.7 0.9 %collective-permute-done.18.refs_5_ = bf16[128,256]{1,0:T(8,128)(2,1)S(1)} collective-permute-done((bf16[128,256]{1,0:T(8,128)(2,1)S(1)}, bf16[128,256]{1,0:T(8,128)(2,1)S(1)}, u32[]{:S(2)}, u32[]{:S(2)}) %collective-permute-start.18) | collective-permute-done | bytes 65568 | tf_op jit(solution)/shard_map/ppermute | solution.py:308
  53.6 1.9 %collective-permute-done.20.refs_7_ = bf16[128,256]{1,0:T(8,128)(2,1)S(1)} collective-permute-done((bf16[128,256]{1,0:T(8,128)(2,1)S(1)}, bf16[128,256]{1,0:T(8,128)(2,1)S(1)}, u32[]{:S(2)}, u32[]{:S(2)}) %collective-permute-start.20) | collective-permute-done | bytes 65568 | tf_op jit(solution)/shard_map/ppermute | solution.py:308
  55.6 1.4 %gate_products_1.1 = (bf16[128,4096]{1,0:T(8,128)(2,1)}, bf16[128,4096]{1,0:T(8,128)(2,1)}, f32[256,256]{1,0:T(8,128)}) custom-call(s32[1]{0:T(128)} %bitcast.pos_ref, bf16[128,4096]{1,0:T(8,128)(2,1)S(1)} %copy-done, bf16[128,4096]{1,0:T(8,128)(2,1)S(1)} %copy-done.1, ...), custom_call_target="tpu_custom_call", output_to_operand_aliasing={{0}: (11, {}), {1}: (12, {})} | custom-call | tf_op jit(solution)/shard_map/gate_products_1/pallas_call | solution.py:425
  (22 shorter events, 0.1 us)
Async XLA Ops:
  0.6 10.5 %copy-start.1 = (bf16[128,4096]{1,0:T(8,128)(2,1)S(1)}, bf16[128,4096]{1,0:T(8,128)(2,1)}, u32[]{:S(2)}) copy-start(bf16[128,4096]{1,0:T(8,128)(2,1)} %value_ref.3) | copy-start | bytes 3145732
  0.6 10.4 %copy-start = (bf16[128,4096]{1,0:T(8,128)(2,1)S(1)}, bf16[128,4096]{1,0:T(8,128)(2,1)}, u32[]{:S(2)}) copy-start(bf16[128,4096]{1,0:T(8,128)(2,1)} %key_ref.3) | copy-start | bytes 3145732
  3.5 15.7 %copy-start.3 = (bf16[128,1024]{1,0:T(8,128)(2,1)S(1)}, bf16[128,1024]{1,0:T(8,128)(2,1)}, u32[]{:S(2)}) copy-start(bf16[128,1024]{1,0:T(8,128)(2,1)} %get-tuple-element.35.refs_0_) | copy-start | bytes 786436
  3.5 18.3 %copy-start.2 = (bf16[1024,256]{1,0:T(8,128)(2,1)S(1)}, bf16[1024,256]{1,0:T(8,128)(2,1)}, u32[]{:S(2)}) copy-start(bf16[1024,256]{1,0:T(8,128)(2,1)} %constant.6.clone.table_ref) | copy-start | bytes 1572868
  3.5 18.3 %copy-start.4 = (bf16[256,256]{1,0:T(8,128)(2,1)S(1)}, bf16[256,256]{1,0:T(8,128)(2,1)}, u32[]{:S(2)}) copy-start(bf16[256,256]{1,0:T(8,128)(2,1)} %refs_0_.1) | copy-start | bytes 393220
  3.5 7.6 %collective-permute-start.3 = (bf16[128,1024]{1,0:T(8,128)(2,1)}, bf16[128,1024]{1,0:T(8,128)(2,1)S(1)}, u32[]{:S(2)}, u32[]{:S(2)}) collective-permute-start(bf16[128,1024]{1,0:T(8,128)(2,1)} %get-tuple-element.36), channel_id=1, source_target_pairs={{0,1},{1,0},{2,3},{3,2},{4,5},{5,4},{6,7},{7,6},{8,9},{9,8},{10,11... | collective-permute-start | bytes 786440 | tf_op jit(solution)/shard_map/ppermute | solution.py:308
  4.0 14.3 %collective-permute-start.4 = (bf16[128,1024]{1,0:T(8,128)(2,1)}, bf16[128,1024]{1,0:T(8,128)(2,1)S(1)}, u32[]{:S(2)}, u32[]{:S(2)}) collective-permute-start(bf16[128,1024]{1,0:T(8,128)(2,1)} %get-tuple-element.37), channel_id=1, source_target_pairs={{0,2},{1,3},{2,0},{3,1},{4,6},{5,7},{6,4},{7,5},{8,10},{9,11},{10,... | collective-permute-start | bytes 786440 | tf_op jit(solution)/shard_map/ppermute | solution.py:308
  6.6 12.6 %collective-permute-start.5 = (bf16[128,1024]{1,0:T(8,128)(2,1)}, bf16[128,1024]{1,0:T(8,128)(2,1)S(1)}, u32[]{:S(2)}, u32[]{:S(2)}) collective-permute-start(bf16[128,1024]{1,0:T(8,128)(2,1)} %get-tuple-element.38), channel_id=1, source_target_pairs={{0,3},{1,2},{2,1},{3,0},{4,7},{5,6},{6,5},{7,4},{8,11},{9,10},{10,... | collective-permute-start | bytes 786440 | tf_op jit(solution)/shard_map/ppermute | solution.py:308
  6.7 9.9 %collective-permute-start = (bf16[256,256]{1,0:T(8,128)(2,1)}, bf16[256,256]{1,0:T(8,128)(2,1)S(1)}, u32[]{:S(2)}, u32[]{:S(2)}) collective-permute-start(bf16[256,256]{1,0:T(8,128)(2,1)} %refs_0_.1), channel_id=1, source_target_pairs={{0,8},{1,9},{2,10},{3,11},{4,12},{5,13},{6,14},{7,15},{8,0},{9,1},... | collective-permute-start | bytes 393224 | tf_op jit(solution)/shard_map/ppermute | solution.py:308
  9.5 7.3 %collective-permute-start.1 = (bf16[256,256]{1,0:T(8,128)(2,1)}, bf16[256,256]{1,0:T(8,128)(2,1)S(1)}, u32[]{:S(2)}, u32[]{:S(2)}) collective-permute-start(bf16[256,256]{1,0:T(8,128)(2,1)} %refs_0_.1), channel_id=1, source_target_pairs={{0,4},{1,5},{2,6},{3,7},{4,0},{5,1},{6,2},{7,3},{8,12},{9,13},{10,... | collective-permute-start | bytes 393224 | tf_op jit(solution)/shard_map/ppermute | solution.py:308
  11.9 13.1 %collective-permute-start.7 = (bf16[256,512]{1,0:T(8,128)(2,1)S(1)}, bf16[256,512]{1,0:T(8,128)(2,1)S(1)}, u32[]{:S(2)}, u32[]{:S(2)}) collective-permute-start(bf16[256,512]{1,0:T(8,128)(2,1)S(1)} %get-tuple-element.42), channel_id=1, source_target_pairs={{0,2},{1,3},{2,0},{3,1},{4,6},{5,7},{6,4},{7,5},{8,10},{9,11},{10,... | collective-permute-start | bytes 786440 | tf_op jit(solution)/shard_map/ppermute | solution.py:308
  16.8 5.0 %collective-permute-start.2 = (bf16[256,256]{1,0:T(8,128)(2,1)S(1)}, bf16[256,256]{1,0:T(8,128)(2,1)S(1)}, u32[]{:S(2)}, u32[]{:S(2)}) collective-permute-start(bf16[256,256]{1,0:T(8,128)(2,1)S(1)} %gate.3), channel_id=1, source_target_pairs={{0,4},{1,5},{2,6},{3,7},{4,0},{5,1},{6,2},{7,3},{8,12},{9,13},{10,... | collective-permute-start | bytes 393224 | tf_op jit(solution)/shard_map/ppermute | solution.py:308
  19.3 10.6 %collective-permute-start.9 = (bf16[256,512]{1,0:T(8,128)(2,1)S(1)}, bf16[256,512]{1,0:T(8,128)(2,1)S(1)}, u32[]{:S(2)}, u32[]{:S(2)}) collective-permute-start(bf16[256,512]{1,0:T(8,128)(2,1)S(1)} %get-tuple-element.44.refs_0_), channel_id=1, source_target_pairs={{4,0},{5,1},{6,2},{7,3},{8,4},{9,5},{10,6},{11,7},{12,8},{13,9},{1... | collective-permute-start | bytes 786440 | tf_op jit(solution)/shard_map/ppermute | solution.py:374
  22.3 7.6 %copy-start.5 = (s32[4]{0:T(128)S(1)}, s32[4]{0:T(128)}, u32[]{:S(2)}) copy-start(s32[4]{0:T(128)} %docs_ref.3) | copy-start | bytes 52
  25.0 4.9 %collective-permute-start.10 = (bf16[256,512]{1,0:T(8,128)(2,1)S(1)}, bf16[256,512]{1,0:T(8,128)(2,1)S(1)}, u32[]{:S(2)}, u32[]{:S(2)}) collective-permute-start(bf16[256,512]{1,0:T(8,128)(2,1)S(1)} %pack_0.1), channel_id=1, source_target_pairs={{0,1},{1,0},{2,3},{3,2},{4,5},{5,4},{6,7},{7,6},{8,9},{9,8},{10,11... | collective-permute-start | bytes 786440 | tf_op jit(solution)/shard_map/ppermute | solution.py:308
  25.1 8.7 %collective-permute-start.8 = (bf16[256,512]{1,0:T(8,128)(2,1)S(1)}, bf16[256,512]{1,0:T(8,128)(2,1)S(1)}, u32[]{:S(2)}, u32[]{:S(2)}) collective-permute-start(bf16[256,512]{1,0:T(8,128)(2,1)S(1)} %gate.4), channel_id=1, source_target_pairs={{0,2},{1,3},{2,0},{3,1},{4,6},{5,7},{6,4},{7,5},{8,10},{9,11},{10,... | collective-permute-start | bytes 786440 | tf_op jit(solution)/shard_map/ppermute | solution.py:308
  26.9 10.7 %collective-permute-start.6 = (bf16[256,512]{1,0:T(8,128)(2,1)S(1)}, bf16[256,512]{1,0:T(8,128)(2,1)S(1)}, u32[]{:S(2)}, u32[]{:S(2)}) collective-permute-start(bf16[256,512]{1,0:T(8,128)(2,1)S(1)} %get-tuple-element.39), channel_id=1, source_target_pairs={{4,0},{5,1},{6,2},{7,3},{8,4},{9,5},{10,6},{11,7},{12,8},{13,9},{1... | collective-permute-start | bytes 786440 | tf_op jit(solution)/shard_map/ppermute | solution.py:374
  33.8 3.8 %collective-permute-start.11 = (bf16[256,512]{1,0:T(8,128)(2,1)S(1)}, bf16[256,512]{1,0:T(8,128)(2,1)S(1)}, u32[]{:S(2)}, u32[]{:S(2)}) collective-permute-start(bf16[256,512]{1,0:T(8,128)(2,1)S(1)} %pack_1.1), channel_id=1, source_target_pairs={{0,1},{1,0},{2,3},{3,2},{4,5},{5,4},{6,7},{7,6},{8,9},{9,8},{10,11... | collective-permute-start | bytes 786440 | tf_op jit(solution)/shard_map/ppermute | solution.py:308
  33.9 7.3 %collective-permute-start.12 = (bf16[128,512]{1,0:T(8,128)(2,1)S(1)}, bf16[128,512]{1,0:T(8,128)(2,1)S(1)}, u32[]{:S(2)}, u32[]{:S(2)}) collective-permute-start(bf16[128,512]{1,0:T(8,128)(2,1)S(1)} %get-tuple-element.51), channel_id=1, source_target_pairs={{0,2},{1,3},{2,0},{3,1},{4,6},{5,7},{6,4},{7,5},{8,10},{9,11},{10,... | collective-permute-start | bytes 393224 | tf_op jit(solution)/shard_map/ppermute | solution.py:308
  35.7 6.4 %collective-permute-start.13 = (bf16[128,512]{1,0:T(8,128)(2,1)S(1)}, bf16[128,512]{1,0:T(8,128)(2,1)S(1)}, u32[]{:S(2)}, u32[]{:S(2)}) collective-permute-start(bf16[128,512]{1,0:T(8,128)(2,1)S(1)} %get-tuple-element.52), channel_id=1, source_target_pairs={{0,3},{1,2},{2,1},{3,0},{4,7},{5,6},{6,5},{7,4},{8,11},{9,10},{10,... | collective-permute-start | bytes 393224 | tf_op jit(solution)/shard_map/ppermute | solution.py:308
  35.8 6.4 %collective-permute-start.14 = (bf16[256,256]{1,0:T(8,128)(2,1)S(1)}, bf16[256,256]{1,0:T(8,128)(2,1)S(1)}, u32[]{:S(2)}, u32[]{:S(2)}) collective-permute-start(bf16[256,256]{1,0:T(8,128)(2,1)S(1)} %get-tuple-element.53), channel_id=1, source_target_pairs={{0,4},{1,5},{2,6},{3,7},{4,0},{5,1},{6,2},{7,3},{8,12},{9,13},{10,... | collective-permute-start | bytes 393224 | tf_op jit(solution)/shard_map/ppermute | solution.py:308
  42.2 9.3 %collective-permute-start.15 = (bf16[128,1024]{1,0:T(8,128)(2,1)S(1)}, bf16[128,1024]{1,0:T(8,128)(2,1)S(1)}, u32[]{:S(2)}, u32[]{:S(2)}) collective-permute-start(bf16[128,1024]{1,0:T(8,128)(2,1)S(1)} %get-tuple-element.54), channel_id=1, source_target_pairs={{0,1},{1,0},{2,3},{3,2},{4,5},{5,4},{6,7},{7,6},{8,9},{9,8},{10,11... | collective-permute-start | bytes 786440 | tf_op jit(solution)/shard_map/ppermute | solution.py:308
  42.5 6.0 %collective-permute-start.19 = (bf16[256,256]{1,0:T(8,128)(2,1)S(1)}, bf16[256,256]{1,0:T(8,128)(2,1)S(1)}, u32[]{:S(2)}, u32[]{:S(2)}) collective-permute-start(bf16[256,256]{1,0:T(8,128)(2,1)S(1)} %get-tuple-element.61), channel_id=1, source_target_pairs={{0,4},{1,5},{2,6},{3,7},{4,0},{5,1},{6,2},{7,3},{8,12},{9,13},{10,... | collective-permute-start | bytes 393224 | tf_op jit(solution)/shard_map/ppermute | solution.py:308
  44.3 9.4 %collective-permute-start.16 = (bf16[128,512]{1,0:T(8,128)(2,1)S(1)}, bf16[128,512]{1,0:T(8,128)(2,1)S(1)}, u32[]{:S(2)}, u32[]{:S(2)}) collective-permute-start(bf16[128,512]{1,0:T(8,128)(2,1)S(1)} %get-tuple-element.55), channel_id=1, source_target_pairs={{0,2},{1,3},{2,0},{3,1},{4,6},{5,7},{6,4},{7,5},{8,10},{9,11},{10,... | collective-permute-start | bytes 393224 | tf_op jit(solution)/shard_map/ppermute | solution.py:308
  45.8 7.9 %collective-permute-start.17 = (bf16[128,512]{1,0:T(8,128)(2,1)S(1)}, bf16[128,512]{1,0:T(8,128)(2,1)S(1)}, u32[]{:S(2)}, u32[]{:S(2)}) collective-permute-start(bf16[128,512]{1,0:T(8,128)(2,1)S(1)} %get-tuple-element.56), channel_id=1, source_target_pairs={{0,3},{1,2},{2,1},{3,0},{4,7},{5,6},{6,5},{7,4},{8,11},{9,10},{10,... | collective-permute-start | bytes 393224 | tf_op jit(solution)/shard_map/ppermute | solution.py:308
  45.8 7.8 %collective-permute-start.18 = (bf16[128,256]{1,0:T(8,128)(2,1)S(1)}, bf16[128,256]{1,0:T(8,128)(2,1)S(1)}, u32[]{:S(2)}, u32[]{:S(2)}) collective-permute-start(bf16[128,256]{1,0:T(8,128)(2,1)S(1)} %get-tuple-element.59), channel_id=1, source_target_pairs={{0,8},{1,9},{2,10},{3,11},{4,12},{5,13},{6,14},{7,15},{8,0},{9,1},... | collective-permute-start | bytes 196616 | tf_op jit(solution)/shard_map/ppermute | solution.py:308
  48.5 7.1 %collective-permute-start.20 = (bf16[128,256]{1,0:T(8,128)(2,1)S(1)}, bf16[128,256]{1,0:T(8,128)(2,1)S(1)}, u32[]{:S(2)}, u32[]{:S(2)}) collective-permute-start(bf16[128,256]{1,0:T(8,128)(2,1)S(1)} %get-tuple-element.63), channel_id=1, source_target_pairs={{0,8},{1,9},{2,10},{3,11},{4,12},{5,13},{6,14},{7,15},{8,0},{9,1},... | collective-permute-start | bytes 196616 | tf_op jit(solution)/shard_map/ppermute | solution.py:308
